TPU v7x, 32 devices: a whole 2x2x4 slice. The times are simulated.
32 devices in a mesh: bx: 4 (over y, x), by: 4 (over z), gz: 2 (over core).
Axes of the slice: x: 2, y: 2, z: 4, core: 2. Of those that a mesh axis runs over, the one named last changes fastest.
Arguments:
- electric_start: float32 [3, 64, 64, 256], P(None, 'by', 'bx', 'gz'), may hold values from -6 to 6
- magnetic_start: float32 [3, 64, 64, 256], P(None, 'by', 'bx', 'gz'), may hold values from -6 to 6
- current_start: float32 [3, 64, 64, 256], P(None, 'by', 'bx', 'gz'), may hold values from -6 to 6
- cotangent: float32 [3, 64, 64, 256], P(None, 'by', 'bx', 'gz'), may hold values from -6 to 6
- level_set: float32 [64, 64, 256], P('by', 'bx', 'gz'), may hold values from -8 to 8
- material: int32 [64, 64, 256], P('by', 'bx', 'gz'), may hold values from 0 to 2
- source_cell: int32 [256], P(('bx', 'by', 'gz')), may hold values from 0 to 32767
- basis: bfloat16 [8192, 64, 256], P(('bx', 'by', 'gz')), may hold values from 0 to 1
- block_owner: int32 [8192, 1], P(('bx', 'by', 'gz')), may hold values from 0 to 15; in each aligned block of 256 rows (0 to 255, 256 to 511, ...) at most 32 rows name the same one
- block_group: int32 [8192], P(('bx', 'by', 'gz')), may hold values from 0 to 127
Outputs:
- final_electric: float32 [3, 64, 64, 256], P(None, 'by', 'bx', 'gz')
- adjoint_electric: float32 [3, 64, 64, 256], P(None, 'by', 'bx', 'gz')
- coef_grad: float32 [64, 4096], P(None, ('bx', 'by', 'gz'))
Inputs may be any that keep to these rules, and one draw needn't show every extreme that they name: `material`: 0 is vacuum, 1 design dielectric, 2 silver. `source_cell`: a flat cell index within the device's own brick; a cell may be named more than once. `block_owner`: among the 256 blocks of one device no owner is named by more than 32 blocks, and in some device one owner is named by exactly 32.
All inputs are finite; a program needn't handle non-finite values.
Results may differ from a plain program's by a relative error of at most 0.0029.
Values sent between devices are 32-bit elements; how exact they have to be, the bound alone decides.
No kernel may reach another device: no remote copies, remote signals or barrier semaphores. Data moves between devices by JAX's collectives and lax.ppermute only.
A program may use at most 64 MiB of HBM per device.

v0:
```python
import jax
import jax.numpy as jnp
from jax import lax
from jax.sharding import PartitionSpec as P

NSTEP = 2
KB = 64
GRP_DEV = 128


time_step = 0.5
drude_keep = 0.9
drude_gain = 1.0
metal_permit = 3.0
design_contrast = 5.0
source_level = 3.0
source_wave = (1.0, -0.6, 0.8, -0.4)


def passed_along(x, axis, by):
    count = lax.axis_size(axis)
    pairs = [(i, i + by) for i in range(count) if 0 <= i + by < count]
    return lax.ppermute(x, axis, pairs)


def face_y(face_cells, offset):
    return passed_along(face_cells, "by", offset)


def face_x(face_cells, offset):
    return passed_along(face_cells, "bx", offset)


def face_z(face_cells, offset):
    return passed_along(face_cells, "gz", offset)


def beside(couple, axis_dim, offset):
    length = couple.shape[axis_dim]
    border_at = 0 if offset < 0 else length - 1
    face_cells = lax.index_in_dim(couple, border_at, axis=axis_dim, keepdims=False)
    if axis_dim == 1:
        arrived = face_y(face_cells, offset)
    elif axis_dim == 2:
        arrived = face_x(face_cells, offset)
    else:
        flattened = face_cells.reshape(face_cells.shape[0], -1)
        arrived = face_z(flattened, offset).reshape(face_cells.shape)
    arrived = jnp.expand_dims(arrived, axis_dim)
    if offset < 0:
        return jnp.concatenate(
            [lax.slice_in_dim(couple, 1, length, axis=axis_dim), arrived], axis=axis_dim
        )
    return jnp.concatenate(
        [arrived, lax.slice_in_dim(couple, 0, length - 1, axis=axis_dim)], axis=axis_dim
    )


def differ(couple, axis_dim, offset):
    neighbour = beside(couple, axis_dim, offset)
    if offset < 0:
        return neighbour - couple
    return couple - neighbour


def curl(fields, offset):
    along_x = differ(jnp.stack([fields[1], fields[2]]), 2, offset)
    along_y = differ(jnp.stack([fields[0], fields[2]]), 1, offset)
    along_z = differ(jnp.stack([fields[0], fields[1]]), 3, offset)
    return jnp.stack([along_y[1] - along_z[1], along_z[0] - along_x[1], along_x[0] - along_y[0]])


def local(
    electric_start,
    magnetic_start,
    current_start,
    cotangent,
    level_set,
    material,
    source_cell,
    basis,
    block_owner,
    block_group,
):
    silver = (material == 2).astype(jnp.float32)
    design = (material == 1).astype(jnp.float32)
    smooth = jax.nn.sigmoid(level_set)
    permit = jnp.where(
        material == 2, metal_permit, jnp.where(material == 1, 1.0 + design_contrast * smooth, 1.0)
    )
    sources = (
        jnp.zeros((material.size,), jnp.float32).at[source_cell].add(1.0).reshape(material.shape)
    )
    electric, magnetic, current = (electric_start, magnetic_start, current_start)
    drives = []
    for moment in range(NSTEP):
        magnetic = magnetic - time_step * curl(electric, -1)
        current = silver * (drude_keep * current + drude_gain * electric)
        drive_term = curl(magnetic, 1) - current
        electric = electric + time_step / permit * drive_term
        electric = electric.at[2].add(source_level * source_wave[moment] * sources)
        drives.append(drive_term)
    step_ratio = time_step / permit
    adj_electric = cotangent
    adj_magnetic = jnp.zeros_like(cotangent)
    adj_current = jnp.zeros_like(cotangent)
    eps_grad = jnp.zeros(material.shape, jnp.float32)
    for moment in reversed(range(NSTEP)):
        scaled = step_ratio * adj_electric
        eps_grad = eps_grad - jnp.sum(scaled * drives[moment], axis=0) / permit
        adj_drive = adj_current - scaled
        adj_magnetic = adj_magnetic + curl(scaled, -1)
        adj_electric = (
            adj_electric + drude_gain * silver * adj_drive - time_step * curl(adj_magnetic, 1)
        )
        adj_current = drude_keep * silver * adj_drive
    level_grad = eps_grad * design * design_contrast * (smooth * (1.0 - smooth))
    cell_grad = level_grad.astype(jnp.bfloat16)
    tile_width = basis.shape[2]
    tile_count = cell_grad.size // tile_width
    block_count = basis.shape[0]
    tile_fan = block_count // tile_count
    cell_tiles = cell_grad.reshape(tile_count, tile_width)
    blocks = basis.reshape(tile_count, tile_fan, KB, tile_width)
    partials = jnp.einsum(
        "tfkc,tc->tfk", blocks, cell_tiles, preferred_element_type=jnp.float32
    ).reshape(block_count, KB)
    size_bx = lax.axis_size("bx")
    planes = size_bx * lax.axis_size("by")
    capacity = max(2, 2 * block_count // planes)
    slots = planes * capacity
    owner_plane = block_owner[:, 0]
    owner_hits = (owner_plane[:, None] == jnp.arange(planes, dtype=jnp.int32)[None, :]).astype(
        jnp.float32
    )
    before = jnp.cumsum(owner_hits, axis=0) - owner_hits
    slot_rank = jnp.sum(before * owner_hits, axis=1).astype(jnp.int32)
    target = owner_plane * capacity + slot_rank
    placing = (target[:, None] == jnp.arange(slots, dtype=jnp.int32)[None, :]).astype(jnp.float32)
    send_vals = jnp.einsum("bk,bs->ks", partials, placing, precision=lax.Precision.HIGHEST)
    send_ids = (
        jnp.einsum(
            "b,bs->s",
            block_group.astype(jnp.float32) + 1.0,
            placing,
            precision=lax.Precision.HIGHEST,
        )[None, :]
        - 1.0
    )
    got_vals, got_ids = (
        lax.all_to_all(send_vals, ("bx", "by"), split_axis=1, concat_axis=1, tiled=True),
        lax.all_to_all(send_ids, ("bx", "by"), split_axis=1, concat_axis=1, tiled=True),
    )
    group_hits = (
        got_ids[0][:, None] == jnp.arange(GRP_DEV, dtype=jnp.int32)[None, :].astype(jnp.float32)
    ).astype(jnp.float32)
    coef_grad = jnp.dot(got_vals, group_hits, precision=lax.Precision.HIGHEST)
    return (electric, adj_electric, coef_grad)


def solution(mesh):
    return jax.shard_map(
        local,
        mesh=mesh,
        in_specs=(
            P(None, "by", "bx", "gz"),
            P(None, "by", "bx", "gz"),
            P(None, "by", "bx", "gz"),
            P(None, "by", "bx", "gz"),
            P("by", "bx", "gz"),
            P("by", "bx", "gz"),
            P(("bx", "by", "gz")),
            P(("bx", "by", "gz"), None, None),
            P(("bx", "by", "gz"), None),
            P(("bx", "by", "gz")),
        ),
        out_specs=(
            P(None, "by", "bx", "gz"),
            P(None, "by", "bx", "gz"),
            P(None, ("bx", "by", "gz")),
        ),
        check_vma=False,
    )
```

profile of v0, /device:TPU:0, one launch (start us, length us, event | category | flops | bytes accessed | tf_op | source)
XLA Modules:
  0.0 156.9 jit_solution(8473862122316755948)
XLA Ops:
  0.7 1.1 fusion.68
  1.8 1.3 collective-permute-start
  3.1 1.1 slice_reduce_fusion.6
  4.3 1.3 collective-permute-start.1
  5.6 0.9 slice.468
  6.5 1.3 collective-permute-start.2
  12.4 10.5 %all-to-all-start.1 = ((f32[1,16,32]{2,0,1:T(1,128)}), f32[1,16,32]{2,0,1:T(1,128)S(1)}, u32[]{:S(2)}, u32[]{:S(2)}) async-start(f32[1,16,32]{2,0,1:T(1,128)} %all_to_all.14), calls=%async_computation.1 | async-start | bytes 16384 | tf_op jit(solution)/shard_map/all_to_all | solution.py:152
  23.6 1.6 %broadcast_select_fusion = (f32[16,16,128]{2,1,0:T(8,128)}, pred[16,16,128]{2,1,0:T(8,128)(4,1)S(1)}) fusion(s32[16,16,128]{2,1,0:T(8,128)} %param.19), kind=kLoop, calls=%fused_computation.156 | loop fusion | flops 65536 | bytes 294912 | tf_op jit(solution)/shard_map/mul | solution.py:116
  27.2 1.6 %fusion.38 = (f32[16,16,128]{2,1,0:T(8,128)S(1)}, pred[16,16,128]{2,1,0:T(8,128)(4,1)}) fusion(pred[16,16,128]{2,1,0:T(8,128)(4,1)S(1)} %get-tuple-element.31, f32[16,16,128]{2,1,0:T(8,128)} %param.18, s32[16,16,128]{2,1,0:T(8,128)} %param.19), kind=kLoop, calls=%fused_computation.153 | loop fusion | flops 294912 | bytes 458752 | tf_op jit(solution)/shard_map/div | solution.py:100
  29.4 1.1 slice.463
  30.5 1.0 slice.467
  33.6 1.2 maximum_subtract_fusion.2
  36.2 1.0 fusion.3
  38.1 3.8 %collective-permute-start.3 = (f32[2,16,128]{2,1,0:T(8,128)}, f32[2,16,128]{2,1,0:T(8,128)S(1)}, u32[]{:S(2)}, u32[]{:S(2)}) collective-permute-start(f32[2,16,128]{2,1,0:T(8,128)} %fusion.56), channel_id=1, source_target_pairs={{0,2},{2,4},{4,6},{1,3},{3,5},{5,7},{8,10},{10,12},{12,14},{9,11},... | collective-permute-start | bytes 49160 | tf_op jit(solution)/shard_map/ppermute | solution.py:23
  42.0 2.5 %collective-permute-start.4 = (f32[2,256]{1,0:T(2,128)S(1)}, f32[2,256]{1,0:T(2,128)}, u32[]{:S(2)}, u32[]{:S(2)}) collective-permute-start(f32[2,256]{1,0:T(2,128)S(1)} %reshape_squeeze.25), channel_id=1, source_target_pairs={{0,1},{2,3},{4,5},{6,7},{8,9},{10,11},{12,13},{14,15},{16,17},{18,... | collective-permute-start | bytes 6152 | tf_op jit(solution)/shard_map/ppermute | solution.py:23
  45.2 3.4 %collective-permute-start.5 = (f32[2,16,128]{2,1,0:T(8,128)}, f32[2,16,128]{2,1,0:T(8,128)S(1)}, u32[]{:S(2)}, u32[]{:S(2)}) collective-permute-start(f32[2,16,128]{2,1,0:T(8,128)} %bitcast.8), channel_id=1, source_target_pairs={{0,8},{8,16},{16,24},{1,9},{9,17},{17,25},{2,10},{10,18},{18,26},{... | collective-permute-start | bytes 49160 | tf_op jit(solution)/shard_map/ppermute | solution.py:23
  48.5 0.9 broadcast_in_dim_reshape.33
  50.6 1.0 constant_dynamic-update-slice_fusion
  52.6 1.3 collective-permute-start.6
  53.9 1.3 collective-permute-start.7
  55.3 1.3 collective-permute-start.13
  61.7 1.3 collective-permute-start.8
  62.9 1.3 collective-permute-start.12
  64.3 1.3 collective-permute-start.14
  65.6 0.9 broadcast_in_dim_reshape.34
  66.5 0.9 broadcast_in_dim_reshape.36
  67.4 1.0 fusion.15
  68.4 1.3 slice_subtract_fusion.9
  69.7 1.1 fusion.4
  71.8 1.0 fusion.13
  72.8 1.3 slice_subtract_fusion.5
  75.9 5.2 %collective-permute-start.9 = (f32[2,16,128]{2,1,0:T(8,128)S(1)}, f32[2,16,128]{2,1,0:T(8,128)S(1)}, u32[]{:S(2)}, u32[]{:S(2)}) collective-permute-start(f32[2,16,128]{2,1,0:T(8,128)S(1)} %fusion.58), channel_id=1, source_target_pairs={{0,2},{2,4},{4,6},{1,3},{3,5},{5,7},{8,10},{10,12},{12,14},{9,11},... | collective-permute-start | bytes 49160 | tf_op jit(solution)/shard_map/ppermute | solution.py:23
  81.1 2.7 %collective-permute-start.10 = (f32[2,256]{1,0:T(2,128)S(1)}, f32[2,256]{1,0:T(2,128)S(1)}, u32[]{:S(2)}, u32[]{:S(2)}) collective-permute-start(f32[2,256]{1,0:T(2,128)S(1)} %reshape_squeeze.27), channel_id=1, source_target_pairs={{0,1},{2,3},{4,5},{6,7},{8,9},{10,11},{12,13},{14,15},{16,17},{18,... | collective-permute-start | bytes 6152 | tf_op jit(solution)/shard_map/ppermute | solution.py:23
  84.0 1.3 collective-permute-start.16
  86.7 5.5 %collective-permute-start.11 = (f32[2,16,128]{2,1,0:T(8,128)S(1)}, f32[2,16,128]{2,1,0:T(8,128)S(1)}, u32[]{:S(2)}, u32[]{:S(2)}) collective-permute-start(f32[2,16,128]{2,1,0:T(8,128)S(1)} %bitcast.139), channel_id=1, source_target_pairs={{0,8},{8,16},{16,24},{1,9},{9,17},{17,25},{2,10},{10,18},{18,26},{... | collective-permute-start | bytes 49160 | tf_op jit(solution)/shard_map/ppermute | solution.py:23
  92.2 4.5 %collective-permute-start.17 = (f32[2,16,128]{2,1,0:T(8,128)S(1)}, f32[2,16,128]{2,1,0:T(8,128)S(1)}, u32[]{:S(2)}, u32[]{:S(2)}) collective-permute-start(f32[2,16,128]{2,1,0:T(8,128)S(1)} %bitcast.131), channel_id=1, source_target_pairs={{0,8},{8,16},{16,24},{1,9},{9,17},{17,25},{2,10},{10,18},{18,26},{... | collective-permute-start | bytes 49160 | tf_op jit(solution)/shard_map/ppermute | solution.py:23
  96.7 3.6 %collective-permute-start.15 = (f32[2,16,128]{2,1,0:T(8,128)S(1)}, f32[2,16,128]{2,1,0:T(8,128)S(1)}, u32[]{:S(2)}, u32[]{:S(2)}) collective-permute-start(f32[2,16,128]{2,1,0:T(8,128)S(1)} %fusion.54), channel_id=1, source_target_pairs={{0,2},{2,4},{4,6},{1,3},{3,5},{5,7},{8,10},{10,12},{12,14},{9,11},... | collective-permute-start | bytes 49160 | tf_op jit(solution)/shard_map/ppermute | solution.py:23
  100.4 0.9 broadcast_in_dim_reshape.35
  101.3 0.9 broadcast_in_dim_reshape.37
  102.2 1.0 fusion.14
  103.2 1.3 slice_subtract_fusion.7
  104.5 1.2 fusion.18
  105.9 1.3 multiply_reduce_fusion.1
  107.4 1.1 fusion.35
  108.5 1.3 collective-permute-start.18
  109.9 1.3 collective-permute-start.19
  111.2 6.7 %fusion.72 = f32[128,1,2,64]{3,1,2,0:T(1,128)S(1)} fusion(bf16[128,256,1,1]{1,2,3,0:T(2,128)(2,1)S(1)} %reshape.178, bf16[128,2,64,256]{3,2,1,0:T(8,128)(2,1)} %bitcast.116), kind=kOutput, calls=%fused_computation.204 | convolution fusion | flops 8388608 | bytes 8519680 | tf_op jit(solution)/shard_map/tfkc,tc->tfk/dot_general | solution.py:125
  117.9 1.1 fusion.69
  120.0 1.8 %reshape.199 = f32[16,1,2048]{2,1,0:T(1,128)} reshape(f32[16,32,64]{2,1,0:T(8,128)} %fusion.69) | data formatting | bytes 262144
  121.8 6.7 %all-to-all-start = ((f32[16,1,2048]{2,1,0:T(1,128)}), f32[16,1,2048]{2,1,0:T(1,128)}, u32[]{:S(2)}, u32[]{:S(2)}) async-start(f32[16,1,2048]{2,1,0:T(1,128)} %reshape.199), calls=%async_computation | async-start | bytes 262144 | tf_op jit(solution)/shard_map/all_to_all | solution.py:151
  128.5 1.3 collective-permute-start.20
  129.8 0.9 broadcast_in_dim_reshape.38
  130.7 1.0 fusion.8
  131.7 2.7 %collective-permute-done.20 = f32[2,16,128]{2,1,0:T(8,128)S(1)} collective-permute-done((f32[2,16,128]{2,1,0:T(8,128)S(1)}, f32[2,16,128]{2,1,0:T(8,128)S(1)}, u32[]{:S(2)}, u32[]{:S(2)}) %collective-permute-start.20) | collective-permute-done | bytes 16416 | tf_op jit(solution)/shard_map/ppermute | solution.py:23
  134.3 1.1 slice_subtract_fusion.3
  137.1 3.5 %collective-permute-start.21 = (f32[2,16,128]{2,1,0:T(8,128)}, f32[2,16,128]{2,1,0:T(8,128)S(1)}, u32[]{:S(2)}, u32[]{:S(2)}) collective-permute-start(f32[2,16,128]{2,1,0:T(8,128)} %fusion.61), channel_id=1, source_target_pairs={{0,2},{2,4},{4,6},{1,3},{3,5},{5,7},{8,10},{10,12},{12,14},{9,11},... | collective-permute-start | bytes 49160 | tf_op jit(solution)/shard_map/ppermute | solution.py:23
  140.8 2.1 %collective-permute-start.22 = (f32[2,256]{1,0:T(2,128)S(1)}, f32[2,256]{1,0:T(2,128)}, u32[]{:S(2)}, u32[]{:S(2)}) collective-permute-start(f32[2,256]{1,0:T(2,128)S(1)} %reshape_squeeze.31), channel_id=1, source_target_pairs={{0,1},{2,3},{4,5},{6,7},{8,9},{10,11},{12,13},{14,15},{16,17},{18,... | collective-permute-start | bytes 6152 | tf_op jit(solution)/shard_map/ppermute | solution.py:23
  143.6 4.1 %collective-permute-start.23 = (f32[2,16,128]{2,1,0:T(8,128)}, f32[2,16,128]{2,1,0:T(8,128)S(1)}, u32[]{:S(2)}, u32[]{:S(2)}) collective-permute-start(f32[2,16,128]{2,1,0:T(8,128)} %bitcast.40), channel_id=1, source_target_pairs={{0,8},{8,16},{16,24},{1,9},{9,17},{17,25},{2,10},{10,18},{18,26},{... | collective-permute-start | bytes 49160 | tf_op jit(solution)/shard_map/ppermute | solution.py:23
  147.7 0.9 broadcast_in_dim_reshape.39
  148.6 1.0 fusion.7
  149.8 1.9 %fusion.6 = (f32[3,16,16,128]{3,2,1,0:T(8,128)}, f32[3,16,16,128]{3,2,1,0:T(8,128)S(1)}) fusion(f32[1,16,16,128]{3,2,1,0:T(8,128)S(1)} %get-tuple-element.64, f32[1,16,16,128]{3,2,1,0:T(8,128)S(1)} %get-tuple-element.65, f32[1,16,16,128]{3,2,1,0:T(8,128)S(1)} %get-tuple-element.63, f32[16,16,128]{2,1,0:T(8,128)} %get-tuple-element.30, ...), kind=kLoop, calls=%fused_computation.26 | loop fusion | flops 1867776 | bytes 3145728 | tf_op jit(solution)/shard_map/sub | solution.py:114
  151.7 0.9 fusion.36
  153.2 1.9 %reduce.26 = f32[16,2048]{1,0:T(8,128)S(1)} reduce(f32[16,1,2048]{2,1,0:T(1,128)} %all-to-all-done, f32[]{:T(128)} %broadcast.191), dimensions={1}, to_apply=%all_to_all.12.reduce_sub_computation | reduce | bytes 262148 | tf_op jit(solution)/shard_map/all_to_all | solution.py:151
  155.2 1.8 %fusion.24 = f32[64,128]{1,0:T(8,128)} fusion(f32[64,512]{0,1:T(8,128)S(1)} %bitcast.117, f32[128]{0:T(128)} %iota_convert_fusion, f32[512]{0:T(512)} %eq.107), kind=kOutput, calls=%fused_computation.109 | convolution fusion | flops 50397184 | bytes 166400 | tf_op jit(solution)/shard_map/dot_general | solution.py:157
  (156 shorter events, 29.3 us)
Async XLA Ops:
  0.6 49.8 %copy-start = (f32[3,16,16,128]{3,2,1,0:T(8,128)S(1)}, f32[3,16,16,128]{3,2,1,0:T(8,128)}, u32[]{:S(2)}) copy-start(f32[3,16,16,128]{3,2,1,0:T(8,128)} %param.14) | copy-start | bytes 1179652
  0.6 35.5 %copy-start.2 = (f32[3,16,16,128]{3,2,1,0:T(8,128)S(1)}, f32[3,16,16,128]{3,2,1,0:T(8,128)}, u32[]{:S(2)}) copy-start(f32[3,16,16,128]{3,2,1,0:T(8,128)} %param.15) | copy-start | bytes 1179652
  0.7 49.7 %copy-start.3 = (f32[3,16,16,128]{3,2,1,0:T(8,128)S(1)}, f32[3,16,16,128]{3,2,1,0:T(8,128)}, u32[]{:S(2)}) copy-start(f32[3,16,16,128]{3,2,1,0:T(8,128)} %param.16) | copy-start | bytes 1179652
  0.7 49.7 %copy-start.1 = (f32[3,16,16,128]{3,2,1,0:T(8,128)S(1)}, f32[3,16,16,128]{3,2,1,0:T(8,128)}, u32[]{:S(2)}) copy-start(f32[3,16,16,128]{3,2,1,0:T(8,128)} %param.17) | copy-start | bytes 1179652
  1.8 31.8 %collective-permute-start = (f32[2,16,128]{2,1,0:T(8,128)S(1)}, f32[2,16,128]{2,1,0:T(8,128)S(1)}, u32[]{:S(2)}, u32[]{:S(2)}) collective-permute-start(f32[2,16,128]{2,1,0:T(8,128)S(1)} %fusion.55), channel_id=1, source_target_pairs={{2,0},{4,2},{6,4},{3,1},{5,3},{7,5},{10,8},{12,10},{14,12},{11,9},... | collective-permute-start | bytes 49160 | tf_op jit(solution)/shard_map/ppermute | solution.py:23
  4.3 27.2 %collective-permute-start.1 = (f32[2,256]{1,0:T(2,128)S(1)}, f32[2,256]{1,0:T(2,128)S(1)}, u32[]{:S(2)}, u32[]{:S(2)}) collective-permute-start(f32[2,256]{1,0:T(2,128)S(1)} %reshape_squeeze.24), channel_id=1, source_target_pairs={{1,0},{3,2},{5,4},{7,6},{9,8},{11,10},{13,12},{15,14},{17,16},{19,... | collective-permute-start | bytes 6152 | tf_op jit(solution)/shard_map/ppermute | solution.py:23
  6.5 27.1 %collective-permute-start.2 = (f32[2,16,128]{2,1,0:T(8,128)S(1)}, f32[2,16,128]{2,1,0:T(8,128)S(1)}, u32[]{:S(2)}, u32[]{:S(2)}) collective-permute-start(f32[2,16,128]{2,1,0:T(8,128)S(1)} %bitcast.137), channel_id=1, source_target_pairs={{8,0},{16,8},{24,16},{9,1},{17,9},{25,17},{10,2},{18,10},{26,18},{... | collective-permute-start | bytes 49160 | tf_op jit(solution)/shard_map/ppermute | solution.py:23
  10.7 1.0 copy-start.15
  12.4 19.3 %all-to-all-start.1 = ((f32[1,16,32]{2,0,1:T(1,128)}), f32[1,16,32]{2,0,1:T(1,128)S(1)}, u32[]{:S(2)}, u32[]{:S(2)}) async-start(f32[1,16,32]{2,0,1:T(1,128)} %all_to_all.14), calls=%async_computation.1 | async-start | bytes 16384 | tf_op jit(solution)/shard_map/all_to_all | solution.py:152
  25.2 6.3 %copy-start.13 = (pred[16,16,128]{2,1,0:T(8,128)(4,1)}, pred[16,16,128]{2,1,0:T(8,128)(4,1)S(1)}, u32[]{:S(2)}) copy-start(pred[16,16,128]{2,1,0:T(8,128)(4,1)S(1)} %get-tuple-element.31) | copy-start | bytes 98308
  35.5 0.6 copy-start.11
  38.1 11.3 %collective-permute-start.3 = (f32[2,16,128]{2,1,0:T(8,128)}, f32[2,16,128]{2,1,0:T(8,128)S(1)}, u32[]{:S(2)}, u32[]{:S(2)}) collective-permute-start(f32[2,16,128]{2,1,0:T(8,128)} %fusion.56), channel_id=1, source_target_pairs={{0,2},{2,4},{4,6},{1,3},{3,5},{5,7},{8,10},{10,12},{12,14},{9,11},... | collective-permute-start | bytes 49160 | tf_op jit(solution)/shard_map/ppermute | solution.py:23
  42.0 6.5 %collective-permute-start.4 = (f32[2,256]{1,0:T(2,128)S(1)}, f32[2,256]{1,0:T(2,128)}, u32[]{:S(2)}, u32[]{:S(2)}) collective-permute-start(f32[2,256]{1,0:T(2,128)S(1)} %reshape_squeeze.25), channel_id=1, source_target_pairs={{0,1},{2,3},{4,5},{6,7},{8,9},{10,11},{12,13},{14,15},{16,17},{18,... | collective-permute-start | bytes 6152 | tf_op jit(solution)/shard_map/ppermute | solution.py:23
  45.2 5.0 %collective-permute-start.5 = (f32[2,16,128]{2,1,0:T(8,128)}, f32[2,16,128]{2,1,0:T(8,128)S(1)}, u32[]{:S(2)}, u32[]{:S(2)}) collective-permute-start(f32[2,16,128]{2,1,0:T(8,128)} %bitcast.8), channel_id=1, source_target_pairs={{0,8},{8,16},{16,24},{1,9},{9,17},{17,25},{2,10},{10,18},{18,26},{... | collective-permute-start | bytes 49160 | tf_op jit(solution)/shard_map/ppermute | solution.py:23
  50.4 1.2 copy-start.4
  52.6 14.8 %collective-permute-start.6 = (f32[2,16,128]{2,1,0:T(8,128)S(1)}, f32[2,16,128]{2,1,0:T(8,128)S(1)}, u32[]{:S(2)}, u32[]{:S(2)}) collective-permute-start(f32[2,16,128]{2,1,0:T(8,128)S(1)} %fusion.57), channel_id=1, source_target_pairs={{2,0},{4,2},{6,4},{3,1},{5,3},{7,5},{10,8},{12,10},{14,12},{11,9},... | collective-permute-start | bytes 49160 | tf_op jit(solution)/shard_map/ppermute | solution.py:23
  53.9 10.3 %collective-permute-start.7 = (f32[2,256]{1,0:T(2,128)S(1)}, f32[2,256]{1,0:T(2,128)S(1)}, u32[]{:S(2)}, u32[]{:S(2)}) collective-permute-start(f32[2,256]{1,0:T(2,128)S(1)} %reshape_squeeze.26), channel_id=1, source_target_pairs={{1,0},{3,2},{5,4},{7,6},{9,8},{11,10},{13,12},{15,14},{17,16},{19,... | collective-permute-start | bytes 6152 | tf_op jit(solution)/shard_map/ppermute | solution.py:23
  55.3 11.2 %collective-permute-start.13 = (f32[2,256]{1,0:T(2,128)S(1)}, f32[2,256]{1,0:T(2,128)S(1)}, u32[]{:S(2)}, u32[]{:S(2)}) collective-permute-start(f32[2,256]{1,0:T(2,128)S(1)} %reshape_squeeze.28), channel_id=1, source_target_pairs={{1,0},{3,2},{5,4},{7,6},{9,8},{11,10},{13,12},{15,14},{17,16},{19,... | collective-permute-start | bytes 6152 | tf_op jit(solution)/shard_map/ppermute | solution.py:23
  61.7 6.7 %collective-permute-start.8 = (f32[2,16,128]{2,1,0:T(8,128)S(1)}, f32[2,16,128]{2,1,0:T(8,128)S(1)}, u32[]{:S(2)}, u32[]{:S(2)}) collective-permute-start(f32[2,16,128]{2,1,0:T(8,128)S(1)} %bitcast.138), channel_id=1, source_target_pairs={{8,0},{16,8},{24,16},{9,1},{17,9},{25,17},{10,2},{18,10},{26,18},{... | collective-permute-start | bytes 49160 | tf_op jit(solution)/shard_map/ppermute | solution.py:23
  62.9 8.9 %collective-permute-start.12 = (f32[2,16,128]{2,1,0:T(8,128)}, f32[2,16,128]{2,1,0:T(8,128)}, u32[]{:S(2)}, u32[]{:S(2)}) collective-permute-start(f32[2,16,128]{2,1,0:T(8,128)} %fusion.59), channel_id=1, source_target_pairs={{2,0},{4,2},{6,4},{3,1},{5,3},{7,5},{10,8},{12,10},{14,12},{11,9},... | collective-permute-start | bytes 49160 | tf_op jit(solution)/shard_map/ppermute | solution.py:23
  64.3 8.6 %collective-permute-start.14 = (f32[2,16,128]{2,1,0:T(8,128)}, f32[2,16,128]{2,1,0:T(8,128)S(1)}, u32[]{:S(2)}, u32[]{:S(2)}) collective-permute-start(f32[2,16,128]{2,1,0:T(8,128)} %bitcast.25), channel_id=1, source_target_pairs={{8,0},{16,8},{24,16},{9,1},{17,9},{25,17},{10,2},{18,10},{26,18},{... | collective-permute-start | bytes 49160 | tf_op jit(solution)/shard_map/ppermute | solution.py:23
  75.9 26.3 %collective-permute-start.9 = (f32[2,16,128]{2,1,0:T(8,128)S(1)}, f32[2,16,128]{2,1,0:T(8,128)S(1)}, u32[]{:S(2)}, u32[]{:S(2)}) collective-permute-start(f32[2,16,128]{2,1,0:T(8,128)S(1)} %fusion.58), channel_id=1, source_target_pairs={{0,2},{2,4},{4,6},{1,3},{3,5},{5,7},{8,10},{10,12},{12,14},{9,11},... | collective-permute-start | bytes 49160 | tf_op jit(solution)/shard_map/ppermute | solution.py:23
  81.1 15.6 %collective-permute-start.10 = (f32[2,256]{1,0:T(2,128)S(1)}, f32[2,256]{1,0:T(2,128)S(1)}, u32[]{:S(2)}, u32[]{:S(2)}) collective-permute-start(f32[2,256]{1,0:T(2,128)S(1)} %reshape_squeeze.27), channel_id=1, source_target_pairs={{0,1},{2,3},{4,5},{6,7},{8,9},{10,11},{12,13},{14,15},{16,17},{18,... | collective-permute-start | bytes 6152 | tf_op jit(solution)/shard_map/ppermute | solution.py:23
  84.0 17.3 %collective-permute-start.16 = (f32[2,256]{1,0:T(2,128)S(1)}, f32[2,256]{1,0:T(2,128)S(1)}, u32[]{:S(2)}, u32[]{:S(2)}) collective-permute-start(f32[2,256]{1,0:T(2,128)S(1)} %reshape_squeeze.29), channel_id=1, source_target_pairs={{0,1},{2,3},{4,5},{6,7},{8,9},{10,11},{12,13},{14,15},{16,17},{18,... | collective-permute-start | bytes 6152 | tf_op jit(solution)/shard_map/ppermute | solution.py:23
  86.7 16.5 %collective-permute-start.11 = (f32[2,16,128]{2,1,0:T(8,128)S(1)}, f32[2,16,128]{2,1,0:T(8,128)S(1)}, u32[]{:S(2)}, u32[]{:S(2)}) collective-permute-start(f32[2,16,128]{2,1,0:T(8,128)S(1)} %bitcast.139), channel_id=1, source_target_pairs={{0,8},{8,16},{16,24},{1,9},{9,17},{17,25},{2,10},{10,18},{18,26},{... | collective-permute-start | bytes 49160 | tf_op jit(solution)/shard_map/ppermute | solution.py:23
  92.2 12.4 %collective-permute-start.17 = (f32[2,16,128]{2,1,0:T(8,128)S(1)}, f32[2,16,128]{2,1,0:T(8,128)S(1)}, u32[]{:S(2)}, u32[]{:S(2)}) collective-permute-start(f32[2,16,128]{2,1,0:T(8,128)S(1)} %bitcast.131), channel_id=1, source_target_pairs={{0,8},{8,16},{16,24},{1,9},{9,17},{17,25},{2,10},{10,18},{18,26},{... | collective-permute-start | bytes 49160 | tf_op jit(solution)/shard_map/ppermute | solution.py:23
  96.7 7.8 %collective-permute-start.15 = (f32[2,16,128]{2,1,0:T(8,128)S(1)}, f32[2,16,128]{2,1,0:T(8,128)S(1)}, u32[]{:S(2)}, u32[]{:S(2)}) collective-permute-start(f32[2,16,128]{2,1,0:T(8,128)S(1)} %fusion.54), channel_id=1, source_target_pairs={{0,2},{2,4},{4,6},{1,3},{3,5},{5,7},{8,10},{10,12},{12,14},{9,11},... | collective-permute-start | bytes 49160 | tf_op jit(solution)/shard_map/ppermute | solution.py:23
  105.8 12.1 %copy-start.14 = (s32[16,32]{1,0:T(8,128)S(1)}, s32[16,32]{1,0:T(8,128)}, u32[]{:S(2)}) copy-start(s32[16,32]{1,0:T(8,128)} %multiply_add_fusion.2) | copy-start | bytes 6148
  105.8 12.1 %copy-start.16 = (s32[256,1]{0,1:T(1,128)S(1)}, s32[256,1]{0,1:T(1,128)}, u32[]{:S(2)}) copy-start(s32[256,1]{0,1:T(1,128)} %copy-done.15) | copy-start | bytes 3076
  105.9 1.3 copy-start.5
  105.9 1.3 copy-start.7
  105.9 1.3 copy-start.9
  108.5 22.2 %collective-permute-start.18 = (f32[2,16,128]{2,1,0:T(8,128)S(1)}, f32[2,16,128]{2,1,0:T(8,128)S(1)}, u32[]{:S(2)}, u32[]{:S(2)}) collective-permute-start(f32[2,16,128]{2,1,0:T(8,128)S(1)} %fusion.60), channel_id=1, source_target_pairs={{2,0},{4,2},{6,4},{3,1},{5,3},{7,5},{10,8},{12,10},{14,12},{11,9},... | collective-permute-start | bytes 49160 | tf_op jit(solution)/shard_map/ppermute | solution.py:23
  109.9 19.9 %collective-permute-start.19 = (f32[2,256]{1,0:T(2,128)S(1)}, f32[2,256]{1,0:T(2,128)S(1)}, u32[]{:S(2)}, u32[]{:S(2)}) collective-permute-start(f32[2,256]{1,0:T(2,128)S(1)} %reshape_squeeze.30), channel_id=1, source_target_pairs={{1,0},{3,2},{5,4},{7,6},{9,8},{11,10},{13,12},{15,14},{17,16},{19,... | collective-permute-start | bytes 6152 | tf_op jit(solution)/shard_map/ppermute | solution.py:23
  117.9 31.9 %copy-start.6 = (f32[1,16,16,128]{3,2,1,0:T(8,128)S(1)}, f32[1,16,16,128]{3,2,1,0:T(8,128)}, u32[]{:S(2)}) copy-start(f32[1,16,16,128]{3,2,1,0:T(8,128)} %copy-done.5) | copy-start | bytes 393220
  117.9 31.9 %copy-start.8 = (f32[1,16,16,128]{3,2,1,0:T(8,128)S(1)}, f32[1,16,16,128]{3,2,1,0:T(8,128)}, u32[]{:S(2)}) copy-start(f32[1,16,16,128]{3,2,1,0:T(8,128)} %copy-done.7) | copy-start | bytes 393220
  117.9 31.9 %copy-start.10 = (f32[1,16,16,128]{3,2,1,0:T(8,128)S(1)}, f32[1,16,16,128]{3,2,1,0:T(8,128)}, u32[]{:S(2)}) copy-start(f32[1,16,16,128]{3,2,1,0:T(8,128)} %copy-done.9) | copy-start | bytes 393220
  121.8 30.9 %all-to-all-start = ((f32[16,1,2048]{2,1,0:T(1,128)}), f32[16,1,2048]{2,1,0:T(1,128)}, u32[]{:S(2)}, u32[]{:S(2)}) async-start(f32[16,1,2048]{2,1,0:T(1,128)} %reshape.199), calls=%async_computation | async-start | bytes 262144 | tf_op jit(solution)/shard_map/all_to_all | solution.py:151
  128.5 5.9 %collective-permute-start.20 = (f32[2,16,128]{2,1,0:T(8,128)S(1)}, f32[2,16,128]{2,1,0:T(8,128)S(1)}, u32[]{:S(2)}, u32[]{:S(2)}) collective-permute-start(f32[2,16,128]{2,1,0:T(8,128)S(1)} %bitcast.140), channel_id=1, source_target_pairs={{8,0},{16,8},{24,16},{9,1},{17,9},{25,17},{10,2},{18,10},{26,18},{... | collective-permute-start | bytes 49160 | tf_op jit(solution)/shard_map/ppermute | solution.py:23
  137.1 11.5 %collective-permute-start.21 = (f32[2,16,128]{2,1,0:T(8,128)}, f32[2,16,128]{2,1,0:T(8,128)S(1)}, u32[]{:S(2)}, u32[]{:S(2)}) collective-permute-start(f32[2,16,128]{2,1,0:T(8,128)} %fusion.61), channel_id=1, source_target_pairs={{0,2},{2,4},{4,6},{1,3},{3,5},{5,7},{8,10},{10,12},{12,14},{9,11},... | collective-permute-start | bytes 49160 | tf_op jit(solution)/shard_map/ppermute | solution.py:23
  140.8 6.9 %collective-permute-start.22 = (f32[2,256]{1,0:T(2,128)S(1)}, f32[2,256]{1,0:T(2,128)}, u32[]{:S(2)}, u32[]{:S(2)}) collective-permute-start(f32[2,256]{1,0:T(2,128)S(1)} %reshape_squeeze.31), channel_id=1, source_target_pairs={{0,1},{2,3},{4,5},{6,7},{8,9},{10,11},{12,13},{14,15},{16,17},{18,... | collective-permute-start | bytes 6152 | tf_op jit(solution)/shard_map/ppermute | solution.py:23
  143.6 6.0 %collective-permute-start.23 = (f32[2,16,128]{2,1,0:T(8,128)}, f32[2,16,128]{2,1,0:T(8,128)S(1)}, u32[]{:S(2)}, u32[]{:S(2)}) collective-permute-start(f32[2,16,128]{2,1,0:T(8,128)} %bitcast.40), channel_id=1, source_target_pairs={{0,8},{8,16},{16,24},{1,9},{9,17},{17,25},{2,10},{10,18},{18,26},{... | collective-permute-start | bytes 49160 | tf_op jit(solution)/shard_map/ppermute | solution.py:23
  152.6 4.3 %copy-start.12 = (f32[3,16,16,128]{3,2,1,0:T(8,128)}, f32[3,16,16,128]{3,2,1,0:T(8,128)S(1)}, u32[]{:S(2)}) copy-start(f32[3,16,16,128]{3,2,1,0:T(8,128)S(1)} %fusion.36) | copy-start | bytes 1179652
where the time goes:
time: 159 us; the launch traced here: 157 us
  starting transfers between devices  75 us (47%)
  other arithmetic  42.2 us (27%)
  local copies, waits for them, and re-layouts  24.8 us (16%)
  matrix products  9.91 us (6%)
  waiting for transfers between devices  3.4 us (2%)
  between operations  1.65 us (1%)
    ppermute x24, starting transfers between devices, passed_along(): return lax.ppermute(x, axis, pairs)  57.7 us
    all_to_all x1, starting transfers between devices, local(): lax.all_to_all(send_ids, ('bx', 'by'), split_axis=1, concat_axis=1, tiled...  10.5 us
    sub x8, other arithmetic, differ(): return neighbour - couple  7.75 us
    all_to_all x1, starting transfers between devices, local(): lax.all_to_all(send_vals, ('bx', 'by'), split_axis=1, concat_axis=1, tile...  6.72 us
    dot_general x1, matrix products, local(): jnp.einsum('tfkc,tc->tfk', blocks, cell_tiles, preferred_element_type=jnp...  6.71 us
    another operation x8, local copies, waits for them, and re-layouts, beside(): arrived = jnp.expand_dims(arrived, axis_dim)  6.51 us
    slice x8, local copies, waits for them, and re-layouts, beside(): lax.slice_in_dim(couple, 1, length, axis=axis_dim)  5.31 us
    sub x7, other arithmetic, differ(): return couple - neighbour  4.77 us
  transfers between devices with their start and end apart: 26, of which 2 were waited for; matrix products, arithmetic and copies ran while one was open for 36% of the time, Pallas kernels for 0%

commit v1 on v0

v1 whole, which is shorter than its diff:
```python
import functools

import jax
import jax.numpy as jnp
from jax import lax
from jax.experimental import pallas as pl
from jax.experimental.pallas import tpu as pltpu
from jax.sharding import PartitionSpec as P

KB = 64
GRP_DEV = 128

time_step = 0.5
drude_keep = 0.9
drude_gain = 1.0
metal_permit = 3.0
design_contrast = 5.0
source_level = 3.0
source_wave = (1.0, -0.6, 0.8, -0.4)

PAIRS, SINGLES = 9, 4
UNITS = 2 * PAIRS + SINGLES
UNITS_PAD = 24
ARRAYS = PAIRS + SINGLES
F32 = jnp.float32
BF16 = jnp.bfloat16
LIMIT = 56 * 1024 * 1024


def is_even(axis):
    return lax.rem(lax.axis_index(axis), 2) == 0


def lanes(shape):
    return lax.broadcasted_iota(jnp.int32, shape, len(shape) - 1)


def prepare_kernel(cells_ref, e_ref, h_ref, j_ref, c_ref, level_ref, mat_ref,
                   fa_ref, fb_ref, b_ref, s_ref, r_ref, w_ref, j1_ref, q_ref):
    ny, nx, nz = mat_ref.shape
    flat = lax.broadcasted_iota(jnp.int32, (nx, nz), 0) * nz + lanes((nx, nz))

    def row(y, carry):
        mat = mat_ref[y]
        silver, design = mat == 2, mat == 1
        smooth = 1.0 / (1.0 + jnp.exp(-level_ref[y]))
        permit = jnp.where(silver, metal_permit, jnp.where(design, 1.0 + design_contrast * smooth, 1.0))
        ratio = time_step / permit
        r_ref[y] = jnp.where(silver, -ratio, ratio)
        w_ref[y] = jnp.where(design, (-design_contrast / time_step) * ratio * smooth * (1.0 - smooth), 0.0)
        count = jnp.zeros((nx, nz), F32)
        for i in range(cells_ref.shape[0]):
            count = count + jnp.where(flat + y * (nx * nz) == cells_ref[i], 1.0, 0.0)
        q_ref[y] = count
        for c in range(3):
            current = jnp.where(silver, drude_keep * j_ref[c, y] + drude_gain * e_ref[c, y], 0.0)
            j1_ref[c, y] = current
            start = e_ref[c, y] - ratio * current
            if c == 2:
                start = start + (source_level * source_wave[0]) * count
            b_ref[c, y] = start
            s_ref[c, y] = ratio * c_ref[c, y]
        return carry

    lax.fori_loop(0, ny, row, 0, unroll=2)

    def face(out, low, near):
        for k, ref in enumerate((e_ref, h_ref, s_ref)):
            for c in range(3):
                for d in range(2):
                    out[6 * k + 2 * c + d] = ref[c, low + d]
        for c in range(3):
            out[18 + c] = b_ref[c, near]
        out[21] = r_ref[near]

    even = is_even("by")

    @pl.when(even)
    def _():
        face(fa_ref, ny - 2, ny - 1)
        face(fb_ref, 0, 0)

    @pl.when(jnp.logical_not(even))
    def _():
        face(fb_ref, ny - 2, ny - 1)
        face(fa_ref, 0, 0)


def x_face_kernel(e_ref, h_ref, s_ref, b_ref, r_ref, ga_ref, gb_ref, xa_ref, xb_ref):
    ny, nx, nz = r_ref.shape
    y_even, x_even = is_even("by"), is_even("bx")

    def face(out, low, near):
        out[:, UNITS:, :] = jnp.zeros((ny + 4, UNITS_PAD - UNITS, nz), F32)
        for k, ref in enumerate((e_ref, h_ref, s_ref)):
            for c in range(3):
                u = 6 * k + 2 * c
                out[2:ny + 2, u:u + 2, :] = ref[c, :, low:low + 2, :]
                for d in range(2):
                    ga, gb = ga_ref[u + d], gb_ref[u + d]
                    out[d, u:u + 2, :] = jnp.where(y_even, gb, ga)[low:low + 2]
                    out[ny + 2 + d, u:u + 2, :] = jnp.where(y_even, ga, gb)[low:low + 2]
        zero = jnp.zeros((SINGLES, nz), F32)
        out[0, 18:UNITS, :] = zero
        out[ny + 3, 18:UNITS, :] = zero
        for u in range(18, UNITS):
            if u < 21:
                out[2:ny + 2, u:u + 1, :] = b_ref[u - 18, :, near:near + 1, :]
            else:
                out[2:ny + 2, u:u + 1, :] = r_ref[:, near:near + 1, :]
            ga, gb = ga_ref[u], gb_ref[u]
            out[1, u:u + 1, :] = jnp.where(y_even, gb, ga)[near:near + 1]
            out[ny + 2, u:u + 1, :] = jnp.where(y_even, ga, gb)[near:near + 1]

    @pl.when(x_even)
    def _():
        face(xa_ref, nx - 2, nx - 1)
        face(xb_ref, 0, 0)

    @pl.when(jnp.logical_not(x_even))
    def _():
        face(xb_ref, nx - 2, nx - 1)
        face(xa_ref, 0, 0)


def extend_kernel(e_ref, h_ref, s_ref, b_ref, r_ref, ga_ref, gb_ref, xa_ref, xb_ref,
                  ext_ref, zp_ref, acc_ref):
    ny, nx, nz = r_ref.shape
    wy, wx = ny + 4, nx + 8
    y_even, x_even = is_even("by"), is_even("bx")
    gz0 = lax.axis_index("gz") == 0
    own = [ref.at[c] for ref in (e_ref, h_ref, s_ref, b_ref) for c in range(3)] + [r_ref]
    ext_ref[:, :, nx:, :] = jnp.zeros((ARRAYS, wy, wx - nx, nz), F32)
    for i in range(ARRAYS):
        ext_ref[i, 2:ny + 2, 0:nx, :] = own[i][...]
        u, deep = (2 * i, 2) if i < PAIRS else (9 + i, 1)
        for d in range(2):
            if deep == 2:
                ga, gb = ga_ref[u + d], gb_ref[u + d]
                ext_ref[i, d, 0:nx, :] = jnp.where(y_even, gb, ga)
                ext_ref[i, ny + 2 + d, 0:nx, :] = jnp.where(y_even, ga, gb)
            else:
                ga, gb, zero = ga_ref[u], gb_ref[u], jnp.zeros((nx, nz), F32)
                ext_ref[i, d, 0:nx, :] = jnp.where(y_even, gb, ga) if d == 1 else zero
                ext_ref[i, ny + 2 + d, 0:nx, :] = jnp.where(y_even, ga, gb) if d == 0 else zero
        xa, xb = xa_ref[:, u:u + deep, :], xb_ref[:, u:u + deep, :]
        ext_ref[i, :, nx:nx + deep, :] = jnp.where(x_even, xa, xb)
        ext_ref[i, :, wx - deep:, :] = jnp.where(x_even, xb, xa)

    lane = lanes((wx, nz))
    back = jnp.where(gz0, 1, 0)

    def pack(y, carry):
        acc = jnp.zeros((wx, nz), F32)
        for i in range(ARRAYS):
            if i < PAIRS:
                acc = jnp.where(lane // 2 == i, pltpu.roll(ext_ref[i, y], 2 * i + 2 * back, 1), acc)
            else:
                acc = jnp.where(lane == 9 + i, pltpu.roll(ext_ref[i, y], 9 + i + back, 1), acc)
        acc_ref[pl.ds(pl.multiple_of(y * wx, 8), wx), :] = acc
        return carry

    lax.fori_loop(0, wy, pack, 0, unroll=2)
    full = acc_ref.shape[0]
    acc_ref[wy * wx:, :] = jnp.zeros((full - wy * wx, nz), F32)
    zp_ref[...] = acc_ref[...].T[:UNITS_PAD]


def curl_of(dx, dy, dz):
    return dy[2] - dz[1], dz[0] - dx[2], dx[1] - dy[0]


def slab_planes(slab_ref, wx, by0, bx0):
    full = slab_ref.shape[2]
    lane = lanes((8, full))
    line = (lane * 683) >> 14
    column = lane - line * wx
    mask = jnp.where((by0 & (line < 2)) | (bx0 & (column >= wx - 2)), 0.0, 1.0)

    def plus(f):
        ahead = lambda a: jnp.where(column == wx - 1, pltpu.roll(a, wx - 1, 1), pltpu.roll(a, full - 1, 1)) - a
        return curl_of(
            (None, ahead(f[1]), ahead(f[2])),
            (pltpu.roll(f[0], full - wx, 1) - f[0], None, pltpu.roll(f[2], full - wx, 1) - f[2]),
            (pltpu.roll(f[0], 7, 0) - f[0], pltpu.roll(f[1], 7, 0) - f[1]),
        )

    def minus(f):
        behind = lambda a: a - jnp.where(column == 0, pltpu.roll(a, full - wx + 1, 1), pltpu.roll(a, 1, 1))
        return curl_of(
            (None, behind(f[1]), behind(f[2])),
            (f[0] - pltpu.roll(f[0], wx, 1), None, f[2] - pltpu.roll(f[2], wx, 1)),
            (f[0] - pltpu.roll(f[0], 1, 0), f[1] - pltpu.roll(f[1], 1, 0)),
        )

    e, h, s, b = ([slab_ref[3 * k + c] for c in range(3)] for k in range(4))
    code = slab_ref[12]
    ratio = jnp.abs(code)
    h1 = [(a - time_step * d) * mask for a, d in zip(h, plus(e))]
    g1 = [d * mask for d in plus(s)]
    e1 = [a + ratio * d for a, d in zip(b, minus(h1))]
    s1 = [jnp.where(code < 0, a * (1.0 - ratio), a) - time_step * ratio * d for a, d in zip(s, minus(g1))]
    h2 = [(a - time_step * d) * mask for a, d in zip(h1, plus(e1))]
    g2 = [(a + d) * mask for a, d in zip(g1, plus(s1))]
    return (e, e1, s, s1), (h1, h2, g1, g2)


def main_kernel(ext_ref, zo_ref, zg_ref, j1_ref, c_ref, w_ref, q_ref, place_ref, ids_ref, basis_ref,
                e2_ref, a0_ref, send_ref,
                slab_ref, plane_ref, col_ref, h1_ref, g1_ref, e1_ref, s1_ref, h2_ref, g2_ref,
                d1_ref, d2_ref, cell_ref, blocks_ref, sem):
    fetch = pltpu.make_async_copy(basis_ref, blocks_ref, sem)
    fetch.start()
    ny, nx, nz = w_ref.shape
    wy, wx = ny + 4, nx + 8
    by0, bx0 = lax.axis_index("by") == 0, lax.axis_index("bx") == 0
    gz0 = lax.axis_index("gz") == 0

    for i in range(ARRAYS):
        u, deep = (2 * i, 2) if i < PAIRS else (9 + i, 1)
        mine, other = zo_ref[u:u + deep, :], zg_ref[u:u + deep, :]
        slab_ref[i] = jnp.zeros(slab_ref.shape[1:], F32)
        slab_ref[i, 2 - deep:2, :] = jnp.where(gz0, mine, other)
        slab_ref[i, 2:2 + deep, :] = jnp.where(gz0, other, mine)
    upper, lower = slab_planes(slab_ref, wx, by0, bx0)
    plane_ref[...] = jnp.zeros(plane_ref.shape, F32)
    for p in range(4):
        for c in range(2):
            plane_ref[2 * p + c:2 * p + c + 1, :] = jnp.where(gz0, upper[p][c][2:3], lower[p][c][1:2])
    col_ref[...] = plane_ref[...].T

    lane = lanes((wx, nz))
    column = lax.broadcasted_iota(jnp.int32, (wx, nz), 0)
    x_mask = jnp.where(bx0 & (column >= wx - 2), 0.0, 1.0)
    up_part, low_part = jnp.where(gz0, 1.0, 0.0), jnp.where(gz0, 0.0, 1.0)

    def mask_of(y):
        return x_mask * jnp.where(by0 & (y < 2), 0.0, 1.0)

    def cols_of(y):
        return col_ref[pl.ds(pl.multiple_of(y * wx, 8), wx), :]

    def plus(ref, y, cols, p):
        f, g = [ref[c, y] for c in range(3)], [ref[c, y + 1] for c in (0, 2)]
        dz = []
        for c in range(2):
            k = 2 * p + c
            beyond = (pltpu.roll(cols, nz - k, 1) if k else cols) * up_part
            dz.append(pltpu.roll(jnp.where(lane == 0, beyond, f[c]), nz - 1, 1) - f[c])
        dx = [None] + [pltpu.roll(f[c], wx - 1, 0) - f[c] for c in (1, 2)]
        return curl_of(dx, (g[0] - f[0], None, g[1] - f[2]), dz)

    def minus(ref, y, cols, p):
        f, g = [ref[c, y] for c in range(3)], [ref[c, y - 1] for c in (0, 2)]
        dz = []
        for c in range(2):
            k = 2 * p + c
            beyond = pltpu.roll(cols, nz - 1 - k, 1) * low_part
            dz.append(f[c] - pltpu.roll(jnp.where(lane == nz - 1, beyond, f[c]), 1, 1))
        dx = [None] + [f[c] - pltpu.roll(f[c], 1, 0) for c in (1, 2)]
        return curl_of(dx, (f[0] - g[0], None, f[2] - g[1]), dz)

    e_ext, h_ext, s_ext, b_ext = (ext_ref.at[3 * k:3 * k + 3] for k in range(4))

    def first_magnetic(y, carry):
        cols, mask = cols_of(y), mask_of(y)
        for c, d in enumerate(plus(e_ext, y, cols, 0)):
            h1_ref[c, y] = (h_ext[c, y] - time_step * d) * mask
        for c, d in enumerate(plus(s_ext, y, cols, 2)):
            g1_ref[c, y] = d * mask
        return carry

    def first_electric(y, carry):
        cols, code = cols_of(y), ext_ref[12, y]
        ratio = jnp.abs(code)
        for c, d in enumerate(minus(h1_ref, y, cols, 0)):
            d1_ref[c, y] = d[:nx]
            e1_ref[c, y] = b_ext[c, y] + ratio * d
        for c, d in enumerate(minus(g1_ref, y, cols, 2)):
            d2_ref[c, y] = d[:nx]
            s = s_ext[c, y]
            s1_ref[c, y] = jnp.where(code < 0, s * (1.0 - ratio), s) - time_step * ratio * d
        return carry

    def second_magnetic(y, carry):
        cols, mask = cols_of(y), mask_of(y)
        for c, d in enumerate(plus(e1_ref, y, cols, 1)):
            h2_ref[c, y] = (h1_ref[c, y] - time_step * d) * mask
        for c, d in enumerate(plus(s1_ref, y, cols, 3)):
            g2_ref[c, y] = (g1_ref[c, y] + d) * mask
        return carry

    def second_electric(y, carry):
        cols, at = cols_of(y), y - 2
        code = ext_ref[12, y, 0:nx, :]
        ratio, silver = jnp.abs(code), code < 0
        eps = jnp.zeros((nx, nz), F32)
        for c, (d, g) in enumerate(zip(minus(h2_ref, y, cols, 1), minus(g2_ref, y, cols, 3))):
            e1, s1, s = e1_ref[c, y, 0:nx, :], s1_ref[c, y, 0:nx, :], s_ext[c, y, 0:nx, :]
            j1 = j1_ref[c, at]
            drive = d[:nx] - jnp.where(silver, drude_keep * j1 + drude_gain * e1, 0.0)
            final = e1 + ratio * drive
            if c == 2:
                final = final + (source_level * source_wave[1]) * q_ref[at]
            e2_ref[c, at] = final
            eps = eps + s * drive + s1 * (d1_ref[c, y] - j1)
            back = c_ref[c, at] - time_step * (d2_ref[c, y] + g[:nx])
            a0_ref[c, at] = back - jnp.where(silver, drude_gain * ((1.0 + drude_keep) * s + s1), 0.0)
        cell_ref[pl.ds(pl.multiple_of(at * nx, 8), nx), :] = w_ref[at] * eps
        return carry

    lax.fori_loop(0, wy - 1, first_magnetic, 0)
    lax.fori_loop(1, wy - 1, first_electric, 0)
    lax.fori_loop(1, wy - 2, second_magnetic, 0)
    lax.fori_loop(2, wy - 2, second_electric, 0)

    tiles = ny * nx // 2
    cells = jnp.concatenate([cell_ref[pl.ds(0, tiles, stride=2), :], cell_ref[pl.ds(1, tiles, stride=2), :]], axis=1)
    cells = cells.astype(BF16)
    fetch.wait()
    tile_rows = blocks_ref.shape[0] // tiles
    group = 8
    at_lane = lanes((tile_rows, tiles))

    def project(n, acc):
        start = pl.multiple_of(n * (group * tile_rows), group * tile_rows)
        prods = lax.dot_general(blocks_ref[pl.ds(start, group * tile_rows), :], cells,
                                (((1,), (1,)), ((), ())), preferred_element_type=F32)
        for i in range(group):
            acc = jnp.where(at_lane == n * group + i, prods[i * tile_rows:(i + 1) * tile_rows], acc)
        return acc

    acc = lax.fori_loop(0, tiles // group, project, jnp.zeros((tile_rows, tiles), F32))
    partial = jnp.concatenate([acc[:KB], acc[KB:]], axis=1)
    high = partial.astype(BF16)
    low = (partial - high.astype(F32)).astype(BF16)
    zero = jnp.zeros(high.shape, BF16)
    out = jnp.zeros((place_ref.shape[1], 2 * KB), F32)
    for part in (high, low):
        for half in range(2):
            rows = jnp.concatenate([part, zero] if half == 0 else [zero, part], axis=0)
            out = out + lax.dot_general(place_ref[half], rows, (((1,), (1,)), ((), ())), preferred_element_type=F32)
    planes, width, _ = send_ref.shape
    send_ref[...] = out.reshape(planes, width, 2 * KB)
    id_row = rows_of(planes, place_ref.shape[2])
    for d in range(planes):
        send_ref[d, id_row:id_row + 1, :] = ids_ref[d:d + 1, :]


def capacity_of(planes, blocks):
    return max(2, 2 * blocks // planes)


def rows_of(planes, blocks):
    return capacity_of(planes, blocks) // 2


def place_kernel(rows, width, owner_ref, group_ref, place_ref, ids_ref):
    blocks = owner_ref.shape[1]
    planes = ids_ref.shape[0]
    row, column = (lax.broadcasted_iota(jnp.int32, (blocks, blocks), k) for k in range(2))
    half = blocks // 2
    swap = jnp.where(row == jnp.where(column < half, 2 * column, 2 * (column - half) + 1), 1.0, 0.0).astype(BF16)

    def arranged(ref):
        wide = jnp.broadcast_to(ref[...].astype(F32), (8, blocks)).astype(BF16)
        return lax.dot_general(wide, swap, (((1,), (0,)), ((), ())), preferred_element_type=F32)[:1]

    owner, group = arranged(owner_ref), arranged(group_ref)
    plane = lax.broadcasted_iota(jnp.int32, (planes, blocks), 0).astype(F32)
    hits = jnp.where(plane == owner, 1.0, 0.0)
    earlier = jnp.where(row < column, 1.0, 0.0).astype(BF16)
    before = lax.dot_general(hits.astype(BF16), earlier, (((1,), (0,)), ((), ())), preferred_element_type=F32)
    rank = jnp.sum(before * hits, axis=0, keepdims=True)
    slots = place_ref.shape[1]
    slot = lax.broadcasted_iota(jnp.int32, (slots, blocks), 0).astype(F32)
    for k in range(2):
        inner = rank - float(k * rows)
        target = jnp.where((inner >= 0.0) & (inner < float(rows)), owner * float(width) + inner, -1.0)
        place_ref[k] = jnp.where(slot == target, 1.0, 0.0).astype(BF16)
    ranks = lax.broadcasted_iota(jnp.int32, (128, blocks), 0).astype(F32)
    ranked = jnp.where(ranks == rank, 1.0, 0.0).astype(BF16)
    named = (hits * (group + 1.0)).astype(BF16)
    ids_ref[...] = lax.dot_general(named, ranked, (((1,), (1,)), ((), ())), preferred_element_type=F32) - 1.0


def collect_kernel(rows, got_ref, coef_ref):
    planes, width, line = got_ref.shape
    shape = (planes, width, line)
    ids = jnp.broadcast_to(got_ref[:, rows:rows + 1, :], shape)
    place = lax.broadcasted_iota(jnp.int32, shape, 1)
    lane = lanes(shape)
    values = got_ref[...].reshape(planes * width, line).T
    high = values.astype(BF16)
    low = (values - high.astype(F32)).astype(BF16)
    parts = []
    for k in range(2):
        mine = jnp.sum(jnp.where(lane == place + k * rows, ids + 1.0, 0.0), axis=2, keepdims=True)
        mine = jnp.where(place < rows, mine, 0.0)
        hits = jnp.where(mine == lane.astype(F32) + 1.0, 1.0, 0.0).astype(BF16)
        hits = hits.reshape(planes * width, line)
        dots = [lax.dot_general(part, hits, (((1,), (0,)), ((), ())), preferred_element_type=F32) for part in (high, low)]
        parts.append((dots[0] + dots[1])[k * KB:(k + 1) * KB])
    coef_ref[...] = parts[0] + parts[1]


def call(kernel, outs, ins, scratch=(), smem_first=False, any_last=False, flops=100000):
    specs = [pl.BlockSpec(memory_space=pltpu.VMEM) for _ in ins]
    if smem_first:
        specs[0] = pl.BlockSpec(memory_space=pltpu.SMEM)
    if any_last:
        specs[-1] = pl.BlockSpec(memory_space=pl.ANY)
    return pl.pallas_call(
        kernel,
        out_shape=[jax.ShapeDtypeStruct(*o) for o in outs],
        in_specs=specs,
        out_specs=[pl.BlockSpec(memory_space=pltpu.VMEM) for _ in outs],
        scratch_shapes=list(scratch),
        compiler_params=pltpu.CompilerParams(vmem_limit_bytes=LIMIT),
    )(*ins)


def swapped(first, second, axis):
    size = lax.axis_size(axis)
    arrived = []
    for start, value in ((0, first), (1, second)):
        pairs = []
        for low in range(start, size - 1, 2):
            pairs += [(low, low + 1), (low + 1, low)]
        arrived.append(lax.ppermute(value, axis, pairs) if pairs else jnp.zeros_like(value))
    return arrived


def local(electric_start, magnetic_start, current_start, cotangent, level_set, material, source_cell, basis,
          block_owner, block_group):
    ny, nx, nz = material.shape
    wy, wx = ny + 4, nx + 8
    field, scalar = ((3, ny, nx, nz), F32), ((ny, nx, nz), F32)
    blocks = basis.shape[0]
    planes = lax.axis_size("bx") * lax.axis_size("by")
    rows = rows_of(planes, blocks)
    width = -(-(rows + 1) // 8) * 8
    place, ids = call(
        functools.partial(place_kernel, rows, width),
        [((2, planes * width, blocks), BF16), ((planes, 128), F32)],
        [block_owner.reshape(1, blocks), block_group.reshape(1, blocks)],
    )
    face = ((UNITS, nx, nz), F32)
    fa, fb, b, s, r, w, j1, q = call(
        prepare_kernel,
        [face, face, field, field, scalar, scalar, field, scalar],
        [source_cell, electric_start, magnetic_start, current_start, cotangent, level_set, material],
        smem_first=True,
    )
    ga, gb = swapped(fa, fb, "by")
    x_face = ((wy, UNITS_PAD, nz), F32)
    xa, xb = call(x_face_kernel, [x_face, x_face], [electric_start, magnetic_start, s, b, r, ga, gb])
    xa, xb = swapped(xa, xb, "bx")
    full = -(-wy * wx // 128) * 128
    ext, zp = call(
        extend_kernel,
        [((ARRAYS, wy, wx, nz), F32), ((UNITS_PAD, full), F32)],
        [electric_start, magnetic_start, s, b, r, ga, gb, xa, xb],
        scratch=[pltpu.VMEM((full, nz), F32)],
    )
    zg = lax.ppermute(zp, "gz", [(0, 1), (1, 0)])
    wide = pltpu.VMEM((3, wy, wx, nz), F32)
    inner = pltpu.VMEM((3, wy, nx, nz), F32)
    electric, adjoint, send = call(
        main_kernel,
        [field, field, ((planes, width, 2 * KB), F32)],
        [ext, zp, zg, j1, cotangent, w, q, place, ids, basis.reshape(blocks * KB, basis.shape[2])],
        scratch=[
            pltpu.VMEM((ARRAYS, 8, full), F32),
            pltpu.VMEM((128, full), F32),
            pltpu.VMEM((full, 128), F32),
            wide, wide, wide, wide, wide, wide,
            inner, inner,
            pltpu.VMEM((ny * nx, nz), F32),
            pltpu.VMEM((blocks * KB, basis.shape[2]), BF16),
            pltpu.SemaphoreType.DMA,
        ],
        any_last=True,
    )
    got = lax.all_to_all(send, ("bx", "by"), split_axis=0, concat_axis=0, tiled=True)
    (coef,) = call(functools.partial(collect_kernel, rows), [((KB, GRP_DEV), F32)], [got])
    return electric, adjoint, coef


def solution(mesh):
    field = P(None, "by", "bx", "gz")
    scalar = P("by", "bx", "gz")
    flat = ("bx", "by", "gz")
    return jax.shard_map(
        local,
        mesh=mesh,
        in_specs=(field, field, field, field, scalar, scalar, P(flat), P(flat, None, None), P(flat, None), P(flat)),
        out_specs=(field, field, P(None, flat)),
        check_vma=False,
    )
```

time: 159 us -> 75.7 us (0.48); the launches traced: 157 us -> 75.3 us
  starting transfers between devices: 75 us -> 6.01 us
  other arithmetic: 42.2 us -> 0 us
  Pallas kernels: 0 us -> 33.7 us
  local copies, waits for them, and re-layouts: 24.8 us -> 2.7 us
  blocking collectives: 0 us -> 21.8 us
  matrix products: 9.91 us -> 0 us
  waiting for transfers between devices: 3.4 us -> 10.4 us
    ppermute x24 -> x5, starting transfers between devices: 57.7 us -> 6.01 us  [the longest x4 6 us: swapped(): lax.ppermute(value, axis, pairs)]
    pallas_call x0 -> x6, Pallas kernels: none -> 33.7 us  [call(): pl.pallas_call(kernel, out_shape=[jax.ShapeDtypeStruct(*o) for o in outs]...]
    all_to_all x0 -> x1, blocking collectives: none -> 21.8 us  [local(): lax.all_to_all(send, ('bx', 'by'), split_axis=0, concat_axis=0, tiled=True)]
    sub x27 -> x0, other arithmetic: 17.6 us -> none  [the longest x8 7.75 us: differ(): return neighbour - couple]
    all_to_all x2 -> x0, starting transfers between devices: 17.2 us -> none  [the longest x1 10.5 us: local(): lax.all_to_all(send_ids, ('bx', 'by'), split_axis=1, concat_axis=1, tiled...]
    slice x33 -> x0, local copies, waits for them, and re-layouts: 12.4 us -> none  [the longest x8 5.31 us: beside(): lax.slice_in_dim(couple, 1, length, axis=axis_dim)]
    dot_general x4 -> x0, matrix products: 9.91 us -> none  [the longest x1 6.71 us: local(): jnp.einsum('tfkc,tc->tfk', blocks, cell_tiles, preferred_element_type=jnp...]
    another operation x19 -> x0, local copies, waits for them, and re-layouts: 7.33 us -> none  [the longest x8 6.51 us: beside(): arrived = jnp.expand_dims(arrived, axis_dim)]
  transfers between devices with their start and end apart: 26 -> 5, of which waited for: 2 -> 2; matrix products, arithmetic and copies ran while one was open for 36% -> 0% of each run, Pallas kernels for 0% -> 2%
where the time goes in v1:
time: 75.7 us; the launch traced here: 75.3 us
  Pallas kernels  33.7 us (45%)
  blocking collectives  21.8 us (29%)
  waiting for transfers between devices  10.4 us (14%)
  starting transfers between devices  6.01 us (8%)
  local copies, waits for them, and re-layouts  2.7 us (4%)
    pallas_call x6, Pallas kernels, call(): pl.pallas_call(kernel, out_shape=[jax.ShapeDtypeStruct(*o) for o in outs]...  33.7 us
    all_to_all x1, blocking collectives, local(): lax.all_to_all(send, ('bx', 'by'), split_axis=0, concat_axis=0, tiled=True)  21.8 us
    ppermute x4, waiting for transfers between devices, swapped(): lax.ppermute(value, axis, pairs)  10.4 us
    ppermute x4, starting transfers between devices, swapped(): lax.ppermute(value, axis, pairs)  6 us
    unnamed x10, local copies, waits for them, and re-layouts  2.7 us
  transfers between devices with their start and end apart: 5, of which 2 were waited for; matrix products, arithmetic and copies ran while one was open for 0% of the time, Pallas kernels for 2%

profile of v1, /device:TPU:0, one launch (start us, length us, event | category | flops | bytes accessed | tf_op | source)
XLA Modules:
  0.0 75.3 jit_solution(7411583098180918250)
XLA Ops:
  0.6 3.1 %shard_map.121 = (f32[22,16,128]{2,1,0:T(8,128)}, f32[22,16,128]{2,1,0:T(8,128)}, f32[3,16,16,128]{3,2,1,0:T(8,128)}, f32[3,16,16,128]{3,2,1,0:T(8,128)}, f32[16...) custom-call(s32[8]{0:T(128)} %cells_ref.1, ...), custom_call_target="tpu_custom_call" | custom-call | tf_op jit(solution)/shard_map/pallas_call | solution.py:413
  3.7 3.0 %collective-permute-start = (f32[22,16,128]{2,1,0:T(8,128)}, f32[22,16,128]{2,1,0:T(8,128)S(1)}, u32[]{:S(2)}, u32[]{:S(2)}) collective-permute-start(f32[22,16,128]{2,1,0:T(8,128)} %get-tuple-element.23), channel_id=1, source_target_pairs={{0,2},{2,0},{4,6},{6,4},{1,3},{3,1},{5,7},{7,5},{8,10},{10,8},{12,... | collective-permute-start | bytes 540680 | tf_op jit(solution)/shard_map/ppermute | solution.py:430
  6.7 0.7 collective-permute-start.1
  7.4 4.1 %collective-permute-done.ga_ref = f32[22,16,128]{2,1,0:T(8,128)S(1)} collective-permute-done((f32[22,16,128]{2,1,0:T(8,128)}, f32[22,16,128]{2,1,0:T(8,128)S(1)}, u32[]{:S(2)}, u32[]{:S(2)}) %collective-permute-start) | collective-permute-done | bytes 180256 | tf_op jit(solution)/shard_map/ppermute | solution.py:430
  11.5 0.0 copy-start
  11.5 0.0 collective-permute-done.1.gb_ref
  11.5 0.0 copy-start.1
  11.5 0.7 copy-done
  12.2 0.1 copy-done.1
  12.2 2.5 %shard_map.122 = (f32[20,24,128]{2,1,0:T(8,128)}, f32[20,24,128]{2,1,0:T(8,128)}) custom-call(f32[3,16,16,128]{3,2,1,0:T(8,128)} %e_ref.5, f32[3,16,16,128]{3,2,1,0:T(8,128)} %h_ref.5, f32[3,16,16,128]{3,2,1,0:T(8,128)} %get-tuple-element.20.s_ref, f32[3,16,16,128]{3,2,1,0:T(8,128)} %get-tuple-element.21.b_ref, f32[16,16,128]{2,1,0:T(8,128)} %get-tuple-element.22.r_ref, ...), custom_call_target="tpu_custom_call" | custom-call | tf_op jit(solution)/shard_map/pallas_call | solution.py:413
  14.7 1.7 %collective-permute-start.2 = (f32[20,24,128]{2,1,0:T(8,128)}, f32[20,24,128]{2,1,0:T(8,128)S(1)}, u32[]{:S(2)}, u32[]{:S(2)}) collective-permute-start(f32[20,24,128]{2,1,0:T(8,128)} %get-tuple-element.25), channel_id=1, source_target_pairs={{0,8},{8,0},{16,24},{24,16},{1,9},{9,1},{17,25},{25,17},{2,10},{10... | collective-permute-start | bytes 737288 | tf_op jit(solution)/shard_map/ppermute | solution.py:430
  16.3 0.7 collective-permute-start.3
  17.0 6.3 %collective-permute-done.2.xa_ref = f32[20,24,128]{2,1,0:T(8,128)S(1)} collective-permute-done((f32[20,24,128]{2,1,0:T(8,128)}, f32[20,24,128]{2,1,0:T(8,128)S(1)}, u32[]{:S(2)}, u32[]{:S(2)}) %collective-permute-start.2) | collective-permute-done | bytes 245792 | tf_op jit(solution)/shard_map/ppermute | solution.py:430
  23.3 0.0 copy-start.2
  23.3 0.0 collective-permute-done.3.xb_ref
  23.3 0.7 copy-done.2
  24.0 0.0 copy-start.3
  24.0 0.7 copy-done.3
  24.7 5.1 %shard_map.123 = (f32[13,20,24,128]{3,2,1,0:T(8,128)}, f32[24,512]{1,0:T(8,128)}) custom-call(f32[3,16,16,128]{3,2,1,0:T(8,128)} %e_ref.5, f32[3,16,16,128]{3,2,1,0:T(8,128)} %h_ref.5, f32[3,16,16,128]{3,2,1,0:T(8,128)} %get-tuple-element.20.s_ref, f32[3,16,16,128]{3,2,1,0:T(8,128)} %get-tuple-element.21.b_ref, f32[16,16,128]{2,1,0:T(8,128)} %get-tuple-element.22.r_ref, ...), custom_call_target="tpu_custom_call" | custom-call | tf_op jit(solution)/shard_map/pallas_call | solution.py:413
  29.7 0.0 collective-permute-start.4
  29.7 1.8 %shard_map.124 = (bf16[2,384,256]{2,1,0:T(8,128)(2,1)}, f32[16,128]{1,0:T(8,128)}) custom-call(s32[1,256]{1,0:T(1,128)} %bitcast.4, s32[1,256]{1,0:T(1,128)} %bitcast.5), custom_call_target="tpu_custom_call" | custom-call | tf_op jit(solution)/shard_map/pallas_call | solution.py:413
  31.6 0.0 collective-permute-done.4.zg_ref
  31.6 0.0 copy-start.4
  31.6 0.6 copy-done.4
  32.2 19.4 %shard_map.125 = (f32[3,16,16,128]{3,2,1,0:T(8,128)}, f32[3,16,16,128]{3,2,1,0:T(8,128)}, f32[16,24,128]{2,1,0:T(8,128)}) custom-call(f32[13,20,24,128]{3,2,1,0:T(8,128)} %get-tuple-element.27.ext_ref, f32[24,512]{1,0:T(8,128)} %get-tuple-element.28.zo_ref, f32[24,512]{1,0:T(8,128)} %copy-done.4, f32[3,16,16,128]{3,2,1,0:T(8,128)} %get-tuple-element.29.j1_ref, ...), custom_call_target="tpu_custom_call" | custom-call | tf_op jit(solution)/shard_map/pallas_call | solution.py:413
  51.6 21.8 %all_to_all.5.got_ref = f32[16,24,128]{2,1,0:T(8,128)} all-to-all(f32[16,24,128]{2,1,0:T(8,128)} %get-tuple-element.36), channel_id=1, replica_groups=mesh['bx'=4,'by'=4,'gz'=2] {'bx','by'}, dimensions={0} | all-to-all | bytes 393216 | tf_op jit(solution)/shard_map/all_to_all | solution.py:485
  73.4 2.0 %shard_map.126 = f32[64,128]{1,0:T(8,128)} custom-call(f32[16,24,128]{2,1,0:T(8,128)} %all_to_all.5.got_ref), custom_call_target="tpu_custom_call" | custom-call | tf_op jit(solution)/shard_map/pallas_call | solution.py:413
Async XLA Ops:
  3.7 7.8 %collective-permute-start = (f32[22,16,128]{2,1,0:T(8,128)}, f32[22,16,128]{2,1,0:T(8,128)S(1)}, u32[]{:S(2)}, u32[]{:S(2)}) collective-permute-start(f32[22,16,128]{2,1,0:T(8,128)} %get-tuple-element.23), channel_id=1, source_target_pairs={{0,2},{2,0},{4,6},{6,4},{1,3},{3,1},{5,7},{7,5},{8,10},{10,8},{12,... | collective-permute-start | bytes 540680 | tf_op jit(solution)/shard_map/ppermute | solution.py:430
  6.7 4.8 %collective-permute-start.1 = (f32[22,16,128]{2,1,0:T(8,128)}, f32[22,16,128]{2,1,0:T(8,128)S(1)}, u32[]{:S(2)}, u32[]{:S(2)}) collective-permute-start(f32[22,16,128]{2,1,0:T(8,128)} %get-tuple-element.24), channel_id=1, source_target_pairs={{2,4},{4,2},{3,5},{5,3},{10,12},{12,10},{11,13},{13,11},{18,20},{2... | collective-permute-start | bytes 540680 | tf_op jit(solution)/shard_map/ppermute | solution.py:430
  11.5 0.7 copy-start
  11.5 0.7 copy-start.1
  14.7 8.7 %collective-permute-start.2 = (f32[20,24,128]{2,1,0:T(8,128)}, f32[20,24,128]{2,1,0:T(8,128)S(1)}, u32[]{:S(2)}, u32[]{:S(2)}) collective-permute-start(f32[20,24,128]{2,1,0:T(8,128)} %get-tuple-element.25), channel_id=1, source_target_pairs={{0,8},{8,0},{16,24},{24,16},{1,9},{9,1},{17,25},{25,17},{2,10},{10... | collective-permute-start | bytes 737288 | tf_op jit(solution)/shard_map/ppermute | solution.py:430
  16.3 7.0 %collective-permute-start.3 = (f32[20,24,128]{2,1,0:T(8,128)}, f32[20,24,128]{2,1,0:T(8,128)S(1)}, u32[]{:S(2)}, u32[]{:S(2)}) collective-permute-start(f32[20,24,128]{2,1,0:T(8,128)} %get-tuple-element.26), channel_id=1, source_target_pairs={{8,16},{16,8},{9,17},{17,9},{10,18},{18,10},{11,19},{19,11},{12,20... | collective-permute-start | bytes 737288 | tf_op jit(solution)/shard_map/ppermute | solution.py:430
  23.3 0.7 copy-start.2
  24.0 0.7 copy-start.3
  29.7 1.8 %collective-permute-start.4 = (f32[24,512]{1,0:T(8,128)}, f32[24,512]{1,0:T(8,128)S(1)}, u32[]{:S(2)}, u32[]{:S(2)}) collective-permute-start(f32[24,512]{1,0:T(8,128)} %get-tuple-element.28.zo_ref), channel_id=1, source_target_pairs={{0,1},{1,0},{2,3},{3,2},{4,5},{5,4},{6,7},{7,6},{8,9},{9,8},{10,11... | collective-permute-start | bytes 147464 | tf_op jit(solution)/shard_map/ppermute | solution.py:466
  31.6 0.6 copy-start.4

commit v2 on v1

--- a/solution.py
+++ b/solution.py
@@ -24,7 +24,6 @@
 ARRAYS = PAIRS + SINGLES
 F32 = jnp.float32
 BF16 = jnp.bfloat16
-LIMIT = 56 * 1024 * 1024
 
 
 def is_even(axis):
@@ -36,7 +35,7 @@
 
 
 def prepare_kernel(cells_ref, e_ref, h_ref, j_ref, c_ref, level_ref, mat_ref,
-                   fa_ref, fb_ref, b_ref, s_ref, r_ref, w_ref, j1_ref, q_ref):
+                   fa_ref, fb_ref, xa_ref, xb_ref, own_ref, w_ref, j1_ref, q_ref, c_out_ref):
     ny, nx, nz = mat_ref.shape
     flat = lax.broadcasted_iota(jnp.int32, (nx, nz), 0) * nz + lanes((nx, nz))
 
@@ -46,93 +45,87 @@
         smooth = 1.0 / (1.0 + jnp.exp(-level_ref[y]))
         permit = jnp.where(silver, metal_permit, jnp.where(design, 1.0 + design_contrast * smooth, 1.0))
         ratio = time_step / permit
-        r_ref[y] = jnp.where(silver, -ratio, ratio)
+        own_ref[12, y] = jnp.where(silver, -ratio, ratio)
         w_ref[y] = jnp.where(design, (-design_contrast / time_step) * ratio * smooth * (1.0 - smooth), 0.0)
         count = jnp.zeros((nx, nz), F32)
         for i in range(cells_ref.shape[0]):
             count = count + jnp.where(flat + y * (nx * nz) == cells_ref[i], 1.0, 0.0)
         q_ref[y] = count
         for c in range(3):
-            current = jnp.where(silver, drude_keep * j_ref[c, y] + drude_gain * e_ref[c, y], 0.0)
+            electric, weight = e_ref[c, y], c_ref[c, y]
+            current = jnp.where(silver, drude_keep * j_ref[c, y] + drude_gain * electric, 0.0)
             j1_ref[c, y] = current
-            start = e_ref[c, y] - ratio * current
+            start = electric - ratio * current
             if c == 2:
                 start = start + (source_level * source_wave[0]) * count
-            b_ref[c, y] = start
-            s_ref[c, y] = ratio * c_ref[c, y]
-        return carry
-
-    lax.fori_loop(0, ny, row, 0, unroll=2)
+            own_ref[c, y] = electric
+            own_ref[3 + c, y] = h_ref[c, y]
+            own_ref[6 + c, y] = ratio * weight
+            own_ref[9 + c, y] = start
+            c_out_ref[c, y] = weight
+        return carry
+
+    lax.fori_loop(0, ny, row, 0, unroll=4)
+
+    def y_face(out, low, near):
+        for i in range(PAIRS):
+            for d in range(2):
+                out[2 * i + d] = own_ref[i, low + d]
+        for i in range(PAIRS, ARRAYS):
+            out[9 + i] = own_ref[i, near]
+
+    def x_face(out, low, near):
+        out[:, UNITS:, :] = jnp.zeros((ny, UNITS_PAD - UNITS, nz), F32)
+        for i in range(PAIRS):
+            out[:, 2 * i:2 * i + 2, :] = own_ref[i, :, low:low + 2, :]
+        for i in range(PAIRS, ARRAYS):
+            out[:, 9 + i:10 + i, :] = own_ref[i, :, near:near + 1, :]
+
+    for face, even, a_ref, b_ref, n in ((y_face, is_even("by"), fa_ref, fb_ref, ny), (x_face, is_even("bx"), xa_ref, xb_ref, nx)):
+        @pl.when(even)
+        def _():
+            face(a_ref, n - 2, n - 1)
+            face(b_ref, 0, 0)
+
+        @pl.when(jnp.logical_not(even))
+        def _():
+            face(b_ref, n - 2, n - 1)
+            face(a_ref, 0, 0)
+
+
+def corner_kernel(ga_ref, gb_ref, ca_ref, cb_ref):
+    nx, nz = ga_ref.shape[1:]
+    y_even, x_even = is_even("by"), is_even("bx")
 
     def face(out, low, near):
-        for k, ref in enumerate((e_ref, h_ref, s_ref)):
-            for c in range(3):
-                for d in range(2):
-                    out[6 * k + 2 * c + d] = ref[c, low + d]
-        for c in range(3):
-            out[18 + c] = b_ref[c, near]
-        out[21] = r_ref[near]
-
-    even = is_even("by")
-
-    @pl.when(even)
-    def _():
-        face(fa_ref, ny - 2, ny - 1)
-        face(fb_ref, 0, 0)
-
-    @pl.when(jnp.logical_not(even))
-    def _():
-        face(fb_ref, ny - 2, ny - 1)
-        face(fa_ref, 0, 0)
-
-
-def x_face_kernel(e_ref, h_ref, s_ref, b_ref, r_ref, ga_ref, gb_ref, xa_ref, xb_ref):
-    ny, nx, nz = r_ref.shape
-    y_even, x_even = is_even("by"), is_even("bx")
-
-    def face(out, low, near):
-        out[:, UNITS:, :] = jnp.zeros((ny + 4, UNITS_PAD - UNITS, nz), F32)
-        for k, ref in enumerate((e_ref, h_ref, s_ref)):
-            for c in range(3):
-                u = 6 * k + 2 * c
-                out[2:ny + 2, u:u + 2, :] = ref[c, :, low:low + 2, :]
-                for d in range(2):
-                    ga, gb = ga_ref[u + d], gb_ref[u + d]
-                    out[d, u:u + 2, :] = jnp.where(y_even, gb, ga)[low:low + 2]
-                    out[ny + 2 + d, u:u + 2, :] = jnp.where(y_even, ga, gb)[low:low + 2]
-        zero = jnp.zeros((SINGLES, nz), F32)
-        out[0, 18:UNITS, :] = zero
-        out[ny + 3, 18:UNITS, :] = zero
-        for u in range(18, UNITS):
-            if u < 21:
-                out[2:ny + 2, u:u + 1, :] = b_ref[u - 18, :, near:near + 1, :]
-            else:
-                out[2:ny + 2, u:u + 1, :] = r_ref[:, near:near + 1, :]
-            ga, gb = ga_ref[u], gb_ref[u]
-            out[1, u:u + 1, :] = jnp.where(y_even, gb, ga)[near:near + 1]
-            out[ny + 2, u:u + 1, :] = jnp.where(y_even, ga, gb)[near:near + 1]
+        out[...] = jnp.zeros(out.shape, F32)
+        for i in range(ARRAYS):
+            u, deep = (2 * i, 2) if i < PAIRS else (9 + i, 1)
+            first = low if deep == 2 else near
+            for d in range(deep):
+                ga, gb = ga_ref[u + d], gb_ref[u + d]
+                out[d if deep == 2 else 1, u:u + deep, :] = jnp.where(y_even, gb, ga)[first:first + deep]
+                out[2 + d, u:u + deep, :] = jnp.where(y_even, ga, gb)[first:first + deep]
 
     @pl.when(x_even)
     def _():
-        face(xa_ref, nx - 2, nx - 1)
-        face(xb_ref, 0, 0)
+        face(ca_ref, nx - 2, nx - 1)
+        face(cb_ref, 0, 0)
 
     @pl.when(jnp.logical_not(x_even))
     def _():
-        face(xb_ref, nx - 2, nx - 1)
-        face(xa_ref, 0, 0)
-
-
-def extend_kernel(e_ref, h_ref, s_ref, b_ref, r_ref, ga_ref, gb_ref, xa_ref, xb_ref,
-                  ext_ref, zp_ref, acc_ref):
-    ny, nx, nz = r_ref.shape
+        face(cb_ref, nx - 2, nx - 1)
+        face(ca_ref, 0, 0)
+
+
+def extend_kernel(own_ref, ga_ref, gb_ref, xa_ref, xb_ref, ca_ref, cb_ref, ext_ref, zp_ref, acc_ref):
+    ny, nx, nz = own_ref.shape[1:]
     wy, wx = ny + 4, nx + 8
     y_even, x_even = is_even("by"), is_even("bx")
     gz0 = lax.axis_index("gz") == 0
-    own = [ref.at[c] for ref in (e_ref, h_ref, s_ref, b_ref) for c in range(3)] + [r_ref]
     ext_ref[:, :, nx:, :] = jnp.zeros((ARRAYS, wy, wx - nx, nz), F32)
     for i in range(ARRAYS):
-        ext_ref[i, 2:ny + 2, 0:nx, :] = own[i][...]
+        ext_ref[i, 2:ny + 2, 0:nx, :] = own_ref[i]
         u, deep = (2 * i, 2) if i < PAIRS else (9 + i, 1)
         for d in range(2):
             if deep == 2:
@@ -143,9 +136,11 @@
                 ga, gb, zero = ga_ref[u], gb_ref[u], jnp.zeros((nx, nz), F32)
                 ext_ref[i, d, 0:nx, :] = jnp.where(y_even, gb, ga) if d == 1 else zero
                 ext_ref[i, ny + 2 + d, 0:nx, :] = jnp.where(y_even, ga, gb) if d == 0 else zero
-        xa, xb = xa_ref[:, u:u + deep, :], xb_ref[:, u:u + deep, :]
-        ext_ref[i, :, nx:nx + deep, :] = jnp.where(x_even, xa, xb)
-        ext_ref[i, :, wx - deep:, :] = jnp.where(x_even, xb, xa)
+        for a_ref, b_ref, first, last, to in ((xa_ref, xb_ref, 0, ny, 2), (ca_ref, cb_ref, 0, 2, 0), (ca_ref, cb_ref, 2, 4, ny + 2)):
+            a, b = a_ref[first:last, u:u + deep, :], b_ref[first:last, u:u + deep, :]
+            rows = slice(to, to + last - first)
+            ext_ref[i, rows, nx:nx + deep, :] = jnp.where(x_even, a, b)
+            ext_ref[i, rows, wx - deep:, :] = jnp.where(x_even, b, a)
 
     lane = lanes((wx, nz))
     back = jnp.where(gz0, 1, 0)
@@ -160,7 +155,7 @@
         acc_ref[pl.ds(pl.multiple_of(y * wx, 8), wx), :] = acc
         return carry
 
-    lax.fori_loop(0, wy, pack, 0, unroll=2)
+    lax.fori_loop(0, wy, pack, 0, unroll=4)
     full = acc_ref.shape[0]
     acc_ref[wy * wx:, :] = jnp.zeros((full - wy * wx, nz), F32)
     zp_ref[...] = acc_ref[...].T[:UNITS_PAD]
@@ -205,12 +200,10 @@
     return (e, e1, s, s1), (h1, h2, g1, g2)
 
 
-def main_kernel(ext_ref, zo_ref, zg_ref, j1_ref, c_ref, w_ref, q_ref, place_ref, ids_ref, basis_ref,
+def main_kernel(ext_ref, zo_ref, zg_ref, j1_ref, c_ref, w_ref, q_ref, place_ref, ids_ref, blocks_ref,
                 e2_ref, a0_ref, send_ref,
                 slab_ref, plane_ref, col_ref, h1_ref, g1_ref, e1_ref, s1_ref, h2_ref, g2_ref,
-                d1_ref, d2_ref, cell_ref, blocks_ref, sem):
-    fetch = pltpu.make_async_copy(basis_ref, blocks_ref, sem)
-    fetch.start()
+                d1_ref, d2_ref, cell_ref):
     ny, nx, nz = w_ref.shape
     wy, wx = ny + 4, nx + 8
     by0, bx0 = lax.axis_index("by") == 0, lax.axis_index("bx") == 0
@@ -309,17 +302,16 @@
         cell_ref[pl.ds(pl.multiple_of(at * nx, 8), nx), :] = w_ref[at] * eps
         return carry
 
-    lax.fori_loop(0, wy - 1, first_magnetic, 0)
-    lax.fori_loop(1, wy - 1, first_electric, 0)
-    lax.fori_loop(1, wy - 2, second_magnetic, 0)
-    lax.fori_loop(2, wy - 2, second_electric, 0)
+    lax.fori_loop(0, wy - 1, first_magnetic, 0, unroll=4)
+    lax.fori_loop(1, wy - 1, first_electric, 0, unroll=4)
+    lax.fori_loop(1, wy - 2, second_magnetic, 0, unroll=4)
+    lax.fori_loop(2, wy - 2, second_electric, 0, unroll=4)
 
     tiles = ny * nx // 2
     cells = jnp.concatenate([cell_ref[pl.ds(0, tiles, stride=2), :], cell_ref[pl.ds(1, tiles, stride=2), :]], axis=1)
     cells = cells.astype(BF16)
-    fetch.wait()
     tile_rows = blocks_ref.shape[0] // tiles
-    group = 8
+    group = 32
     at_lane = lanes((tile_rows, tiles))
 
     def project(n, acc):
@@ -330,7 +322,7 @@
             acc = jnp.where(at_lane == n * group + i, prods[i * tile_rows:(i + 1) * tile_rows], acc)
         return acc
 
-    acc = lax.fori_loop(0, tiles // group, project, jnp.zeros((tile_rows, tiles), F32))
+    acc = lax.fori_loop(0, tiles // group, project, jnp.zeros((tile_rows, tiles), F32), unroll=2)
     partial = jnp.concatenate([acc[:KB], acc[KB:]], axis=1)
     high = partial.astype(BF16)
     low = (partial - high.astype(F32)).astype(BF16)
@@ -355,7 +347,9 @@
     return capacity_of(planes, blocks) // 2
 
 
-def place_kernel(rows, width, owner_ref, group_ref, place_ref, ids_ref):
+def place_kernel(rows, width, owner_ref, group_ref, basis_ref, place_ref, ids_ref, blocks_ref, sem):
+    fetch = pltpu.make_async_copy(basis_ref, blocks_ref, sem)
+    fetch.start()
     blocks = owner_ref.shape[1]
     planes = ids_ref.shape[0]
     row, column = (lax.broadcasted_iota(jnp.int32, (blocks, blocks), k) for k in range(2))
@@ -382,6 +376,7 @@
     ranked = jnp.where(ranks == rank, 1.0, 0.0).astype(BF16)
     named = (hits * (group + 1.0)).astype(BF16)
     ids_ref[...] = lax.dot_general(named, ranked, (((1,), (1,)), ((), ())), preferred_element_type=F32) - 1.0
+    fetch.wait()
 
 
 def collect_kernel(rows, got_ref, coef_ref):
@@ -404,20 +399,18 @@
     coef_ref[...] = parts[0] + parts[1]
 
 
-def call(kernel, outs, ins, scratch=(), smem_first=False, any_last=False, flops=100000):
-    specs = [pl.BlockSpec(memory_space=pltpu.VMEM) for _ in ins]
-    if smem_first:
-        specs[0] = pl.BlockSpec(memory_space=pltpu.SMEM)
-    if any_last:
-        specs[-1] = pl.BlockSpec(memory_space=pl.ANY)
+def call(kernel, outs, ins, scratch=(), places=None, leave=0, limit=16, cost=None):
+    spaces = places or [pltpu.VMEM] * len(ins)
+    keep = lambda a, space: pltpu.with_memory_space_constraint(a, space) if space is pltpu.VMEM else a
     return pl.pallas_call(
         kernel,
-        out_shape=[jax.ShapeDtypeStruct(*o) for o in outs],
-        in_specs=specs,
+        out_shape=[jax.ShapeDtypeStruct(*o) if i < leave else pltpu.VMEM(*o) for i, o in enumerate(outs)],
+        in_specs=[pl.BlockSpec(memory_space=pltpu.VMEM if space is None else space) for space in spaces],
         out_specs=[pl.BlockSpec(memory_space=pltpu.VMEM) for _ in outs],
         scratch_shapes=list(scratch),
-        compiler_params=pltpu.CompilerParams(vmem_limit_bytes=LIMIT),
-    )(*ins)
+        compiler_params=pltpu.CompilerParams(vmem_limit_bytes=limit * 1024 * 1024),
+        cost_estimate=cost,
+    )(*[keep(a, space) for a, space in zip(ins, spaces)])
 
 
 def swapped(first, second, axis):
@@ -440,27 +433,31 @@
     planes = lax.axis_size("bx") * lax.axis_size("by")
     rows = rows_of(planes, blocks)
     width = -(-(rows + 1) // 8) * 8
-    place, ids = call(
-        functools.partial(place_kernel, rows, width),
-        [((2, planes * width, blocks), BF16), ((planes, 128), F32)],
-        [block_owner.reshape(1, blocks), block_group.reshape(1, blocks)],
-    )
-    face = ((UNITS, nx, nz), F32)
-    fa, fb, b, s, r, w, j1, q = call(
+    y_face, x_face, corner = ((UNITS, nx, nz), F32), ((ny, UNITS_PAD, nz), F32), ((4, UNITS_PAD, nz), F32)
+    fa, fb, xa, xb, own, w, j1, q, weight = call(
         prepare_kernel,
-        [face, face, field, field, scalar, scalar, field, scalar],
+        [y_face, y_face, x_face, x_face, ((ARRAYS, ny, nx, nz), F32), scalar, field, scalar, field],
         [source_cell, electric_start, magnetic_start, current_start, cotangent, level_set, material],
-        smem_first=True,
+        places=[pltpu.SMEM] + [None] * 6, limit=58,
     )
     ga, gb = swapped(fa, fb, "by")
-    x_face = ((wy, UNITS_PAD, nz), F32)
-    xa, xb = call(x_face_kernel, [x_face, x_face], [electric_start, magnetic_start, s, b, r, ga, gb])
     xa, xb = swapped(xa, xb, "bx")
+    ca, cb = call(corner_kernel, [corner, corner], [ga, gb])
+    ca, cb, owner, group = lax.optimization_barrier((ca, cb, block_owner.reshape(1, blocks), block_group.reshape(1, blocks)))
+    ca, cb = swapped(ca, cb, "bx")
+    place, ids, basis_here = call(
+        functools.partial(place_kernel, rows, width),
+        [((2, planes * width, blocks), BF16), ((planes, 128), F32), ((blocks * KB, basis.shape[2]), BF16)],
+        [owner, group, basis.reshape(blocks * KB, basis.shape[2])],
+        scratch=[pltpu.SemaphoreType.DMA],
+        places=[None, None, pltpu.HBM], limit=46,
+    )
+    ca, cb, ids = lax.optimization_barrier((ca, cb, ids))
     full = -(-wy * wx // 128) * 128
     ext, zp = call(
         extend_kernel,
         [((ARRAYS, wy, wx, nz), F32), ((UNITS_PAD, full), F32)],
-        [electric_start, magnetic_start, s, b, r, ga, gb, xa, xb],
+        [own, ga, gb, xa, xb, ca, cb],
         scratch=[pltpu.VMEM((full, nz), F32)],
     )
     zg = lax.ppermute(zp, "gz", [(0, 1), (1, 0)])
@@ -469,7 +466,7 @@
     electric, adjoint, send = call(
         main_kernel,
         [field, field, ((planes, width, 2 * KB), F32)],
-        [ext, zp, zg, j1, cotangent, w, q, place, ids, basis.reshape(blocks * KB, basis.shape[2])],
+        [ext, zp, zg, j1, weight, w, q, place, ids, basis_here],
         scratch=[
             pltpu.VMEM((ARRAYS, 8, full), F32),
             pltpu.VMEM((128, full), F32),
@@ -477,13 +474,12 @@
             wide, wide, wide, wide, wide, wide,
             inner, inner,
             pltpu.VMEM((ny * nx, nz), F32),
-            pltpu.VMEM((blocks * KB, basis.shape[2]), BF16),
-            pltpu.SemaphoreType.DMA,
         ],
-        any_last=True,
+        leave=2,
+        limit=24,
     )
     got = lax.all_to_all(send, ("bx", "by"), split_axis=0, concat_axis=0, tiled=True)
-    (coef,) = call(functools.partial(collect_kernel, rows), [((KB, GRP_DEV), F32)], [got])
+    (coef,) = call(functools.partial(collect_kernel, rows), [((KB, GRP_DEV), F32)], [got], leave=1)
     return electric, adjoint, coef
 
 

time: 75.7 us -> 49.2 us (0.65)
  Pallas kernels: 33.7 us -> 16.8 us
  waiting for transfers between devices: 10.4 us -> 3.76 us
  blocking collectives: 21.8 us -> 18.3 us
  starting transfers between devices: 6.01 us -> 9.33 us
  local copies, waits for them, and re-layouts: 2.7 us -> 0 us
    pallas_call x6, Pallas kernels: 33.7 us -> 16.8 us  [call(): pl.pallas_call(kernel, out_shape=[jax.ShapeDtypeStruct(*o) if i < leave e...]
    ppermute x4 -> x6, waiting for transfers between devices: 10.4 us -> 2.54 us  [swapped(): lax.ppermute(value, axis, pairs)]
    all_to_all x1, blocking collectives: 21.8 us -> 18.3 us  [local(): lax.all_to_all(send, ('bx', 'by'), split_axis=0, concat_axis=0, tiled=True)]
    ppermute x4 -> x6, starting transfers between devices: 6 us -> 9.28 us  [swapped(): lax.ppermute(value, axis, pairs)]
    unnamed x10 -> x0, local copies, waits for them, and re-layouts: 2.7 us -> none
    ppermute x1, waiting for transfers between devices: 0.01 us -> 1.22 us  [local(): zg = lax.ppermute(zp, 'gz', [(0, 1), (1, 0)])]
  transfers between devices with their start and end apart: 5 -> 7, of which waited for: 2 -> 3; matrix products, arithmetic and copies ran while one was open for 0% -> 0% of each run, Pallas kernels for 2% -> 8%
where the time goes in v2:
time: 49.2 us; the launch traced here: 48.9 us
  blocking collectives  18.3 us (37%)
  Pallas kernels  16.8 us (34%)
  starting transfers between devices  9.33 us (19%)
  waiting for transfers between devices  3.76 us (8%)
  between operations  0.7 us (1%)
    all_to_all x1, blocking collectives, local(): lax.all_to_all(send, ('bx', 'by'), split_axis=0, concat_axis=0, tiled=True)  18.3 us
    pallas_call x6, Pallas kernels, call(): pl.pallas_call(kernel, out_shape=[jax.ShapeDtypeStruct(*o) if i < leave e...  16.8 us
    ppermute x6, starting transfers between devices, swapped(): lax.ppermute(value, axis, pairs)  9.28 us
    ppermute x6, waiting for transfers between devices, swapped(): lax.ppermute(value, axis, pairs)  2.54 us
    ppermute x1, waiting for transfers between devices, local(): zg = lax.ppermute(zp, 'gz', [(0, 1), (1, 0)])  1.22 us
  transfers between devices with their start and end apart: 7, of which 3 were waited for; matrix products, arithmetic and copies ran while one was open for 0% of the time, Pallas kernels for 8%

profile of v2, /device:TPU:0, one launch (start us, length us, event | category | flops | bytes accessed | tf_op | source)
XLA Modules:
  0.0 48.9 jit_solution(11884632145910831184)
XLA Ops:
  0.6 2.0 %shard_map.121 = (f32[22,16,128]{2,1,0:T(8,128)S(1)}, f32[22,16,128]{2,1,0:T(8,128)S(1)}, f32[16,24,128]{2,1,0:T(8,128)S(1)}, f32[16,24,128]{2,1,0:T(8,128)S(1)}...) custom-call(s32[8]{0:T(128)} %cells_ref.1, ...), custom_call_target="tpu_custom_call" | custom-call | tf_op jit(solution)/shard_map/pallas_call | solution.py:405
  2.6 3.1 %collective-permute-start = (f32[22,16,128]{2,1,0:T(8,128)S(1)}, f32[22,16,128]{2,1,0:T(8,128)S(1)}, u32[]{:S(2)}, u32[]{:S(2)}) collective-permute-start(f32[22,16,128]{2,1,0:T(8,128)S(1)} %get-tuple-element.30), channel_id=1, source_target_pairs={{0,2},{2,0},{4,6},{6,4},{1,3},{3,1},{5,7},{7,5},{8,10},{10,8},{12,... | collective-permute-start | bytes 540680 | tf_op jit(solution)/shard_map/ppermute | solution.py:423
  5.7 0.7 %collective-permute-start.1 = (f32[22,16,128]{2,1,0:T(8,128)S(1)}, f32[22,16,128]{2,1,0:T(8,128)S(1)}, u32[]{:S(2)}, u32[]{:S(2)}) collective-permute-start(f32[22,16,128]{2,1,0:T(8,128)S(1)} %get-tuple-element.31), channel_id=1, source_target_pairs={{2,4},{4,2},{3,5},{5,3},{10,12},{12,10},{11,13},{13,11},{18,20},{2... | collective-permute-start | bytes 540680 | tf_op jit(solution)/shard_map/ppermute | solution.py:423
  6.4 1.6 %collective-permute-start.2 = (f32[16,24,128]{2,1,0:T(8,128)S(1)}, f32[16,24,128]{2,1,0:T(8,128)S(1)}, u32[]{:S(2)}, u32[]{:S(2)}) collective-permute-start(f32[16,24,128]{2,1,0:T(8,128)S(1)} %get-tuple-element.32), channel_id=1, source_target_pairs={{0,8},{8,0},{16,24},{24,16},{1,9},{9,1},{17,25},{25,17},{2,10},{10... | collective-permute-start | bytes 589832 | tf_op jit(solution)/shard_map/ppermute | solution.py:423
  7.9 0.7 %collective-permute-start.3 = (f32[16,24,128]{2,1,0:T(8,128)S(1)}, f32[16,24,128]{2,1,0:T(8,128)S(1)}, u32[]{:S(2)}, u32[]{:S(2)}) collective-permute-start(f32[16,24,128]{2,1,0:T(8,128)S(1)} %get-tuple-element.33), channel_id=1, source_target_pairs={{8,16},{16,8},{9,17},{17,9},{10,18},{18,10},{11,19},{19,11},{12,20... | collective-permute-start | bytes 589832 | tf_op jit(solution)/shard_map/ppermute | solution.py:423
  8.6 1.7 %collective-permute-done.ga_ref = f32[22,16,128]{2,1,0:T(8,128)S(1)} collective-permute-done((f32[22,16,128]{2,1,0:T(8,128)S(1)}, f32[22,16,128]{2,1,0:T(8,128)S(1)}, u32[]{:S(2)}, u32[]{:S(2)}) %collective-permute-start) | collective-permute-done | bytes 180256 | tf_op jit(solution)/shard_map/ppermute | solution.py:423
  10.3 0.0 collective-permute-done.1.gb_ref
  10.3 2.7 %collective-permute-start.4 = (f32[4,24,128]{2,1,0:T(8,128)S(1)}, f32[4,24,128]{2,1,0:T(8,128)S(1)}, u32[]{:S(2)}, u32[]{:S(2)}) collective-permute-start(f32[4,24,128]{2,1,0:T(8,128)S(1)} %get-tuple-element.36), channel_id=1, source_target_pairs={{0,8},{8,0},{16,24},{24,16},{1,9},{9,1},{17,25},{25,17},{2,10},{10... | collective-permute-start | bytes 147464 | tf_op jit(solution)/shard_map/ppermute | solution.py:423
  13.0 0.7 %collective-permute-start.5 = (f32[4,24,128]{2,1,0:T(8,128)S(1)}, f32[4,24,128]{2,1,0:T(8,128)S(1)}, u32[]{:S(2)}, u32[]{:S(2)}) collective-permute-start(f32[4,24,128]{2,1,0:T(8,128)S(1)} %get-tuple-element.37), channel_id=1, source_target_pairs={{8,16},{16,8},{9,17},{17,9},{10,18},{18,10},{11,19},{19,11},{12,20... | collective-permute-start | bytes 147464 | tf_op jit(solution)/shard_map/ppermute | solution.py:423
  13.6 4.1 %shard_map.123 = (bf16[2,384,256]{2,1,0:T(8,128)(2,1)S(1)}, f32[16,128]{1,0:T(8,128)S(1)}, bf16[16384,256]{1,0:T(8,128)(2,1)S(1)}) custom-call(s32[1,256]{1,0:T(1,128)} %bitcast.4, s32[1,256]{1,0:T(1,128)} %bitcast.5, bf16[16384,256]{1,0:T(8,128)(2,1)} %bitcast.3), custom_call_target="tpu_custom_call" | custom-call | tf_op jit(solution)/shard_map/pallas_call | solution.py:405
  17.7 0.9 %collective-permute-done.4.ca_ref = f32[4,24,128]{2,1,0:T(8,128)S(1)} collective-permute-done((f32[4,24,128]{2,1,0:T(8,128)S(1)}, f32[4,24,128]{2,1,0:T(8,128)S(1)}, u32[]{:S(2)}, u32[]{:S(2)}) %collective-permute-start.4) | collective-permute-done | bytes 49184 | tf_op jit(solution)/shard_map/ppermute | solution.py:423
  18.6 0.0 collective-permute-done.5.cb_ref
  18.6 0.0 collective-permute-done.2.xa_ref
  18.6 0.0 collective-permute-done.3.xb_ref
  18.6 1.6 %shard_map.124 = (f32[13,20,24,128]{3,2,1,0:T(8,128)S(1)}, f32[24,512]{1,0:T(8,128)S(1)}) custom-call(f32[13,16,16,128]{3,2,1,0:T(8,128)S(1)} %get-tuple-element.29.own_ref, f32[22,16,128]{2,1,0:T(8,128)S(1)} %collective-permute-done.ga_ref, f32[22,16,128]{2,1,0:T(8,128)S(1)} %collective-permute-done.1.gb_ref, ...), custom_call_target="tpu_custom_call" | custom-call | tf_op jit(solution)/shard_map/pallas_call | solution.py:405
  20.3 0.1 collective-permute-start.6
  20.3 1.2 %collective-permute-done.6.zg_ref = f32[24,512]{1,0:T(8,128)S(1)} collective-permute-done((f32[24,512]{1,0:T(8,128)S(1)}, f32[24,512]{1,0:T(8,128)S(1)}, u32[]{:S(2)}, u32[]{:S(2)}) %collective-permute-start.6) | collective-permute-done | bytes 49184 | tf_op jit(solution)/shard_map/ppermute | solution.py:463
  21.5 8.0 %shard_map.125 = (f32[3,16,16,128]{3,2,1,0:T(8,128)}, f32[3,16,16,128]{3,2,1,0:T(8,128)}, f32[16,24,128]{2,1,0:T(8,128)S(1)}) custom-call(f32[13,20,24,128]{3,2,1,0:T(8,128)S(1)} %get-tuple-element.43.ext_ref, f32[24,512]{1,0:T(8,128)S(1)} %get-tuple-element.44.zo_ref, f32[24,512]{1,0:T(8,128)S(1)} %collective-permute-done.6.zg_ref, ...), custom_call_target="tpu_custom_call" | custom-call | tf_op jit(solution)/shard_map/pallas_call | solution.py:405
  29.6 18.3 %all_to_all.5.got_ref = f32[16,24,128]{2,1,0:T(8,128)S(1)} all-to-all(f32[16,24,128]{2,1,0:T(8,128)S(1)} %get-tuple-element.54), channel_id=1, replica_groups=mesh['bx'=4,'by'=4,'gz'=2] {'bx','by'}, dimensions={0} | all-to-all | bytes 393216 | tf_op jit(solution)/shard_map/all_to_all | solution.py:481
  47.8 1.0 %shard_map.126 = f32[64,128]{1,0:T(8,128)} custom-call(f32[16,24,128]{2,1,0:T(8,128)S(1)} %all_to_all.5.got_ref), custom_call_target="tpu_custom_call" | custom-call | tf_op jit(solution)/shard_map/pallas_call | solution.py:405
  (1 shorter events, 0.0 us)
Async XLA Ops:
  2.6 7.6 %collective-permute-start = (f32[22,16,128]{2,1,0:T(8,128)S(1)}, f32[22,16,128]{2,1,0:T(8,128)S(1)}, u32[]{:S(2)}, u32[]{:S(2)}) collective-permute-start(f32[22,16,128]{2,1,0:T(8,128)S(1)} %get-tuple-element.30), channel_id=1, source_target_pairs={{0,2},{2,0},{4,6},{6,4},{1,3},{3,1},{5,7},{7,5},{8,10},{10,8},{12,... | collective-permute-start | bytes 540680 | tf_op jit(solution)/shard_map/ppermute | solution.py:423
  5.7 4.6 %collective-permute-start.1 = (f32[22,16,128]{2,1,0:T(8,128)S(1)}, f32[22,16,128]{2,1,0:T(8,128)S(1)}, u32[]{:S(2)}, u32[]{:S(2)}) collective-permute-start(f32[22,16,128]{2,1,0:T(8,128)S(1)} %get-tuple-element.31), channel_id=1, source_target_pairs={{2,4},{4,2},{3,5},{5,3},{10,12},{12,10},{11,13},{13,11},{18,20},{2... | collective-permute-start | bytes 540680 | tf_op jit(solution)/shard_map/ppermute | solution.py:423
  6.4 12.2 %collective-permute-start.2 = (f32[16,24,128]{2,1,0:T(8,128)S(1)}, f32[16,24,128]{2,1,0:T(8,128)S(1)}, u32[]{:S(2)}, u32[]{:S(2)}) collective-permute-start(f32[16,24,128]{2,1,0:T(8,128)S(1)} %get-tuple-element.32), channel_id=1, source_target_pairs={{0,8},{8,0},{16,24},{24,16},{1,9},{9,1},{17,25},{25,17},{2,10},{10... | collective-permute-start | bytes 589832 | tf_op jit(solution)/shard_map/ppermute | solution.py:423
  7.9 10.7 %collective-permute-start.3 = (f32[16,24,128]{2,1,0:T(8,128)S(1)}, f32[16,24,128]{2,1,0:T(8,128)S(1)}, u32[]{:S(2)}, u32[]{:S(2)}) collective-permute-start(f32[16,24,128]{2,1,0:T(8,128)S(1)} %get-tuple-element.33), channel_id=1, source_target_pairs={{8,16},{16,8},{9,17},{17,9},{10,18},{18,10},{11,19},{19,11},{12,20... | collective-permute-start | bytes 589832 | tf_op jit(solution)/shard_map/ppermute | solution.py:423
  10.3 8.3 %collective-permute-start.4 = (f32[4,24,128]{2,1,0:T(8,128)S(1)}, f32[4,24,128]{2,1,0:T(8,128)S(1)}, u32[]{:S(2)}, u32[]{:S(2)}) collective-permute-start(f32[4,24,128]{2,1,0:T(8,128)S(1)} %get-tuple-element.36), channel_id=1, source_target_pairs={{0,8},{8,0},{16,24},{24,16},{1,9},{9,1},{17,25},{25,17},{2,10},{10... | collective-permute-start | bytes 147464 | tf_op jit(solution)/shard_map/ppermute | solution.py:423
  13.0 5.6 %collective-permute-start.5 = (f32[4,24,128]{2,1,0:T(8,128)S(1)}, f32[4,24,128]{2,1,0:T(8,128)S(1)}, u32[]{:S(2)}, u32[]{:S(2)}) collective-permute-start(f32[4,24,128]{2,1,0:T(8,128)S(1)} %get-tuple-element.37), channel_id=1, source_target_pairs={{8,16},{16,8},{9,17},{17,9},{10,18},{18,10},{11,19},{19,11},{12,20... | collective-permute-start | bytes 147464 | tf_op jit(solution)/shard_map/ppermute | solution.py:423
  20.3 1.3 %collective-permute-start.6 = (f32[24,512]{1,0:T(8,128)S(1)}, f32[24,512]{1,0:T(8,128)S(1)}, u32[]{:S(2)}, u32[]{:S(2)}) collective-permute-start(f32[24,512]{1,0:T(8,128)S(1)} %get-tuple-element.44.zo_ref), channel_id=1, source_target_pairs={{0,1},{1,0},{2,3},{3,2},{4,5},{5,4},{6,7},{7,6},{8,9},{9,8},{10,11... | collective-permute-start | bytes 147464 | tf_op jit(solution)/shard_map/ppermute | solution.py:463

commit v3 on v2

--- a/solution.py
+++ b/solution.py
@@ -18,10 +18,9 @@
 source_level = 3.0
 source_wave = (1.0, -0.6, 0.8, -0.4)
 
-PAIRS, SINGLES = 9, 4
-UNITS = 2 * PAIRS + SINGLES
-UNITS_PAD = 24
-ARRAYS = PAIRS + SINGLES
+PAIRS, ARRAYS = 9, 13
+UNITS = ARRAYS + 4
+Z_UNITS = 24
 F32 = jnp.float32
 BF16 = jnp.bfloat16
 
@@ -67,80 +66,104 @@
 
     lax.fori_loop(0, ny, row, 0, unroll=4)
 
-    def y_face(out, low, near):
-        for i in range(PAIRS):
-            for d in range(2):
-                out[2 * i + d] = own_ref[i, low + d]
-        for i in range(PAIRS, ARRAYS):
-            out[9 + i] = own_ref[i, near]
-
-    def x_face(out, low, near):
-        out[:, UNITS:, :] = jnp.zeros((ny, UNITS_PAD - UNITS, nz), F32)
-        for i in range(PAIRS):
-            out[:, 2 * i:2 * i + 2, :] = own_ref[i, :, low:low + 2, :]
-        for i in range(PAIRS, ARRAYS):
-            out[:, 9 + i:10 + i, :] = own_ref[i, :, near:near + 1, :]
+    def y_face(out, near, deep, up):
+        layers = [[own_ref[i, y] for i in range(ARRAYS)] for y in (near, deep)]
+        for u, unit in enumerate(face_units(*layers, 1, up)):
+            out[u] = unit
+
+    lines = own_ref.reshape(ARRAYS * ny * nx, nz)
+
+    def x_face(out, near, deep, up):
+        layers = [[lines[pl.ds(i * ny * nx + x, ny, stride=nx), :] for i in range(ARRAYS)] for x in (near, deep)]
+        for u, unit in enumerate(face_units(*layers, 0, up)):
+            out[u] = unit
 
     for face, even, a_ref, b_ref, n in ((y_face, is_even("by"), fa_ref, fb_ref, ny), (x_face, is_even("bx"), xa_ref, xb_ref, nx)):
         @pl.when(even)
         def _():
-            face(a_ref, n - 2, n - 1)
-            face(b_ref, 0, 0)
+            face(a_ref, n - 1, n - 2, True)
+            face(b_ref, 0, 1, False)
 
         @pl.when(jnp.logical_not(even))
         def _():
-            face(b_ref, n - 2, n - 1)
-            face(a_ref, 0, 0)
+            face(b_ref, n - 1, n - 2, True)
+            face(a_ref, 0, 1, False)
+
+
+def face_units(near, deep, axis, up):
+    first, second = (axis + 1) % 3, (axis + 2) % 3
+    units = list(near)
+    if up:
+        ratio = jnp.abs(near[12])
+        units[9 + first] = near[9 + first] + ratio * (deep[3 + second] + time_step * deep[first])
+        units[9 + second] = near[9 + second] - ratio * (deep[3 + first] - time_step * deep[second])
+    else:
+        units[3 + first] = near[3 + first] + time_step * deep[second]
+        units[3 + second] = near[3 + second] - time_step * deep[first]
+    return units + [deep[axis], deep[6], deep[7], deep[8]]
+
+
+def sides(axis, even, a, b):
+    at, zero = lax.axis_index(axis), jnp.zeros(a.shape, F32)
+    lower = jnp.where(at == 0, zero, jnp.where(even, b, a))
+    upper = jnp.where(at == lax.axis_size(axis) - 1, zero, jnp.where(even, a, b))
+    return lower, upper
+
+
+def rows_along_y(ga_ref, gb_ref):
+    even, zero = is_even("by"), jnp.zeros(ga_ref.shape[1:], F32)
+    units = [sides("by", even, ga_ref[u], gb_ref[u]) for u in range(UNITS)]
+    lower, upper = ([unit[k] for unit in units] for k in range(2))
+    below = [zero, lower[13], zero] + [zero] * 3 + lower[14:] + [zero] * 4
+    above = [zero] * 6 + upper[14:] + [zero] * 4
+    return below, lower[:ARRAYS], upper[:ARRAYS], above
 
 
 def corner_kernel(ga_ref, gb_ref, ca_ref, cb_ref):
-    nx, nz = ga_ref.shape[1:]
-    y_even, x_even = is_even("by"), is_even("bx")
-
-    def face(out, low, near):
-        out[...] = jnp.zeros(out.shape, F32)
-        for i in range(ARRAYS):
-            u, deep = (2 * i, 2) if i < PAIRS else (9 + i, 1)
-            first = low if deep == 2 else near
-            for d in range(deep):
-                ga, gb = ga_ref[u + d], gb_ref[u + d]
-                out[d if deep == 2 else 1, u:u + deep, :] = jnp.where(y_even, gb, ga)[first:first + deep]
-                out[2 + d, u:u + deep, :] = jnp.where(y_even, ga, gb)[first:first + deep]
-
-    @pl.when(x_even)
+    nx = ga_ref.shape[1]
+    rows = rows_along_y(ga_ref, gb_ref)
+    even = is_even("bx")
+    ca_ref[4 * UNITS:, :] = jnp.zeros((ca_ref.shape[0] - 4 * UNITS, ca_ref.shape[1]), F32)
+    cb_ref[4 * UNITS:, :] = jnp.zeros((cb_ref.shape[0] - 4 * UNITS, cb_ref.shape[1]), F32)
+
+    def face(out, near, deep, up):
+        for k, row in enumerate(rows):
+            for u, unit in enumerate(face_units([a[near:near + 1] for a in row], [a[deep:deep + 1] for a in row], 0, up)):
+                out[4 * u + k:4 * u + k + 1, :] = unit
+
+    @pl.when(even)
     def _():
-        face(ca_ref, nx - 2, nx - 1)
-        face(cb_ref, 0, 0)
-
-    @pl.when(jnp.logical_not(x_even))
+        face(ca_ref, nx - 1, nx - 2, True)
+        face(cb_ref, 0, 1, False)
+
+    @pl.when(jnp.logical_not(even))
     def _():
-        face(cb_ref, nx - 2, nx - 1)
-        face(ca_ref, 0, 0)
+        face(cb_ref, nx - 1, nx - 2, True)
+        face(ca_ref, 0, 1, False)
 
 
 def extend_kernel(own_ref, ga_ref, gb_ref, xa_ref, xb_ref, ca_ref, cb_ref, ext_ref, zp_ref, acc_ref):
     ny, nx, nz = own_ref.shape[1:]
     wy, wx = ny + 4, nx + 8
-    y_even, x_even = is_even("by"), is_even("bx")
+    x_even = is_even("bx")
     gz0 = lax.axis_index("gz") == 0
     ext_ref[:, :, nx:, :] = jnp.zeros((ARRAYS, wy, wx - nx, nz), F32)
-    for i in range(ARRAYS):
-        ext_ref[i, 2:ny + 2, 0:nx, :] = own_ref[i]
-        u, deep = (2 * i, 2) if i < PAIRS else (9 + i, 1)
-        for d in range(2):
-            if deep == 2:
-                ga, gb = ga_ref[u + d], gb_ref[u + d]
-                ext_ref[i, d, 0:nx, :] = jnp.where(y_even, gb, ga)
-                ext_ref[i, ny + 2 + d, 0:nx, :] = jnp.where(y_even, ga, gb)
-            else:
-                ga, gb, zero = ga_ref[u], gb_ref[u], jnp.zeros((nx, nz), F32)
-                ext_ref[i, d, 0:nx, :] = jnp.where(y_even, gb, ga) if d == 1 else zero
-                ext_ref[i, ny + 2 + d, 0:nx, :] = jnp.where(y_even, ga, gb) if d == 0 else zero
-        for a_ref, b_ref, first, last, to in ((xa_ref, xb_ref, 0, ny, 2), (ca_ref, cb_ref, 0, 2, 0), (ca_ref, cb_ref, 2, 4, ny + 2)):
-            a, b = a_ref[first:last, u:u + deep, :], b_ref[first:last, u:u + deep, :]
-            rows = slice(to, to + last - first)
-            ext_ref[i, rows, nx:nx + deep, :] = jnp.where(x_even, a, b)
-            ext_ref[i, rows, wx - deep:, :] = jnp.where(x_even, b, a)
+    ext_ref[:, 2:ny + 2, 0:nx, :] = own_ref[...]
+    for y, row in zip((0, 1, ny + 2, ny + 3), rows_along_y(ga_ref, gb_ref)):
+        for i in range(ARRAYS):
+            ext_ref[i, y, 0:nx, :] = row[i]
+    lines = ext_ref.reshape(ARRAYS * wy * wx, nz)
+    for u in range(UNITS):
+        i, near = (u, True) if u < ARRAYS else ((0, 6, 7, 8)[u - ARRAYS], False)
+        lower, upper = sides("bx", x_even, xa_ref[u], xb_ref[u])
+        low_corner, up_corner = sides("bx", x_even, ca_ref[4 * u:4 * u + 4, :], cb_ref[4 * u:4 * u + 4, :])
+        for x, side, corner in ((wx - 1 if near else wx - 2, lower, low_corner), (nx if near else nx + 1, upper, up_corner)):
+            if u == ARRAYS and side is upper:
+                continue
+            start = i * wy * wx + x
+            lines[pl.ds(start + 2 * wx, ny, stride=wx), :] = side
+            for k, y in enumerate((0, 1, ny + 2, ny + 3)):
+                lines[start + y * wx:start + y * wx + 1, :] = corner[k:k + 1]
 
     lane = lanes((wx, nz))
     back = jnp.where(gz0, 1, 0)
@@ -158,7 +181,7 @@
     lax.fori_loop(0, wy, pack, 0, unroll=4)
     full = acc_ref.shape[0]
     acc_ref[wy * wx:, :] = jnp.zeros((full - wy * wx, nz), F32)
-    zp_ref[...] = acc_ref[...].T[:UNITS_PAD]
+    zp_ref[...] = acc_ref[...].T[:Z_UNITS]
 
 
 def curl_of(dx, dy, dz):
@@ -200,10 +223,15 @@
     return (e, e1, s, s1), (h1, h2, g1, g2)
 
 
-def main_kernel(ext_ref, zo_ref, zg_ref, j1_ref, c_ref, w_ref, q_ref, place_ref, ids_ref, blocks_ref,
-                e2_ref, a0_ref, send_ref,
+def main_kernel(ext_ref, zo_ref, zg_ref, j1_ref, c_ref, w_ref, q_ref, owner_ref, group_ref, basis_ref,
+                e2_ref, a0_ref, send_ref, place_ref, ids_ref, blocks_ref, sem,
                 slab_ref, plane_ref, col_ref, h1_ref, g1_ref, e1_ref, s1_ref, h2_ref, g2_ref,
                 d1_ref, d2_ref, cell_ref):
+    fetch = pltpu.make_async_copy(basis_ref, blocks_ref, sem)
+    fetch.start()
+    planes, width, _ = send_ref.shape
+    rows = rows_of(planes, owner_ref.shape[1])
+    make_places(rows, width, owner_ref, group_ref, place_ref, ids_ref)
     ny, nx, nz = w_ref.shape
     wy, wx = ny + 4, nx + 8
     by0, bx0 = lax.axis_index("by") == 0, lax.axis_index("bx") == 0
@@ -220,75 +248,79 @@
     for p in range(4):
         for c in range(2):
             plane_ref[2 * p + c:2 * p + c + 1, :] = jnp.where(gz0, upper[p][c][2:3], lower[p][c][1:2])
-    col_ref[...] = plane_ref[...].T
+    rest = plane_ref[0:8, :]
+    for k in range(3):
+        part = rest.astype(BF16).astype(F32)
+        plane_ref[8 * k:8 * k + 8, :] = part
+        rest = rest - part
+    wide = 8 * nz
+    row, place = lax.broadcasted_iota(jnp.int32, (128, wide), 0), lanes((128, wide))
+    border = place % nz == jnp.where(gz0, 0, nz - 1)
+    chosen = jnp.where(border & (row % 8 == place // nz) & (row < 24), 1.0, 0.0).astype(BF16)
+    col_ref[...] = lax.dot_general(plane_ref[...].T.astype(BF16), chosen, (((1,), (0,)), ((), ())), preferred_element_type=F32)
 
     lane = lanes((wx, nz))
     column = lax.broadcasted_iota(jnp.int32, (wx, nz), 0)
     x_mask = jnp.where(bx0 & (column >= wx - 2), 0.0, 1.0)
-    up_part, low_part = jnp.where(gz0, 1.0, 0.0), jnp.where(gz0, 0.0, 1.0)
 
     def mask_of(y):
         return x_mask * jnp.where(by0 & (y < 2), 0.0, 1.0)
 
-    def cols_of(y):
-        return col_ref[pl.ds(pl.multiple_of(y * wx, 8), wx), :]
-
-    def plus(ref, y, cols, p):
+    def beyond(y, k):
+        return col_ref[pl.ds(pl.multiple_of(y * wx, 8), wx), k * nz:(k + 1) * nz]
+
+    def plus(ref, y, p):
         f, g = [ref[c, y] for c in range(3)], [ref[c, y + 1] for c in (0, 2)]
         dz = []
         for c in range(2):
-            k = 2 * p + c
-            beyond = (pltpu.roll(cols, nz - k, 1) if k else cols) * up_part
-            dz.append(pltpu.roll(jnp.where(lane == 0, beyond, f[c]), nz - 1, 1) - f[c])
+            dz.append(pltpu.roll(jnp.where(lane == 0, beyond(y, 2 * p + c), f[c]), nz - 1, 1) - f[c])
         dx = [None] + [pltpu.roll(f[c], wx - 1, 0) - f[c] for c in (1, 2)]
         return curl_of(dx, (g[0] - f[0], None, g[1] - f[2]), dz)
 
-    def minus(ref, y, cols, p):
+    def minus(ref, y, p):
         f, g = [ref[c, y] for c in range(3)], [ref[c, y - 1] for c in (0, 2)]
         dz = []
         for c in range(2):
-            k = 2 * p + c
-            beyond = pltpu.roll(cols, nz - 1 - k, 1) * low_part
-            dz.append(f[c] - pltpu.roll(jnp.where(lane == nz - 1, beyond, f[c]), 1, 1))
+            dz.append(f[c] - pltpu.roll(jnp.where(lane == nz - 1, beyond(y, 2 * p + c), f[c]), 1, 1))
         dx = [None] + [f[c] - pltpu.roll(f[c], 1, 0) for c in (1, 2)]
         return curl_of(dx, (f[0] - g[0], None, f[2] - g[1]), dz)
 
     e_ext, h_ext, s_ext, b_ext = (ext_ref.at[3 * k:3 * k + 3] for k in range(4))
 
     def first_magnetic(y, carry):
-        cols, mask = cols_of(y), mask_of(y)
-        for c, d in enumerate(plus(e_ext, y, cols, 0)):
+        mask = mask_of(y)
+        for c, d in enumerate(plus(e_ext, y, 0)):
             h1_ref[c, y] = (h_ext[c, y] - time_step * d) * mask
-        for c, d in enumerate(plus(s_ext, y, cols, 2)):
+        for c, d in enumerate(plus(s_ext, y, 2)):
             g1_ref[c, y] = d * mask
         return carry
 
     def first_electric(y, carry):
-        cols, code = cols_of(y), ext_ref[12, y]
+        code = ext_ref[12, y]
         ratio = jnp.abs(code)
-        for c, d in enumerate(minus(h1_ref, y, cols, 0)):
+        for c, d in enumerate(minus(h1_ref, y, 0)):
             d1_ref[c, y] = d[:nx]
             e1_ref[c, y] = b_ext[c, y] + ratio * d
-        for c, d in enumerate(minus(g1_ref, y, cols, 2)):
+        for c, d in enumerate(minus(g1_ref, y, 2)):
             d2_ref[c, y] = d[:nx]
             s = s_ext[c, y]
             s1_ref[c, y] = jnp.where(code < 0, s * (1.0 - ratio), s) - time_step * ratio * d
         return carry
 
     def second_magnetic(y, carry):
-        cols, mask = cols_of(y), mask_of(y)
-        for c, d in enumerate(plus(e1_ref, y, cols, 1)):
+        mask = mask_of(y)
+        for c, d in enumerate(plus(e1_ref, y, 1)):
             h2_ref[c, y] = (h1_ref[c, y] - time_step * d) * mask
-        for c, d in enumerate(plus(s1_ref, y, cols, 3)):
+        for c, d in enumerate(plus(s1_ref, y, 3)):
             g2_ref[c, y] = (g1_ref[c, y] + d) * mask
         return carry
 
     def second_electric(y, carry):
-        cols, at = cols_of(y), y - 2
+        at = y - 2
         code = ext_ref[12, y, 0:nx, :]
         ratio, silver = jnp.abs(code), code < 0
         eps = jnp.zeros((nx, nz), F32)
-        for c, (d, g) in enumerate(zip(minus(h2_ref, y, cols, 1), minus(g2_ref, y, cols, 3))):
+        for c, (d, g) in enumerate(zip(minus(h2_ref, y, 1), minus(g2_ref, y, 3))):
             e1, s1, s = e1_ref[c, y, 0:nx, :], s1_ref[c, y, 0:nx, :], s_ext[c, y, 0:nx, :]
             j1 = j1_ref[c, at]
             drive = d[:nx] - jnp.where(silver, drude_keep * j1 + drude_gain * e1, 0.0)
@@ -310,6 +342,7 @@
     tiles = ny * nx // 2
     cells = jnp.concatenate([cell_ref[pl.ds(0, tiles, stride=2), :], cell_ref[pl.ds(1, tiles, stride=2), :]], axis=1)
     cells = cells.astype(BF16)
+    fetch.wait()
     tile_rows = blocks_ref.shape[0] // tiles
     group = 32
     at_lane = lanes((tile_rows, tiles))
@@ -330,13 +363,11 @@
     out = jnp.zeros((place_ref.shape[1], 2 * KB), F32)
     for part in (high, low):
         for half in range(2):
-            rows = jnp.concatenate([part, zero] if half == 0 else [zero, part], axis=0)
-            out = out + lax.dot_general(place_ref[half], rows, (((1,), (1,)), ((), ())), preferred_element_type=F32)
-    planes, width, _ = send_ref.shape
+            both = jnp.concatenate([part, zero] if half == 0 else [zero, part], axis=0)
+            out = out + lax.dot_general(place_ref[half], both, (((1,), (1,)), ((), ())), preferred_element_type=F32)
     send_ref[...] = out.reshape(planes, width, 2 * KB)
-    id_row = rows_of(planes, place_ref.shape[2])
     for d in range(planes):
-        send_ref[d, id_row:id_row + 1, :] = ids_ref[d:d + 1, :]
+        send_ref[d, rows:rows + 1, :] = ids_ref[d:d + 1, :]
 
 
 def capacity_of(planes, blocks):
@@ -347,9 +378,7 @@
     return capacity_of(planes, blocks) // 2
 
 
-def place_kernel(rows, width, owner_ref, group_ref, basis_ref, place_ref, ids_ref, blocks_ref, sem):
-    fetch = pltpu.make_async_copy(basis_ref, blocks_ref, sem)
-    fetch.start()
+def make_places(rows, width, owner_ref, group_ref, place_ref, ids_ref):
     blocks = owner_ref.shape[1]
     planes = ids_ref.shape[0]
     row, column = (lax.broadcasted_iota(jnp.int32, (blocks, blocks), k) for k in range(2))
@@ -376,7 +405,6 @@
     ranked = jnp.where(ranks == rank, 1.0, 0.0).astype(BF16)
     named = (hits * (group + 1.0)).astype(BF16)
     ids_ref[...] = lax.dot_general(named, ranked, (((1,), (1,)), ((), ())), preferred_element_type=F32) - 1.0
-    fetch.wait()
 
 
 def collect_kernel(rows, got_ref, coef_ref):
@@ -414,13 +442,21 @@
 
 
 def swapped(first, second, axis):
-    size = lax.axis_size(axis)
+    axes = ("bx", "by", "gz")
+    sizes = [lax.axis_size(name) for name in axes]
+    along = axes.index(axis)
     arrived = []
     for start, value in ((0, first), (1, second)):
         pairs = []
-        for low in range(start, size - 1, 2):
-            pairs += [(low, low + 1), (low + 1, low)]
-        arrived.append(lax.ppermute(value, axis, pairs) if pairs else jnp.zeros_like(value))
+        for flat in range(sizes[0] * sizes[1] * sizes[2]):
+            at = [flat // (sizes[1] * sizes[2]), flat // sizes[2] % sizes[1], flat % sizes[2]]
+            other = at[along] + 1 if at[along] % 2 == start else at[along] - 1
+            if 0 <= other < sizes[along]:
+                at[along] = other
+            else:
+                at[2] = (at[2] + 1) % sizes[2]
+            pairs.append((flat, (at[0] * sizes[1] + at[1]) * sizes[2] + at[2]))
+        arrived.append(lax.ppermute(value, axes, pairs))
     return arrived
 
 
@@ -433,30 +469,21 @@
     planes = lax.axis_size("bx") * lax.axis_size("by")
     rows = rows_of(planes, blocks)
     width = -(-(rows + 1) // 8) * 8
-    y_face, x_face, corner = ((UNITS, nx, nz), F32), ((ny, UNITS_PAD, nz), F32), ((4, UNITS_PAD, nz), F32)
+    y_face, x_face, corner = ((UNITS, nx, nz), F32), ((UNITS, ny, nz), F32), ((-(-4 * UNITS // 8) * 8, nz), F32)
     fa, fb, xa, xb, own, w, j1, q, weight = call(
         prepare_kernel,
         [y_face, y_face, x_face, x_face, ((ARRAYS, ny, nx, nz), F32), scalar, field, scalar, field],
         [source_cell, electric_start, magnetic_start, current_start, cotangent, level_set, material],
         places=[pltpu.SMEM] + [None] * 6, limit=58,
     )
+    xa, xb = swapped(xa, xb, "bx")
     ga, gb = swapped(fa, fb, "by")
-    xa, xb = swapped(xa, xb, "bx")
     ca, cb = call(corner_kernel, [corner, corner], [ga, gb])
-    ca, cb, owner, group = lax.optimization_barrier((ca, cb, block_owner.reshape(1, blocks), block_group.reshape(1, blocks)))
     ca, cb = swapped(ca, cb, "bx")
-    place, ids, basis_here = call(
-        functools.partial(place_kernel, rows, width),
-        [((2, planes * width, blocks), BF16), ((planes, 128), F32), ((blocks * KB, basis.shape[2]), BF16)],
-        [owner, group, basis.reshape(blocks * KB, basis.shape[2])],
-        scratch=[pltpu.SemaphoreType.DMA],
-        places=[None, None, pltpu.HBM], limit=46,
-    )
-    ca, cb, ids = lax.optimization_barrier((ca, cb, ids))
     full = -(-wy * wx // 128) * 128
     ext, zp = call(
         extend_kernel,
-        [((ARRAYS, wy, wx, nz), F32), ((UNITS_PAD, full), F32)],
+        [((ARRAYS, wy, wx, nz), F32), ((Z_UNITS, full), F32)],
         [own, ga, gb, xa, xb, ca, cb],
         scratch=[pltpu.VMEM((full, nz), F32)],
     )
@@ -466,17 +493,22 @@
     electric, adjoint, send = call(
         main_kernel,
         [field, field, ((planes, width, 2 * KB), F32)],
-        [ext, zp, zg, j1, weight, w, q, place, ids, basis_here],
+        [ext, zp, zg, j1, weight, w, q, block_owner.reshape(1, blocks), block_group.reshape(1, blocks),
+         basis.reshape(blocks * KB, basis.shape[2])],
         scratch=[
+            pltpu.VMEM((2, planes * width, blocks), BF16),
+            pltpu.VMEM((planes, 128), F32),
+            pltpu.VMEM((blocks * KB, basis.shape[2]), BF16),
+            pltpu.SemaphoreType.DMA,
             pltpu.VMEM((ARRAYS, 8, full), F32),
             pltpu.VMEM((128, full), F32),
-            pltpu.VMEM((full, 128), F32),
+            pltpu.VMEM((full, 8 * nz), F32),
             wide, wide, wide, wide, wide, wide,
             inner, inner,
             pltpu.VMEM((ny * nx, nz), F32),
         ],
-        leave=2,
-        limit=24,
+        places=[pltpu.VMEM] * 7 + [None, None, pl.ANY],
+        limit=50,
     )
     got = lax.all_to_all(send, ("bx", "by"), split_axis=0, concat_axis=0, tiled=True)
     (coef,) = call(functools.partial(collect_kernel, rows), [((KB, GRP_DEV), F32)], [got], leave=1)

time: 49.2 us -> 43.9 us (0.89)
  blocking collectives: 18.3 us -> 0 us
  waiting for transfers between devices: 3.76 us -> 16 us
  Pallas kernels: 16.8 us -> 12.6 us
  starting transfers between devices: 9.33 us -> 12.9 us
  local copies, waits for them, and re-layouts: 0 us -> 1.49 us
    all_to_all x1 -> x0, blocking collectives: 18.3 us -> none  [local(): lax.all_to_all(send, ('bx', 'by'), split_axis=0, concat_axis=0, tiled=True)]
    all_to_all x0 -> x1, waiting for transfers between devices: none -> 8.02 us  [local(): lax.all_to_all(send, ('bx', 'by'), split_axis=0, concat_axis=0, tiled=True)]
    all_to_all x0 -> x1, starting transfers between devices: none -> 6.3 us  [local(): lax.all_to_all(send, ('bx', 'by'), split_axis=0, concat_axis=0, tiled=True)]
    pallas_call x6 -> x5, Pallas kernels: 16.8 us -> 12.6 us  [call(): pl.pallas_call(kernel, out_shape=[jax.ShapeDtypeStruct(*o) if i < leave e...]
    ppermute x6, waiting for transfers between devices: 2.54 us -> 6.73 us  [swapped(): arrived.append(lax.ppermute(value, axes, pairs))]
    ppermute x6, starting transfers between devices: 9.28 us -> 6.53 us  [swapped(): arrived.append(lax.ppermute(value, axes, pairs))]
    unnamed x0 -> x2, local copies, waits for them, and re-layouts: none -> 1.49 us
  transfers between devices with their start and end apart: 7 -> 8, of which waited for: 3 -> 5; matrix products, arithmetic and copies ran while one was open for 0% -> 3% of each run, Pallas kernels for 8% -> 0%
where the time goes in v3:
time: 43.9 us; the launch traced here: 43.6 us
  waiting for transfers between devices  16 us (36%)
  starting transfers between devices  12.9 us (29%)
  Pallas kernels  12.6 us (29%)
  local copies, waits for them, and re-layouts  1.49 us (3%)
  between operations  0.68 us (2%)
    pallas_call x5, Pallas kernels, call(): pl.pallas_call(kernel, out_shape=[jax.ShapeDtypeStruct(*o) if i < leave e...  12.6 us
    all_to_all x1, waiting for transfers between devices, local(): lax.all_to_all(send, ('bx', 'by'), split_axis=0, concat_axis=0, tiled=True)  8.02 us
    ppermute x6, waiting for transfers between devices, swapped(): arrived.append(lax.ppermute(value, axes, pairs))  6.73 us
    ppermute x6, starting transfers between devices, swapped(): arrived.append(lax.ppermute(value, axes, pairs))  6.53 us
    all_to_all x1, starting transfers between devices, local(): lax.all_to_all(send, ('bx', 'by'), split_axis=0, concat_axis=0, tiled=True)  6.3 us
    unnamed x2, local copies, waits for them, and re-layouts  1.49 us
    ppermute x1, waiting for transfers between devices, local(): zg = lax.ppermute(zp, 'gz', [(0, 1), (1, 0)])  1.22 us
  transfers between devices with their start and end apart: 8, of which 5 were waited for; matrix products, arithmetic and copies ran while one was open for 3% of the time, Pallas kernels for 0%

profile of v3, /device:TPU:0, one launch (start us, length us, event | category | flops | bytes accessed | tf_op | source)
XLA Modules:
  0.0 43.6 jit_solution(12913032553683283831)
XLA Ops:
  0.6 1.9 %shard_map.121 = (f32[17,16,128]{2,1,0:T(8,128)S(1)}, f32[17,16,128]{2,1,0:T(8,128)S(1)}, f32[17,16,128]{2,1,0:T(8,128)S(1)}, f32[17,16,128]{2,1,0:T(8,128)S(1)}...) custom-call(s32[8]{0:T(128)} %cells_ref.1, ...), custom_call_target="tpu_custom_call" | custom-call | tf_op jit(solution)/shard_map/pallas_call | solution.py:433
  2.6 3.1 %collective-permute-start = (f32[17,16,128]{2,1,0:T(8,128)S(1)}, f32[17,16,128]{2,1,0:T(8,128)S(1)}, u32[]{:S(2)}, u32[]{:S(2)}) collective-permute-start(f32[17,16,128]{2,1,0:T(8,128)S(1)} %get-tuple-element.20), channel_id=1, source_target_pairs={{0,2},{1,3},{2,0},{3,1},{4,6},{5,7},{6,4},{7,5},{8,10},{9,11},{10,... | collective-permute-start | bytes 417800 | tf_op jit(solution)/shard_map/ppermute | solution.py:459
  5.7 0.0 collective-permute-start.1
  5.7 1.5 %collective-permute-start.2 = (f32[17,16,128]{2,1,0:T(8,128)S(1)}, f32[17,16,128]{2,1,0:T(8,128)S(1)}, u32[]{:S(2)}, u32[]{:S(2)}) collective-permute-start(f32[17,16,128]{2,1,0:T(8,128)S(1)} %get-tuple-element.22), channel_id=1, source_target_pairs={{0,8},{1,9},{2,10},{3,11},{4,12},{5,13},{6,14},{7,15},{8,0},{9,1},... | collective-permute-start | bytes 417800 | tf_op jit(solution)/shard_map/ppermute | solution.py:459
  7.2 0.2 collective-permute-start.3
  7.4 1.9 %collective-permute-done.ga_ref = f32[17,16,128]{2,1,0:T(8,128)S(1)} collective-permute-done((f32[17,16,128]{2,1,0:T(8,128)S(1)}, f32[17,16,128]{2,1,0:T(8,128)S(1)}, u32[]{:S(2)}, u32[]{:S(2)}) %collective-permute-start) | collective-permute-done | bytes 139296 | tf_op jit(solution)/shard_map/ppermute | solution.py:459
  9.3 0.0 collective-permute-done.1.gb_ref
  9.3 0.1 shard_map.122
  9.4 1.7 %collective-permute-start.4 = (f32[72,128]{1,0:T(8,128)S(1)}, f32[72,128]{1,0:T(8,128)S(1)}, u32[]{:S(2)}, u32[]{:S(2)}) collective-permute-start(f32[72,128]{1,0:T(8,128)S(1)} %get-tuple-element.24), channel_id=1, source_target_pairs={{0,8},{1,9},{2,10},{3,11},{4,12},{5,13},{6,14},{7,15},{8,0},{9,1},... | collective-permute-start | bytes 110600 | tf_op jit(solution)/shard_map/ppermute | solution.py:459
  11.1 0.0 collective-permute-start.5
  11.1 1.0 %collective-permute-done.2.xa_ref = f32[17,16,128]{2,1,0:T(8,128)S(1)} collective-permute-done((f32[17,16,128]{2,1,0:T(8,128)S(1)}, f32[17,16,128]{2,1,0:T(8,128)S(1)}, u32[]{:S(2)}, u32[]{:S(2)}) %collective-permute-start.2) | collective-permute-done | bytes 139296 | tf_op jit(solution)/shard_map/ppermute | solution.py:459
  12.1 0.0 collective-permute-done.3.xb_ref
  12.2 3.8 %collective-permute-done.4.ca_ref = f32[72,128]{1,0:T(8,128)S(1)} collective-permute-done((f32[72,128]{1,0:T(8,128)S(1)}, f32[72,128]{1,0:T(8,128)S(1)}, u32[]{:S(2)}, u32[]{:S(2)}) %collective-permute-start.4) | collective-permute-done | bytes 36896 | tf_op jit(solution)/shard_map/ppermute | solution.py:459
  15.9 0.0 collective-permute-done.5.cb_ref
  15.9 1.5 %shard_map.123 = (f32[13,20,24,128]{3,2,1,0:T(8,128)S(1)}, f32[24,512]{1,0:T(8,128)S(1)}) custom-call(f32[13,16,16,128]{3,2,1,0:T(8,128)S(1)} %get-tuple-element.19.own_ref, f32[17,16,128]{2,1,0:T(8,128)S(1)} %collective-permute-done.ga_ref, f32[17,16,128]{2,1,0:T(8,128)S(1)} %collective-permute-done.1.gb_ref, ...), custom_call_target="tpu_custom_call" | custom-call | tf_op jit(solution)/shard_map/pallas_call | solution.py:433
  17.5 0.1 collective-permute-start.6
  17.5 1.2 %collective-permute-done.6.zg_ref = f32[24,512]{1,0:T(8,128)S(1)} collective-permute-done((f32[24,512]{1,0:T(8,128)S(1)}, f32[24,512]{1,0:T(8,128)S(1)}, u32[]{:S(2)}, u32[]{:S(2)}) %collective-permute-start.6) | collective-permute-done | bytes 49184 | tf_op jit(solution)/shard_map/ppermute | solution.py:490
  18.7 8.0 %shard_map.124 = (f32[3,16,16,128]{3,2,1,0:T(8,128)S(1)}, f32[3,16,16,128]{3,2,1,0:T(8,128)S(1)}, f32[16,24,128]{2,1,0:T(8,128)}) custom-call(f32[13,20,24,128]{3,2,1,0:T(8,128)S(1)} %get-tuple-element.26.ext_ref, f32[24,512]{1,0:T(8,128)S(1)} %get-tuple-element.27.zo_ref, f32[24,512]{1,0:T(8,128)S(1)} %collective-permute-done.6.zg_ref, ...), custom_call_target="tpu_custom_call" | custom-call | tf_op jit(solution)/shard_map/pallas_call | solution.py:433
  26.7 6.3 %all-to-all-start = ((f32[16,24,128]{2,1,0:T(8,128)}), f32[16,24,128]{2,1,0:T(8,128)S(1)}, u32[]{:S(2)}, u32[]{:S(2)}) async-start(f32[16,24,128]{2,1,0:T(8,128)} %get-tuple-element.34), calls=%async_computation | async-start | bytes 393216 | tf_op jit(solution)/shard_map/all_to_all | solution.py:513
  33.0 0.7 %copy.13 = f32[3,16,16,128]{3,2,1,0:T(8,128)} copy(f32[3,16,16,128]{3,2,1,0:T(8,128)S(1)} %get-tuple-element.35) | data formatting | bytes 786432
  33.8 0.7 %copy.14 = f32[3,16,16,128]{3,2,1,0:T(8,128)} copy(f32[3,16,16,128]{3,2,1,0:T(8,128)S(1)} %get-tuple-element.36) | data formatting | bytes 786432
  34.5 8.0 %all-to-all-done.got_ref = f32[16,24,128]{2,1,0:T(8,128)S(1)} async-done(((f32[16,24,128]{2,1,0:T(8,128)}), f32[16,24,128]{2,1,0:T(8,128)S(1)}, u32[]{:S(2)}, u32[]{:S(2)}) %all-to-all-start) | async-done | bytes 196640 | tf_op jit(solution)/shard_map/all_to_all | solution.py:513
  42.6 1.0 %shard_map.125 = f32[64,128]{1,0:T(8,128)} custom-call(f32[16,24,128]{2,1,0:T(8,128)S(1)} %all-to-all-done.got_ref), custom_call_target="tpu_custom_call" | custom-call | tf_op jit(solution)/shard_map/pallas_call | solution.py:433
Async XLA Ops:
  2.6 6.8 %collective-permute-start = (f32[17,16,128]{2,1,0:T(8,128)S(1)}, f32[17,16,128]{2,1,0:T(8,128)S(1)}, u32[]{:S(2)}, u32[]{:S(2)}) collective-permute-start(f32[17,16,128]{2,1,0:T(8,128)S(1)} %get-tuple-element.20), channel_id=1, source_target_pairs={{0,2},{1,3},{2,0},{3,1},{4,6},{5,7},{6,4},{7,5},{8,10},{9,11},{10,... | collective-permute-start | bytes 417800 | tf_op jit(solution)/shard_map/ppermute | solution.py:459
  5.7 3.7 %collective-permute-start.1 = (f32[17,16,128]{2,1,0:T(8,128)S(1)}, f32[17,16,128]{2,1,0:T(8,128)S(1)}, u32[]{:S(2)}, u32[]{:S(2)}) collective-permute-start(f32[17,16,128]{2,1,0:T(8,128)S(1)} %get-tuple-element.21), channel_id=1, source_target_pairs={{0,1},{1,0},{2,4},{3,5},{4,2},{5,3},{6,7},{7,6},{8,9},{9,8},{10,12... | collective-permute-start | bytes 417800 | tf_op jit(solution)/shard_map/ppermute | solution.py:459
  5.7 6.5 %collective-permute-start.2 = (f32[17,16,128]{2,1,0:T(8,128)S(1)}, f32[17,16,128]{2,1,0:T(8,128)S(1)}, u32[]{:S(2)}, u32[]{:S(2)}) collective-permute-start(f32[17,16,128]{2,1,0:T(8,128)S(1)} %get-tuple-element.22), channel_id=1, source_target_pairs={{0,8},{1,9},{2,10},{3,11},{4,12},{5,13},{6,14},{7,15},{8,0},{9,1},... | collective-permute-start | bytes 417800 | tf_op jit(solution)/shard_map/ppermute | solution.py:459
  7.2 5.0 %collective-permute-start.3 = (f32[17,16,128]{2,1,0:T(8,128)S(1)}, f32[17,16,128]{2,1,0:T(8,128)S(1)}, u32[]{:S(2)}, u32[]{:S(2)}) collective-permute-start(f32[17,16,128]{2,1,0:T(8,128)S(1)} %get-tuple-element.23), channel_id=1, source_target_pairs={{0,1},{1,0},{2,3},{3,2},{4,5},{5,4},{6,7},{7,6},{8,16},{9,17},{10,... | collective-permute-start | bytes 417800 | tf_op jit(solution)/shard_map/ppermute | solution.py:459
  9.4 6.5 %collective-permute-start.4 = (f32[72,128]{1,0:T(8,128)S(1)}, f32[72,128]{1,0:T(8,128)S(1)}, u32[]{:S(2)}, u32[]{:S(2)}) collective-permute-start(f32[72,128]{1,0:T(8,128)S(1)} %get-tuple-element.24), channel_id=1, source_target_pairs={{0,8},{1,9},{2,10},{3,11},{4,12},{5,13},{6,14},{7,15},{8,0},{9,1},... | collective-permute-start | bytes 110600 | tf_op jit(solution)/shard_map/ppermute | solution.py:459
  11.1 4.8 %collective-permute-start.5 = (f32[72,128]{1,0:T(8,128)S(1)}, f32[72,128]{1,0:T(8,128)S(1)}, u32[]{:S(2)}, u32[]{:S(2)}) collective-permute-start(f32[72,128]{1,0:T(8,128)S(1)} %get-tuple-element.25), channel_id=1, source_target_pairs={{0,1},{1,0},{2,3},{3,2},{4,5},{5,4},{6,7},{7,6},{8,16},{9,17},{10,... | collective-permute-start | bytes 110600 | tf_op jit(solution)/shard_map/ppermute | solution.py:459
  17.5 1.3 %collective-permute-start.6 = (f32[24,512]{1,0:T(8,128)S(1)}, f32[24,512]{1,0:T(8,128)S(1)}, u32[]{:S(2)}, u32[]{:S(2)}) collective-permute-start(f32[24,512]{1,0:T(8,128)S(1)} %get-tuple-element.27.zo_ref), channel_id=1, source_target_pairs={{0,1},{1,0},{2,3},{3,2},{4,5},{5,4},{6,7},{7,6},{8,9},{9,8},{10,11... | collective-permute-start | bytes 147464 | tf_op jit(solution)/shard_map/ppermute | solution.py:490
  26.7 15.8 %all-to-all-start = ((f32[16,24,128]{2,1,0:T(8,128)}), f32[16,24,128]{2,1,0:T(8,128)S(1)}, u32[]{:S(2)}, u32[]{:S(2)}) async-start(f32[16,24,128]{2,1,0:T(8,128)} %get-tuple-element.34), calls=%async_computation | async-start | bytes 393216 | tf_op jit(solution)/shard_map/all_to_all | solution.py:513

commit v4 on v3

--- a/solution.py
+++ b/solution.py
@@ -33,8 +33,10 @@
     return lax.broadcasted_iota(jnp.int32, shape, len(shape) - 1)
 
 
-def prepare_kernel(cells_ref, e_ref, h_ref, j_ref, c_ref, level_ref, mat_ref,
-                   fa_ref, fb_ref, xa_ref, xb_ref, own_ref, w_ref, j1_ref, q_ref, c_out_ref):
+def prepare_kernel(cells_ref, e_ref, h_ref, j_ref, c_ref, level_ref, mat_ref, owner_ref, group_ref,
+                   fa_ref, fb_ref, xa_ref, xb_ref, own_ref, w_ref, j1_ref, q_ref, c_out_ref, owner_out_ref, group_out_ref):
+    owner_out_ref[...] = owner_ref[...]
+    group_out_ref[...] = group_ref[...]
     ny, nx, nz = mat_ref.shape
     flat = lax.broadcasted_iota(jnp.int32, (nx, nz), 0) * nz + lanes((nx, nz))
 
@@ -142,46 +144,56 @@
         face(ca_ref, 0, 1, False)
 
 
-def extend_kernel(own_ref, ga_ref, gb_ref, xa_ref, xb_ref, ca_ref, cb_ref, ext_ref, zp_ref, acc_ref):
-    ny, nx, nz = own_ref.shape[1:]
-    wy, wx = ny + 4, nx + 8
-    x_even = is_even("bx")
-    gz0 = lax.axis_index("gz") == 0
-    ext_ref[:, :, nx:, :] = jnp.zeros((ARRAYS, wy, wx - nx, nz), F32)
-    ext_ref[:, 2:ny + 2, 0:nx, :] = own_ref[...]
+def gather_planes(ref, y, back):
+    shape = ref.shape[2:]
+    lane, acc = lanes(shape), jnp.zeros(shape, F32)
+    for i in range(ARRAYS):
+        if i < PAIRS:
+            acc = jnp.where(lane // 2 == i, pltpu.roll(ref[i, y], 2 * i + 2 * back, 1), acc)
+        else:
+            acc = jnp.where(lane == 9 + i, pltpu.roll(ref[i, y], 9 + i + back, 1), acc)
+    return acc
+
+
+def widen_kernel(rows, width, own_ref, ga_ref, gb_ref, owner_ref, group_ref, body_ref, acc_ref, place_ref, ids_ref):
+    make_places(rows, width, owner_ref, group_ref, place_ref, ids_ref)
+    ny = own_ref.shape[1]
+    body_ref[:, 2:ny + 2] = own_ref[...]
     for y, row in zip((0, 1, ny + 2, ny + 3), rows_along_y(ga_ref, gb_ref)):
         for i in range(ARRAYS):
-            ext_ref[i, y, 0:nx, :] = row[i]
-    lines = ext_ref.reshape(ARRAYS * wy * wx, nz)
+            body_ref[i, y] = row[i]
+    back = jnp.where(lax.axis_index("gz") == 0, 1, 0)
+
+    for y in range(ny + 4):
+        acc_ref[y] = gather_planes(body_ref, y, back)
+
+
+def extend_kernel(acc_ref, xa_ref, xb_ref, ca_ref, cb_ref, side_ref, zp_ref, all_ref):
+    wy, nx, nz = acc_ref.shape
+    ny, ws = wy - 4, side_ref.shape[2]
+    wx = nx + ws
+    x_even = is_even("bx")
+    side_ref[...] = jnp.zeros(side_ref.shape, F32)
+    lines = side_ref.reshape(ARRAYS * wy * ws, nz)
     for u in range(UNITS):
         i, near = (u, True) if u < ARRAYS else ((0, 6, 7, 8)[u - ARRAYS], False)
         lower, upper = sides("bx", x_even, xa_ref[u], xb_ref[u])
         low_corner, up_corner = sides("bx", x_even, ca_ref[4 * u:4 * u + 4, :], cb_ref[4 * u:4 * u + 4, :])
-        for x, side, corner in ((wx - 1 if near else wx - 2, lower, low_corner), (nx if near else nx + 1, upper, up_corner)):
-            if u == ARRAYS and side is upper:
+        for x, rows, corner in ((ws - 1 if near else ws - 2, lower, low_corner), (0 if near else 1, upper, up_corner)):
+            if u == ARRAYS and rows is upper:
                 continue
-            start = i * wy * wx + x
-            lines[pl.ds(start + 2 * wx, ny, stride=wx), :] = side
+            start = i * wy * ws + x
+            lines[pl.ds(start + 2 * ws, ny, stride=ws), :] = rows
             for k, y in enumerate((0, 1, ny + 2, ny + 3)):
-                lines[start + y * wx:start + y * wx + 1, :] = corner[k:k + 1]
-
-    lane = lanes((wx, nz))
-    back = jnp.where(gz0, 1, 0)
-
-    def pack(y, carry):
-        acc = jnp.zeros((wx, nz), F32)
-        for i in range(ARRAYS):
-            if i < PAIRS:
-                acc = jnp.where(lane // 2 == i, pltpu.roll(ext_ref[i, y], 2 * i + 2 * back, 1), acc)
-            else:
-                acc = jnp.where(lane == 9 + i, pltpu.roll(ext_ref[i, y], 9 + i + back, 1), acc)
-        acc_ref[pl.ds(pl.multiple_of(y * wx, 8), wx), :] = acc
-        return carry
-
-    lax.fori_loop(0, wy, pack, 0, unroll=4)
-    full = acc_ref.shape[0]
-    acc_ref[wy * wx:, :] = jnp.zeros((full - wy * wx, nz), F32)
-    zp_ref[...] = acc_ref[...].T[:Z_UNITS]
+                lines[start + y * ws:start + y * ws + 1, :] = corner[k:k + 1]
+    back = jnp.where(lax.axis_index("gz") == 0, 1, 0)
+
+    for y in range(wy):
+        all_ref[y * wx:y * wx + nx, :] = acc_ref[y]
+        all_ref[y * wx + nx:(y + 1) * wx, :] = gather_planes(side_ref, y, back)
+    full = all_ref.shape[0]
+    all_ref[wy * wx:, :] = jnp.zeros((full - wy * wx, nz), F32)
+    zp_ref[...] = all_ref[...].T[:Z_UNITS]
 
 
 def curl_of(dx, dy, dz):
@@ -193,7 +205,7 @@
     lane = lanes((8, full))
     line = (lane * 683) >> 14
     column = lane - line * wx
-    mask = jnp.where((by0 & (line < 2)) | (bx0 & (column >= wx - 2)), 0.0, 1.0)
+    half = jnp.where((by0 & (line < 2)) | (bx0 & (column >= wx - 2)), 0.0, time_step)
 
     def plus(f):
         ahead = lambda a: jnp.where(column == wx - 1, pltpu.roll(a, wx - 1, 1), pltpu.roll(a, full - 1, 1)) - a
@@ -214,26 +226,50 @@
     e, h, s, b = ([slab_ref[3 * k + c] for c in range(3)] for k in range(4))
     code = slab_ref[12]
     ratio = jnp.abs(code)
-    h1 = [(a - time_step * d) * mask for a, d in zip(h, plus(e))]
-    g1 = [d * mask for d in plus(s)]
+    h1 = [a - half * d for a, d in zip(h, plus(e))]
+    g1 = [half * d for d in plus(s)]
     e1 = [a + ratio * d for a, d in zip(b, minus(h1))]
-    s1 = [jnp.where(code < 0, a * (1.0 - ratio), a) - time_step * ratio * d for a, d in zip(s, minus(g1))]
-    h2 = [(a - time_step * d) * mask for a, d in zip(h1, plus(e1))]
-    g2 = [(a + d) * mask for a, d in zip(g1, plus(s1))]
+    s1 = [jnp.where(code < 0, a * (1.0 - ratio), a) - ratio * d for a, d in zip(s, minus(g1))]
+    h2 = [a - half * d for a, d in zip(h1, plus(e1))]
+    g2 = [a + half * d for a, d in zip(g1, plus(s1))]
     return (e, e1, s, s1), (h1, h2, g1, g2)
 
 
-def main_kernel(ext_ref, zo_ref, zg_ref, j1_ref, c_ref, w_ref, q_ref, owner_ref, group_ref, basis_ref,
-                e2_ref, a0_ref, send_ref, place_ref, ids_ref, blocks_ref, sem,
-                slab_ref, plane_ref, col_ref, h1_ref, g1_ref, e1_ref, s1_ref, h2_ref, g2_ref,
-                d1_ref, d2_ref, cell_ref):
-    fetch = pltpu.make_async_copy(basis_ref, blocks_ref, sem)
-    fetch.start()
-    planes, width, _ = send_ref.shape
-    rows = rows_of(planes, owner_ref.shape[1])
-    make_places(rows, width, owner_ref, group_ref, place_ref, ids_ref)
+class Borders:
+    def __init__(self, col_ref, wx, nz):
+        self.col_ref, self.wx, self.nz, self.lane = col_ref, wx, nz, lanes((wx, nz))
+
+    def beyond(self, y, k):
+        return self.col_ref[pl.ds(pl.multiple_of(y * self.wx, 8), self.wx), k * self.nz:(k + 1) * self.nz]
+
+    def plus(self, get, y, p):
+        f, g = [get(c, y) for c in range(3)], [get(c, y + 1) for c in (0, 2)]
+        dz = [pltpu.roll(jnp.where(self.lane == 0, self.beyond(y, 2 * p + c), f[c]), self.nz - 1, 1) - f[c] for c in range(2)]
+        dx = [None] + [pltpu.roll(f[c], self.wx - 1, 0) - f[c] for c in (1, 2)]
+        return curl_of(dx, (g[0] - f[0], None, g[1] - f[2]), dz)
+
+    def minus(self, get, y, p):
+        f, g = [get(c, y) for c in range(3)], [get(c, y - 1) for c in (0, 2)]
+        dz = [f[c] - pltpu.roll(jnp.where(self.lane == self.nz - 1, self.beyond(y, 2 * p + c), f[c]), 1, 1) for c in range(2)]
+        dx = [None] + [f[c] - pltpu.roll(f[c], 1, 0) for c in (1, 2)]
+        return curl_of(dx, (f[0] - g[0], None, f[2] - g[1]), dz)
+
+
+def halves(wx, nz):
+    by0, bx0 = lax.axis_index("by") == 0, lax.axis_index("bx") == 0
+    column = lax.broadcasted_iota(jnp.int32, (wx, nz), 0)
+    along = jnp.where(bx0 & (column >= wx - 2), 0.0, time_step)
+    return lambda y: along * jnp.where(by0 & (y < 2), 0.0, 1.0)
+
+
+def main_kernel(body_ref, side_ref, zo_ref, zg_ref, j1_ref, c_ref, w_ref, q_ref, place_ref, ids_ref, blocks_ref,
+                e2_ref, a0_ref, send_ref,
+                slab_ref, plane_ref, col_ref, h1_ref, e1_ref, h2_ref, g1_ref, s1_ref, g2_ref,
+                d1_ref, back_ref, cell_ref, partial_ref):
+    size = 2 * w_ref.shape[1] * w_ref.shape[2] // blocks_ref.shape[1] * (2 * KB)
     ny, nx, nz = w_ref.shape
-    wy, wx = ny + 4, nx + 8
+    tile_rows = size // nx
+    wy, wx = ny + 4, nx + side_ref.shape[2]
     by0, bx0 = lax.axis_index("by") == 0, lax.axis_index("bx") == 0
     gz0 = lax.axis_index("gz") == 0
 
@@ -259,115 +295,115 @@
     chosen = jnp.where(border & (row % 8 == place // nz) & (row < 24), 1.0, 0.0).astype(BF16)
     col_ref[...] = lax.dot_general(plane_ref[...].T.astype(BF16), chosen, (((1,), (0,)), ((), ())), preferred_element_type=F32)
 
-    lane = lanes((wx, nz))
-    column = lax.broadcasted_iota(jnp.int32, (wx, nz), 0)
-    x_mask = jnp.where(bx0 & (column >= wx - 2), 0.0, 1.0)
-
-    def mask_of(y):
-        return x_mask * jnp.where(by0 & (y < 2), 0.0, 1.0)
-
-    def beyond(y, k):
-        return col_ref[pl.ds(pl.multiple_of(y * wx, 8), wx), k * nz:(k + 1) * nz]
-
-    def plus(ref, y, p):
-        f, g = [ref[c, y] for c in range(3)], [ref[c, y + 1] for c in (0, 2)]
-        dz = []
-        for c in range(2):
-            dz.append(pltpu.roll(jnp.where(lane == 0, beyond(y, 2 * p + c), f[c]), nz - 1, 1) - f[c])
-        dx = [None] + [pltpu.roll(f[c], wx - 1, 0) - f[c] for c in (1, 2)]
-        return curl_of(dx, (g[0] - f[0], None, g[1] - f[2]), dz)
-
-    def minus(ref, y, p):
-        f, g = [ref[c, y] for c in range(3)], [ref[c, y - 1] for c in (0, 2)]
-        dz = []
-        for c in range(2):
-            dz.append(f[c] - pltpu.roll(jnp.where(lane == nz - 1, beyond(y, 2 * p + c), f[c]), 1, 1))
-        dx = [None] + [f[c] - pltpu.roll(f[c], 1, 0) for c in (1, 2)]
-        return curl_of(dx, (f[0] - g[0], None, f[2] - g[1]), dz)
-
-    e_ext, h_ext, s_ext, b_ext = (ext_ref.at[3 * k:3 * k + 3] for k in range(4))
-
-    def first_magnetic(y, carry):
-        mask = mask_of(y)
-        for c, d in enumerate(plus(e_ext, y, 0)):
-            h1_ref[c, y] = (h_ext[c, y] - time_step * d) * mask
-        for c, d in enumerate(plus(s_ext, y, 2)):
-            g1_ref[c, y] = d * mask
-        return carry
-
-    def first_electric(y, carry):
-        code = ext_ref[12, y]
+    borders, half = Borders(col_ref, wx, nz), halves(wx, nz)
+
+    def array(k):
+        return lambda c, y: jnp.concatenate([body_ref[3 * k + c, y], side_ref[3 * k + c, y]], axis=0)
+
+    def row_of(ref):
+        return lambda c, y: ref[c, y]
+
+    electric, magnetic, scaled, start = (array(k) for k in range(4))
+
+    def first_magnetic(y):
+        factor = half(y)
+        for c, d in enumerate(borders.plus(electric, y, 0)):
+            h1_ref[c, y] = magnetic(c, y) - factor * d
+        for c, d in enumerate(borders.plus(scaled, y, 2)):
+            g1_ref[c, y] = factor * d
+
+    def first_electric(y):
+        code = array(4)(0, y)
         ratio = jnp.abs(code)
-        for c, d in enumerate(minus(h1_ref, y, 0)):
+        kept = jnp.where(code < 0, 1.0 - ratio, 1.0)
+        for c, d in enumerate(borders.minus(row_of(h1_ref), y, 0)):
             d1_ref[c, y] = d[:nx]
-            e1_ref[c, y] = b_ext[c, y] + ratio * d
-        for c, d in enumerate(minus(g1_ref, y, 2)):
-            d2_ref[c, y] = d[:nx]
-            s = s_ext[c, y]
-            s1_ref[c, y] = jnp.where(code < 0, s * (1.0 - ratio), s) - time_step * ratio * d
-        return carry
-
-    def second_magnetic(y, carry):
-        mask = mask_of(y)
-        for c, d in enumerate(plus(e1_ref, y, 1)):
-            h2_ref[c, y] = (h1_ref[c, y] - time_step * d) * mask
-        for c, d in enumerate(plus(s1_ref, y, 3)):
-            g2_ref[c, y] = (g1_ref[c, y] + d) * mask
-        return carry
-
-    def second_electric(y, carry):
+            e1_ref[c, y] = start(c, y) + ratio * d
+        for c, d in enumerate(borders.minus(row_of(g1_ref), y, 2)):
+            back_ref[c, y] = d[:nx]
+            s1_ref[c, y] = scaled(c, y) * kept - ratio * d
+
+    def second_magnetic(y):
+        factor = half(y)
+        for c, d in enumerate(borders.plus(row_of(e1_ref), y, 1)):
+            h2_ref[c, y] = h1_ref[c, y] - factor * d
+
+    def second_electric(y):
         at = y - 2
-        code = ext_ref[12, y, 0:nx, :]
+        code = body_ref[12, y]
         ratio, silver = jnp.abs(code), code < 0
         eps = jnp.zeros((nx, nz), F32)
-        for c, (d, g) in enumerate(zip(minus(h2_ref, y, 1), minus(g2_ref, y, 3))):
-            e1, s1, s = e1_ref[c, y, 0:nx, :], s1_ref[c, y, 0:nx, :], s_ext[c, y, 0:nx, :]
-            j1 = j1_ref[c, at]
+        for c, d in enumerate(borders.minus(row_of(h2_ref), y, 1)):
+            e1, j1 = e1_ref[c, y, 0:nx, :], j1_ref[c, at]
             drive = d[:nx] - jnp.where(silver, drude_keep * j1 + drude_gain * e1, 0.0)
             final = e1 + ratio * drive
             if c == 2:
                 final = final + (source_level * source_wave[1]) * q_ref[at]
             e2_ref[c, at] = final
-            eps = eps + s * drive + s1 * (d1_ref[c, y] - j1)
-            back = c_ref[c, at] - time_step * (d2_ref[c, y] + g[:nx])
-            a0_ref[c, at] = back - jnp.where(silver, drude_gain * ((1.0 + drude_keep) * s + s1), 0.0)
+            eps = eps + body_ref[6 + c, y] * drive + s1_ref[c, y, 0:nx, :] * (d1_ref[c, y] - j1)
         cell_ref[pl.ds(pl.multiple_of(at * nx, 8), nx), :] = w_ref[at] * eps
-        return carry
-
-    lax.fori_loop(0, wy - 1, first_magnetic, 0, unroll=4)
-    lax.fori_loop(1, wy - 1, first_electric, 0, unroll=4)
-    lax.fori_loop(1, wy - 2, second_magnetic, 0, unroll=4)
-    lax.fori_loop(2, wy - 2, second_electric, 0, unroll=4)
-
-    tiles = ny * nx // 2
-    cells = jnp.concatenate([cell_ref[pl.ds(0, tiles, stride=2), :], cell_ref[pl.ds(1, tiles, stride=2), :]], axis=1)
-    cells = cells.astype(BF16)
-    fetch.wait()
-    tile_rows = blocks_ref.shape[0] // tiles
-    group = 32
-    at_lane = lanes((tile_rows, tiles))
-
-    def project(n, acc):
-        start = pl.multiple_of(n * (group * tile_rows), group * tile_rows)
-        prods = lax.dot_general(blocks_ref[pl.ds(start, group * tile_rows), :], cells,
-                                (((1,), (1,)), ((), ())), preferred_element_type=F32)
+
+    def last_magnetic(y):
+        factor = half(y)
+        for c, d in enumerate(borders.plus(row_of(s1_ref), y, 3)):
+            g2_ref[c, y] = g1_ref[c, y] + factor * d
+
+    def last_electric(y):
+        silver = body_ref[12, y] < 0
+        for c, d in enumerate(borders.minus(row_of(g2_ref), y, 3)):
+            lost = jnp.where(silver, drude_gain * ((1.0 + drude_keep) * body_ref[6 + c, y] + s1_ref[c, y, 0:nx, :]), 0.0)
+            a0_ref[c, y - 2] = c_ref[c, y - 2] - back_ref[c, y] - d[:nx] - lost
+
+    for y in range(wy - 1):
+        first_magnetic(y)
+    for y in range(1, wy - 1):
+        first_electric(y)
+    for y in range(1, wy - 2):
+        second_magnetic(y)
+
+    group = nx
+    sub = lax.broadcasted_iota(jnp.int32, (group, tile_rows), 0)
+
+    def project(n):
+        parts = [cell_ref[pl.ds(n * 2 * group + k, group, stride=2), :] for k in range(2)]
+        cells = jnp.concatenate(parts, axis=1).astype(BF16)
+        prods = lax.dot_general(cells, blocks_ref[n * size:(n + 1) * size, :], (((1,), (1,)), ((), ())), preferred_element_type=F32)
+        acc = jnp.zeros((group, tile_rows), F32)
         for i in range(group):
-            acc = jnp.where(at_lane == n * group + i, prods[i * tile_rows:(i + 1) * tile_rows], acc)
-        return acc
-
-    acc = lax.fori_loop(0, tiles // group, project, jnp.zeros((tile_rows, tiles), F32), unroll=2)
-    partial = jnp.concatenate([acc[:KB], acc[KB:]], axis=1)
-    high = partial.astype(BF16)
-    low = (partial - high.astype(F32)).astype(BF16)
-    zero = jnp.zeros(high.shape, BF16)
-    out = jnp.zeros((place_ref.shape[1], 2 * KB), F32)
-    for part in (high, low):
-        for half in range(2):
-            both = jnp.concatenate([part, zero] if half == 0 else [zero, part], axis=0)
-            out = out + lax.dot_general(place_ref[half], both, (((1,), (1,)), ((), ())), preferred_element_type=F32)
-    send_ref[...] = out.reshape(planes, width, 2 * KB)
+            acc = jnp.where(sub == i, prods[:, i * tile_rows:(i + 1) * tile_rows], acc)
+        partial_ref[n * group:(n + 1) * group, :] = acc
+
+    second_electric(2)
+    second_electric(3)
+    last_magnetic(1)
+    for n in range(1, ny // 2):
+        for y in (2 * n + 2, 2 * n + 3):
+            second_electric(y)
+        for y in (2 * n, 2 * n + 1):
+            last_magnetic(y)
+        for y in (2 * n, 2 * n + 1):
+            last_electric(y)
+        project(n - 1)
+    for y in (ny, ny + 1):
+        last_magnetic(y)
+    for y in (ny, ny + 1):
+        last_electric(y)
+    project(ny // 2 - 1)
+
+    partial = partial_ref[...]
+    turned = pltpu.roll(partial, KB, 1)
+    low_lanes = lanes(partial.shape) < KB
+    low = [jnp.where(low_lanes, a, 0.0) for a in (partial, turned)]
+    high = [jnp.where(low_lanes, 0.0, a) for a in (turned, partial)]
+    rhs = jnp.concatenate(low + high, axis=0)
+    most = rhs.astype(BF16)
+    rhs = jnp.concatenate([most, (rhs - most.astype(F32)).astype(BF16)], axis=0)
+    lhs = jnp.concatenate([place_ref[0], place_ref[1], place_ref[0], place_ref[1]], axis=1)
+    send_ref[...] = lax.dot_general(lhs, rhs, (((1,), (0,)), ((), ())), preferred_element_type=F32)
+    planes = ids_ref.shape[0]
+    width = send_ref.shape[0] // planes
     for d in range(planes):
-        send_ref[d, rows:rows + 1, :] = ids_ref[d:d + 1, :]
+        send_ref[d * width + width - 1:(d + 1) * width, :] = ids_ref[d:d + 1, :]
 
 
 def capacity_of(planes, blocks):
@@ -407,21 +443,28 @@
     ids_ref[...] = lax.dot_general(named, ranked, (((1,), (1,)), ((), ())), preferred_element_type=F32) - 1.0
 
 
-def collect_kernel(rows, got_ref, coef_ref):
-    planes, width, line = got_ref.shape
-    shape = (planes, width, line)
-    ids = jnp.broadcast_to(got_ref[:, rows:rows + 1, :], shape)
-    place = lax.broadcasted_iota(jnp.int32, shape, 1)
-    lane = lanes(shape)
-    values = got_ref[...].reshape(planes * width, line).T
+def collect_kernel(planes, got_ref, coef_ref, ids_ref):
+    total, line = got_ref.shape
+    width = total // planes
+    rows = width - 1
+    ids_ref[...] = jnp.zeros(ids_ref.shape, F32)
+    for d in range(planes):
+        ids_ref[d:d + 1, :] = got_ref[d * width + rows:(d + 1) * width, :] + 1.0
+    shape = (total, line)
+    index = lax.broadcasted_iota(jnp.int32, shape, 0)
+    source = jnp.zeros(shape, jnp.int32)
+    for d in range(1, planes):
+        source = source + jnp.where(index >= d * width, 1, 0)
+    place, lane = index - source * width, lanes(shape)
+    spread = jnp.where(source == lane, 1.0, 0.0).astype(BF16)
+    ids = lax.dot_general(spread, ids_ref[...].astype(BF16), (((1,), (0,)), ((), ())), preferred_element_type=F32)
+    values = got_ref[...].T
     high = values.astype(BF16)
     low = (values - high.astype(F32)).astype(BF16)
     parts = []
     for k in range(2):
-        mine = jnp.sum(jnp.where(lane == place + k * rows, ids + 1.0, 0.0), axis=2, keepdims=True)
-        mine = jnp.where(place < rows, mine, 0.0)
-        hits = jnp.where(mine == lane.astype(F32) + 1.0, 1.0, 0.0).astype(BF16)
-        hits = hits.reshape(planes * width, line)
+        mine = jnp.sum(jnp.where(lane == place + k * rows, ids, 0.0), axis=1, keepdims=True)
+        hits = jnp.where((mine == lane.astype(F32) + 1.0) & (place < rows), 1.0, 0.0).astype(BF16)
         dots = [lax.dot_general(part, hits, (((1,), (0,)), ((), ())), preferred_element_type=F32) for part in (high, low)]
         parts.append((dots[0] + dots[1])[k * KB:(k + 1) * KB])
     coef_ref[...] = parts[0] + parts[1]
@@ -468,50 +511,64 @@
     blocks = basis.shape[0]
     planes = lax.axis_size("bx") * lax.axis_size("by")
     rows = rows_of(planes, blocks)
-    width = -(-(rows + 1) // 8) * 8
+    width = rows + 1
     y_face, x_face, corner = ((UNITS, nx, nz), F32), ((UNITS, ny, nz), F32), ((-(-4 * UNITS // 8) * 8, nz), F32)
-    fa, fb, xa, xb, own, w, j1, q, weight = call(
+    names = ((1, blocks), jnp.int32)
+    fa, fb, xa, xb, own, w, j1, q, weight, owner, group = call(
         prepare_kernel,
-        [y_face, y_face, x_face, x_face, ((ARRAYS, ny, nx, nz), F32), scalar, field, scalar, field],
-        [source_cell, electric_start, magnetic_start, current_start, cotangent, level_set, material],
-        places=[pltpu.SMEM] + [None] * 6, limit=58,
+        [y_face, y_face, x_face, x_face, ((ARRAYS, ny, nx, nz), F32), scalar, field, scalar, field, names, names],
+        [source_cell, electric_start, magnetic_start, current_start, cotangent, level_set, material,
+         block_owner.reshape(1, blocks), block_group.reshape(1, blocks)],
+        places=[pltpu.SMEM] + [None] * 8,
+        limit=58,
     )
+    ga, gb = swapped(fa, fb, "by")
     xa, xb = swapped(xa, xb, "bx")
-    ga, gb = swapped(fa, fb, "by")
     ca, cb = call(corner_kernel, [corner, corner], [ga, gb])
+    ca, cb, owner, group = lax.optimization_barrier((ca, cb, owner, group))
     ca, cb = swapped(ca, cb, "bx")
+    flat_basis = basis.reshape(blocks * KB, basis.shape[2])
+    chunk = 2 * nx * nz // basis.shape[2] * (2 * KB)
+    body, acc, place, ids = call(
+        functools.partial(widen_kernel, rows, width),
+        [((ARRAYS, wy, nx, nz), F32), ((wy, nx, nz), F32), ((2, planes * width, blocks), BF16), ((planes, 128), F32)],
+        [own, ga, gb, owner, group],
+        cost=pl.CostEstimate(flops=5_000_000_000, transcendentals=0, bytes_accessed=1000),
+    )
+    ca, cb, ids, acc = lax.optimization_barrier((ca, cb, ids, acc))
     full = -(-wy * wx // 128) * 128
-    ext, zp = call(
+    side, zp = call(
         extend_kernel,
-        [((ARRAYS, wy, wx, nz), F32), ((Z_UNITS, full), F32)],
-        [own, ga, gb, xa, xb, ca, cb],
+        [((ARRAYS, wy, wx - nx, nz), F32), ((Z_UNITS, full), F32)],
+        [acc, xa, xb, ca, cb],
         scratch=[pltpu.VMEM((full, nz), F32)],
     )
     zg = lax.ppermute(zp, "gz", [(0, 1), (1, 0)])
-    wide = pltpu.VMEM((3, wy, wx, nz), F32)
-    inner = pltpu.VMEM((3, wy, nx, nz), F32)
+    wide, inner = ((3, wy, wx, nz), F32), ((3, wy, nx, nz), F32)
     electric, adjoint, send = call(
         main_kernel,
-        [field, field, ((planes, width, 2 * KB), F32)],
-        [ext, zp, zg, j1, weight, w, q, block_owner.reshape(1, blocks), block_group.reshape(1, blocks),
-         basis.reshape(blocks * KB, basis.shape[2])],
+        [field, field, ((planes * width, 2 * KB), F32)],
+        [body, side, zp, zg, j1, weight, w, q, place, ids, flat_basis],
         scratch=[
-            pltpu.VMEM((2, planes * width, blocks), BF16),
-            pltpu.VMEM((planes, 128), F32),
-            pltpu.VMEM((blocks * KB, basis.shape[2]), BF16),
-            pltpu.SemaphoreType.DMA,
             pltpu.VMEM((ARRAYS, 8, full), F32),
             pltpu.VMEM((128, full), F32),
             pltpu.VMEM((full, 8 * nz), F32),
-            wide, wide, wide, wide, wide, wide,
-            inner, inner,
+            *[pltpu.VMEM(*wide)] * 6,
+            pltpu.VMEM(*inner), pltpu.VMEM(*inner),
             pltpu.VMEM((ny * nx, nz), F32),
+            pltpu.VMEM((ny * nx // 2, 2 * KB), F32),
         ],
-        places=[pltpu.VMEM] * 7 + [None, None, pl.ANY],
-        limit=50,
+        limit=20,
     )
+    send = send.reshape(planes * width, 1, 2 * KB)
     got = lax.all_to_all(send, ("bx", "by"), split_axis=0, concat_axis=0, tiled=True)
-    (coef,) = call(functools.partial(collect_kernel, rows), [((KB, GRP_DEV), F32)], [got], leave=1)
+    (coef,) = call(
+        functools.partial(collect_kernel, planes),
+        [((KB, GRP_DEV), F32)],
+        [got.reshape(planes * width, 2 * KB)],
+        scratch=[pltpu.VMEM((128, 2 * KB), F32)],
+        leave=1,
+    )
     return electric, adjoint, coef
 
 

time: 43.9 us -> 38.4 us (0.87)
  Pallas kernels: 12.6 us -> 9 us
  waiting for transfers between devices: 16 us -> 14.1 us
    pallas_call x5 -> x6, Pallas kernels: 12.6 us -> 9 us  [call(): pl.pallas_call(kernel, out_shape=[jax.ShapeDtypeStruct(*o) if i < leave e...]
    all_to_all x1, waiting for transfers between devices: 8.02 us -> 6.83 us  [local(): lax.all_to_all(send, ('bx', 'by'), split_axis=0, concat_axis=0, tiled=True)]
    ppermute x6, waiting for transfers between devices: 6.73 us -> 6.06 us  [swapped(): arrived.append(lax.ppermute(value, axes, pairs))]
    unnamed x2 -> x6, local copies, waits for them, and re-layouts: 1.49 us -> 1.5 us
  transfers between devices with their start and end apart: 8 -> 8, of which waited for: 5 -> 4; matrix products, arithmetic and copies ran while one was open for 3% -> 4% of each run, Pallas kernels for 0% -> 2%
where the time goes in v4:
time: 38.4 us; the launch traced here: 38.2 us
  waiting for transfers between devices  14.1 us (37%)
  starting transfers between devices  12.9 us (34%)
  Pallas kernels  9 us (23%)
  local copies, waits for them, and re-layouts  1.5 us (4%)
  between operations  0.69 us (2%)
    pallas_call x6, Pallas kernels, call(): pl.pallas_call(kernel, out_shape=[jax.ShapeDtypeStruct(*o) if i < leave e...  9 us
    all_to_all x1, waiting for transfers between devices, local(): lax.all_to_all(send, ('bx', 'by'), split_axis=0, concat_axis=0, tiled=True)  6.83 us
    ppermute x6, starting transfers between devices, swapped(): arrived.append(lax.ppermute(value, axes, pairs))  6.53 us
    all_to_all x1, starting transfers between devices, local(): lax.all_to_all(send, ('bx', 'by'), split_axis=0, concat_axis=0, tiled=True)  6.3 us
    ppermute x6, waiting for transfers between devices, swapped(): arrived.append(lax.ppermute(value, axes, pairs))  6.06 us
    unnamed x6, local copies, waits for them, and re-layouts  1.5 us
    ppermute x1, waiting for transfers between devices, local(): zg = lax.ppermute(zp, 'gz', [(0, 1), (1, 0)])  1.22 us
  transfers between devices with their start and end apart: 8, of which 4 were waited for; matrix products, arithmetic and copies ran while one was open for 4% of the time, Pallas kernels for 2%

profile of v4, /device:TPU:0, one launch (start us, length us, event | category | flops | bytes accessed | tf_op | source)
XLA Modules:
  0.0 38.2 jit_solution(3598275646925823450)
XLA Ops:
  0.6 2.0 %shard_map.121 = (f32[17,16,128]{2,1,0:T(8,128)S(1)}, f32[17,16,128]{2,1,0:T(8,128)S(1)}, f32[17,16,128]{2,1,0:T(8,128)S(1)}, f32[17,16,128]{2,1,0:T(8,128)S(1)}...) custom-call(s32[8]{0:T(128)} %cells_ref.1, ...), custom_call_target="tpu_custom_call" | custom-call | tf_op jit(solution)/shard_map/pallas_call | solution.py:476
  2.6 3.1 %collective-permute-start = (f32[17,16,128]{2,1,0:T(8,128)S(1)}, f32[17,16,128]{2,1,0:T(8,128)S(1)}, u32[]{:S(2)}, u32[]{:S(2)}) collective-permute-start(f32[17,16,128]{2,1,0:T(8,128)S(1)} %get-tuple-element.34), channel_id=1, source_target_pairs={{0,2},{1,3},{2,0},{3,1},{4,6},{5,7},{6,4},{7,5},{8,10},{9,11},{10,... | collective-permute-start | bytes 417800 | tf_op jit(solution)/shard_map/ppermute | solution.py:502
  5.7 0.0 collective-permute-start.1
  5.7 1.5 %collective-permute-start.4 = (f32[17,16,128]{2,1,0:T(8,128)S(1)}, f32[17,16,128]{2,1,0:T(8,128)S(1)}, u32[]{:S(2)}, u32[]{:S(2)}) collective-permute-start(f32[17,16,128]{2,1,0:T(8,128)S(1)} %get-tuple-element.48), channel_id=1, source_target_pairs={{0,8},{1,9},{2,10},{3,11},{4,12},{5,13},{6,14},{7,15},{8,0},{9,1},... | collective-permute-start | bytes 417800 | tf_op jit(solution)/shard_map/ppermute | solution.py:502
  7.2 0.2 collective-permute-start.5
  7.4 1.9 %collective-permute-done.ga_ref = f32[17,16,128]{2,1,0:T(8,128)S(1)} collective-permute-done((f32[17,16,128]{2,1,0:T(8,128)S(1)}, f32[17,16,128]{2,1,0:T(8,128)S(1)}, u32[]{:S(2)}, u32[]{:S(2)}) %collective-permute-start) | collective-permute-done | bytes 139296 | tf_op jit(solution)/shard_map/ppermute | solution.py:502
  9.4 0.0 collective-permute-done.1.gb_ref
  9.4 0.1 shard_map.122
  9.5 1.7 %collective-permute-start.2 = (f32[72,128]{1,0:T(8,128)S(1)}, f32[72,128]{1,0:T(8,128)S(1)}, u32[]{:S(2)}, u32[]{:S(2)}) collective-permute-start(f32[72,128]{1,0:T(8,128)S(1)} %get-tuple-element.43), channel_id=1, source_target_pairs={{0,8},{1,9},{2,10},{3,11},{4,12},{5,13},{6,14},{7,15},{8,0},{9,1},... | collective-permute-start | bytes 110600 | tf_op jit(solution)/shard_map/ppermute | solution.py:502
  11.2 0.0 collective-permute-start.3
  11.2 0.0 slice-start
  11.2 0.0 slice-start.1
  11.2 0.7 %shard_map.123 = (f32[13,20,16,128]{3,2,1,0:T(8,128)S(1)}, f32[20,16,128]{2,1,0:T(8,128)S(1)}, bf16[2,272,256]{2,1,0:T(8,128)(2,1)S(1)}, f32[16,128]{1,0:T(8,128)S(1)}) custom-call(f32[13,16,16,128]{3,2,1,0:T(8,128)S(1)} %get-tuple-element.33.own_ref, f32[17,16,128]{2,1,0:T(8,128)S(1)} %collective-permute-done.ga_ref, ...), custom_call_target="tpu_custom_call" | custom-call | flops 5000000000 | bytes 1000 | tf_op jit(solution)/shard_map/pallas_call | solution.py:476
  11.9 4.1 %collective-permute-done.2.ca_ref = f32[72,128]{1,0:T(8,128)S(1)} collective-permute-done((f32[72,128]{1,0:T(8,128)S(1)}, f32[72,128]{1,0:T(8,128)S(1)}, u32[]{:S(2)}, u32[]{:S(2)}) %collective-permute-start.2) | collective-permute-done | bytes 36896 | tf_op jit(solution)/shard_map/ppermute | solution.py:502
  16.0 0.0 collective-permute-done.3.cb_ref
  16.0 0.0 collective-permute-done.4.xa_ref
  16.0 0.0 collective-permute-done.5.xb_ref
  16.0 0.5 %shard_map.124 = (f32[13,20,8,128]{3,2,1,0:T(8,128)S(1)}, f32[24,512]{1,0:T(8,128)S(1)}) custom-call(f32[20,16,128]{2,1,0:T(8,128)S(1)} %get-tuple-element.47.acc_ref, f32[17,16,128]{2,1,0:T(8,128)S(1)} %collective-permute-done.4.xa_ref, f32[17,16,128]{2,1,0:T(8,128)S(1)} %collective-permute-done.5.xb_ref, f32[72,128]{1,0:T(8,128)S(1)} %collective-permute-done.2.ca_ref, ...), custom_call_target="tpu_custom_call" | custom-call | tf_op jit(solution)/shard_map/pallas_call | solution.py:476
  16.5 0.1 collective-permute-start.6
  16.6 1.2 %collective-permute-done.6.zg_ref = f32[24,512]{1,0:T(8,128)S(1)} collective-permute-done((f32[24,512]{1,0:T(8,128)S(1)}, f32[24,512]{1,0:T(8,128)S(1)}, u32[]{:S(2)}, u32[]{:S(2)}) %collective-permute-start.6) | collective-permute-done | bytes 49184 | tf_op jit(solution)/shard_map/ppermute | solution.py:546
  17.8 0.0 slice-done
  17.8 0.0 slice-done.1
  17.8 4.6 %shard_map.125 = (f32[3,16,16,128]{3,2,1,0:T(8,128)S(1)}, f32[3,16,16,128]{3,2,1,0:T(8,128)S(1)}, f32[272,128]{1,0:T(8,128)}) custom-call(f32[13,20,16,128]{3,2,1,0:T(8,128)S(1)} %get-tuple-element.42.body_ref, f32[13,20,8,128]{3,2,1,0:T(8,128)S(1)} %get-tuple-element.52.side_ref, f32[24,512]{1,0:T(8,128)S(1)} %get-tuple-element.53.zo_ref, ...), custom_call_target="tpu_custom_call" | custom-call | tf_op jit(solution)/shard_map/pallas_call | solution.py:476
  22.4 6.3 %all-to-all-start = ((f32[272,1,128]{2,1,0:T(1,128)}), f32[272,1,128]{2,1,0:T(1,128)S(1)}, u32[]{:S(2)}, u32[]{:S(2)}) async-start(f32[272,1,128]{2,1,0:T(1,128)} %bitcast.4), calls=%async_computation | async-start | bytes 278528 | tf_op jit(solution)/shard_map/all_to_all | solution.py:564
  28.7 0.7 %copy.14 = f32[3,16,16,128]{3,2,1,0:T(8,128)} copy(f32[3,16,16,128]{3,2,1,0:T(8,128)S(1)} %get-tuple-element.63) | data formatting | bytes 786432
  29.4 0.7 %copy.15 = f32[3,16,16,128]{3,2,1,0:T(8,128)} copy(f32[3,16,16,128]{3,2,1,0:T(8,128)S(1)} %get-tuple-element.64) | data formatting | bytes 786432
  30.2 6.8 %all-to-all-done = f32[272,1,128]{2,1,0:T(1,128)S(1)} async-done(((f32[272,1,128]{2,1,0:T(1,128)}), f32[272,1,128]{2,1,0:T(1,128)S(1)}, u32[]{:S(2)}, u32[]{:S(2)}) %all-to-all-start) | async-done | bytes 139296 | tf_op jit(solution)/shard_map/all_to_all | solution.py:564
  37.0 1.2 %shard_map.126 = f32[64,128]{1,0:T(8,128)} custom-call(f32[272,128]{1,0:T(8,128)S(1)} %bitcast.10), custom_call_target="tpu_custom_call" | custom-call | tf_op jit(solution)/shard_map/pallas_call | solution.py:476
  (1 shorter events, 0.0 us)
Async XLA Ops:
  2.6 6.8 %collective-permute-start = (f32[17,16,128]{2,1,0:T(8,128)S(1)}, f32[17,16,128]{2,1,0:T(8,128)S(1)}, u32[]{:S(2)}, u32[]{:S(2)}) collective-permute-start(f32[17,16,128]{2,1,0:T(8,128)S(1)} %get-tuple-element.34), channel_id=1, source_target_pairs={{0,2},{1,3},{2,0},{3,1},{4,6},{5,7},{6,4},{7,5},{8,10},{9,11},{10,... | collective-permute-start | bytes 417800 | tf_op jit(solution)/shard_map/ppermute | solution.py:502
  5.7 3.7 %collective-permute-start.1 = (f32[17,16,128]{2,1,0:T(8,128)S(1)}, f32[17,16,128]{2,1,0:T(8,128)S(1)}, u32[]{:S(2)}, u32[]{:S(2)}) collective-permute-start(f32[17,16,128]{2,1,0:T(8,128)S(1)} %get-tuple-element.35), channel_id=1, source_target_pairs={{0,1},{1,0},{2,4},{3,5},{4,2},{5,3},{6,7},{7,6},{8,9},{9,8},{10,12... | collective-permute-start | bytes 417800 | tf_op jit(solution)/shard_map/ppermute | solution.py:502
  5.7 10.2 %collective-permute-start.4 = (f32[17,16,128]{2,1,0:T(8,128)S(1)}, f32[17,16,128]{2,1,0:T(8,128)S(1)}, u32[]{:S(2)}, u32[]{:S(2)}) collective-permute-start(f32[17,16,128]{2,1,0:T(8,128)S(1)} %get-tuple-element.48), channel_id=1, source_target_pairs={{0,8},{1,9},{2,10},{3,11},{4,12},{5,13},{6,14},{7,15},{8,0},{9,1},... | collective-permute-start | bytes 417800 | tf_op jit(solution)/shard_map/ppermute | solution.py:502
  7.2 8.8 %collective-permute-start.5 = (f32[17,16,128]{2,1,0:T(8,128)S(1)}, f32[17,16,128]{2,1,0:T(8,128)S(1)}, u32[]{:S(2)}, u32[]{:S(2)}) collective-permute-start(f32[17,16,128]{2,1,0:T(8,128)S(1)} %get-tuple-element.49), channel_id=1, source_target_pairs={{0,1},{1,0},{2,3},{3,2},{4,5},{5,4},{6,7},{7,6},{8,16},{9,17},{10,... | collective-permute-start | bytes 417800 | tf_op jit(solution)/shard_map/ppermute | solution.py:502
  9.5 6.5 %collective-permute-start.2 = (f32[72,128]{1,0:T(8,128)S(1)}, f32[72,128]{1,0:T(8,128)S(1)}, u32[]{:S(2)}, u32[]{:S(2)}) collective-permute-start(f32[72,128]{1,0:T(8,128)S(1)} %get-tuple-element.43), channel_id=1, source_target_pairs={{0,8},{1,9},{2,10},{3,11},{4,12},{5,13},{6,14},{7,15},{8,0},{9,1},... | collective-permute-start | bytes 110600 | tf_op jit(solution)/shard_map/ppermute | solution.py:502
  11.2 4.8 %collective-permute-start.3 = (f32[72,128]{1,0:T(8,128)S(1)}, f32[72,128]{1,0:T(8,128)S(1)}, u32[]{:S(2)}, u32[]{:S(2)}) collective-permute-start(f32[72,128]{1,0:T(8,128)S(1)} %get-tuple-element.44), channel_id=1, source_target_pairs={{0,1},{1,0},{2,3},{3,2},{4,5},{5,4},{6,7},{7,6},{8,16},{9,17},{10,... | collective-permute-start | bytes 110600 | tf_op jit(solution)/shard_map/ppermute | solution.py:502
  11.2 6.6 %slice-start = ((s8[8388608]{0:T(1024)(128)(4,1)}), s8[4194304]{0:T(1024)(128)(4,1)S(1)}, s32[]{:S(2)}) async-start(s8[8388608]{0:T(1024)(128)(4,1)} %bitcast.7), calls=%async_computation.1 | async-start | bytes 8388608
  11.2 6.6 %slice-start.1 = ((s8[8388608]{0:T(1024)(128)(4,1)}), s8[4194304]{0:T(1024)(128)(4,1)S(1)}, s32[]{:S(2)}) async-start(s8[8388608]{0:T(1024)(128)(4,1)} %bitcast.7), calls=%async_computation.2 | async-start | bytes 8388608
  16.5 1.3 %collective-permute-start.6 = (f32[24,512]{1,0:T(8,128)S(1)}, f32[24,512]{1,0:T(8,128)S(1)}, u32[]{:S(2)}, u32[]{:S(2)}) collective-permute-start(f32[24,512]{1,0:T(8,128)S(1)} %get-tuple-element.53.zo_ref), channel_id=1, source_target_pairs={{0,1},{1,0},{2,3},{3,2},{4,5},{5,4},{6,7},{7,6},{8,9},{9,8},{10,11... | collective-permute-start | bytes 147464 | tf_op jit(solution)/shard_map/ppermute | solution.py:546
  22.4 14.6 %all-to-all-start = ((f32[272,1,128]{2,1,0:T(1,128)}), f32[272,1,128]{2,1,0:T(1,128)S(1)}, u32[]{:S(2)}, u32[]{:S(2)}) async-start(f32[272,1,128]{2,1,0:T(1,128)} %bitcast.4), calls=%async_computation | async-start | bytes 278528 | tf_op jit(solution)/shard_map/all_to_all | solution.py:564

commit v5 on v4

--- a/solution.py
+++ b/solution.py
@@ -20,6 +20,8 @@
 
 PAIRS, ARRAYS = 9, 13
 UNITS = ARRAYS + 4
+CORNER = [(0, u) for u in (1, 5, 6, 7, 8, 15)] + [(k, u) for k in (1, 2) for u in range(UNITS)] + [(3, u) for u in (6, 8, 14)]
+CORNER_LINES = -(-len(CORNER) // 8) * 8
 Z_UNITS = 24
 F32 = jnp.float32
 BF16 = jnp.bfloat16
@@ -66,7 +68,7 @@
             c_out_ref[c, y] = weight
         return carry
 
-    lax.fori_loop(0, ny, row, 0, unroll=4)
+    lax.fori_loop(0, ny, row, 0, unroll=8)
 
     def y_face(out, near, deep, up):
         layers = [[own_ref[i, y] for i in range(ARRAYS)] for y in (near, deep)]
@@ -125,13 +127,13 @@
     nx = ga_ref.shape[1]
     rows = rows_along_y(ga_ref, gb_ref)
     even = is_even("bx")
-    ca_ref[4 * UNITS:, :] = jnp.zeros((ca_ref.shape[0] - 4 * UNITS, ca_ref.shape[1]), F32)
-    cb_ref[4 * UNITS:, :] = jnp.zeros((cb_ref.shape[0] - 4 * UNITS, cb_ref.shape[1]), F32)
+    for ref in (ca_ref, cb_ref):
+        ref[len(CORNER):, :] = jnp.zeros((CORNER_LINES - len(CORNER), ref.shape[1]), F32)
 
     def face(out, near, deep, up):
-        for k, row in enumerate(rows):
-            for u, unit in enumerate(face_units([a[near:near + 1] for a in row], [a[deep:deep + 1] for a in row], 0, up)):
-                out[4 * u + k:4 * u + k + 1, :] = unit
+        units = [face_units([a[near:near + 1] for a in row], [a[deep:deep + 1] for a in row], 0, up) for row in rows]
+        for line, (k, u) in enumerate(CORNER):
+            out[line:line + 1, :] = units[k][u]
 
     @pl.when(even)
     def _():
@@ -175,17 +177,19 @@
     x_even = is_even("bx")
     side_ref[...] = jnp.zeros(side_ref.shape, F32)
     lines = side_ref.reshape(ARRAYS * wy * ws, nz)
+    low_corner, up_corner = sides("bx", x_even, ca_ref[...], cb_ref[...])
     for u in range(UNITS):
         i, near = (u, True) if u < ARRAYS else ((0, 6, 7, 8)[u - ARRAYS], False)
         lower, upper = sides("bx", x_even, xa_ref[u], xb_ref[u])
-        low_corner, up_corner = sides("bx", x_even, ca_ref[4 * u:4 * u + 4, :], cb_ref[4 * u:4 * u + 4, :])
         for x, rows, corner in ((ws - 1 if near else ws - 2, lower, low_corner), (0 if near else 1, upper, up_corner)):
             if u == ARRAYS and rows is upper:
                 continue
             start = i * wy * ws + x
             lines[pl.ds(start + 2 * ws, ny, stride=ws), :] = rows
-            for k, y in enumerate((0, 1, ny + 2, ny + 3)):
-                lines[start + y * ws:start + y * ws + 1, :] = corner[k:k + 1]
+            for line, (k, unit) in enumerate(CORNER):
+                if unit == u:
+                    at = start + (0, 1, ny + 2, ny + 3)[k] * ws
+                    lines[at:at + 1, :] = corner[line:line + 1]
     back = jnp.where(lax.axis_index("gz") == 0, 1, 0)
 
     for y in range(wy):
@@ -512,7 +516,7 @@
     planes = lax.axis_size("bx") * lax.axis_size("by")
     rows = rows_of(planes, blocks)
     width = rows + 1
-    y_face, x_face, corner = ((UNITS, nx, nz), F32), ((UNITS, ny, nz), F32), ((-(-4 * UNITS // 8) * 8, nz), F32)
+    y_face, x_face, corner = ((UNITS, nx, nz), F32), ((UNITS, ny, nz), F32), ((CORNER_LINES, nz), F32)
     names = ((1, blocks), jnp.int32)
     fa, fb, xa, xb, own, w, j1, q, weight, owner, group = call(
         prepare_kernel,

time: 38.4 us -> 38.2 us (level)
  waiting for transfers between devices: 14.1 us -> 13.7 us
where the time goes in v5:
time: 38.2 us; the launch traced here: 38 us
  waiting for transfers between devices  13.7 us (36%)
  starting transfers between devices  13.1 us (34%)
  Pallas kernels  8.92 us (23%)
  local copies, waits for them, and re-layouts  1.5 us (4%)
  between operations  0.69 us (2%)
    pallas_call x6, Pallas kernels, call(): pl.pallas_call(kernel, out_shape=[jax.ShapeDtypeStruct(*o) if i < leave e...  8.92 us
    all_to_all x1, waiting for transfers between devices, local(): lax.all_to_all(send, ('bx', 'by'), split_axis=0, concat_axis=0, tiled=True)  6.83 us
    all_to_all x1, starting transfers between devices, local(): lax.all_to_all(send, ('bx', 'by'), split_axis=0, concat_axis=0, tiled=True)  6.54 us
    ppermute x6, starting transfers between devices, swapped(): arrived.append(lax.ppermute(value, axes, pairs))  6.53 us
    ppermute x6, waiting for transfers between devices, swapped(): arrived.append(lax.ppermute(value, axes, pairs))  5.69 us
    unnamed x6, local copies, waits for them, and re-layouts  1.5 us
    ppermute x1, waiting for transfers between devices, local(): zg = lax.ppermute(zp, 'gz', [(0, 1), (1, 0)])  1.22 us
  transfers between devices with their start and end apart: 8, of which 4 were waited for; matrix products, arithmetic and copies ran while one was open for 4% of the time, Pallas kernels for 2%

profile of v5, /device:TPU:0, one launch (start us, length us, event | category | flops | bytes accessed | tf_op | source)
XLA Modules:
  0.0 38.0 jit_solution(8850284961527338895)
XLA Ops:
  0.6 2.0 %shard_map.121 = (f32[17,16,128]{2,1,0:T(8,128)S(1)}, f32[17,16,128]{2,1,0:T(8,128)S(1)}, f32[17,16,128]{2,1,0:T(8,128)S(1)}, f32[17,16,128]{2,1,0:T(8,128)S(1)}...) custom-call(s32[8]{0:T(128)} %cells_ref.1, ...), custom_call_target="tpu_custom_call" | custom-call | tf_op jit(solution)/shard_map/pallas_call | solution.py:480
  2.6 3.1 %collective-permute-start = (f32[17,16,128]{2,1,0:T(8,128)S(1)}, f32[17,16,128]{2,1,0:T(8,128)S(1)}, u32[]{:S(2)}, u32[]{:S(2)}) collective-permute-start(f32[17,16,128]{2,1,0:T(8,128)S(1)} %get-tuple-element.34), channel_id=1, source_target_pairs={{0,2},{1,3},{2,0},{3,1},{4,6},{5,7},{6,4},{7,5},{8,10},{9,11},{10,... | collective-permute-start | bytes 417800 | tf_op jit(solution)/shard_map/ppermute | solution.py:506
  5.7 0.0 collective-permute-start.1
  5.7 1.5 %collective-permute-start.4 = (f32[17,16,128]{2,1,0:T(8,128)S(1)}, f32[17,16,128]{2,1,0:T(8,128)S(1)}, u32[]{:S(2)}, u32[]{:S(2)}) collective-permute-start(f32[17,16,128]{2,1,0:T(8,128)S(1)} %get-tuple-element.48), channel_id=1, source_target_pairs={{0,8},{1,9},{2,10},{3,11},{4,12},{5,13},{6,14},{7,15},{8,0},{9,1},... | collective-permute-start | bytes 417800 | tf_op jit(solution)/shard_map/ppermute | solution.py:506
  7.2 0.2 collective-permute-start.5
  7.4 1.9 %collective-permute-done.ga_ref = f32[17,16,128]{2,1,0:T(8,128)S(1)} collective-permute-done((f32[17,16,128]{2,1,0:T(8,128)S(1)}, f32[17,16,128]{2,1,0:T(8,128)S(1)}, u32[]{:S(2)}, u32[]{:S(2)}) %collective-permute-start) | collective-permute-done | bytes 139296 | tf_op jit(solution)/shard_map/ppermute | solution.py:506
  9.4 0.0 collective-permute-done.1.gb_ref
  9.4 0.1 shard_map.122
  9.4 1.7 %collective-permute-start.2 = (f32[48,128]{1,0:T(8,128)S(1)}, f32[48,128]{1,0:T(8,128)S(1)}, u32[]{:S(2)}, u32[]{:S(2)}) collective-permute-start(f32[48,128]{1,0:T(8,128)S(1)} %get-tuple-element.43), channel_id=1, source_target_pairs={{0,8},{1,9},{2,10},{3,11},{4,12},{5,13},{6,14},{7,15},{8,0},{9,1},... | collective-permute-start | bytes 73736 | tf_op jit(solution)/shard_map/ppermute | solution.py:506
  11.2 0.0 collective-permute-start.3
  11.2 0.0 slice-start
  11.2 0.0 slice-start.1
  11.2 0.7 %shard_map.123 = (f32[13,20,16,128]{3,2,1,0:T(8,128)S(1)}, f32[20,16,128]{2,1,0:T(8,128)S(1)}, bf16[2,272,256]{2,1,0:T(8,128)(2,1)S(1)}, f32[16,128]{1,0:T(8,128)S(1)}) custom-call(f32[13,16,16,128]{3,2,1,0:T(8,128)S(1)} %get-tuple-element.33.own_ref, f32[17,16,128]{2,1,0:T(8,128)S(1)} %collective-permute-done.ga_ref, ...), custom_call_target="tpu_custom_call" | custom-call | flops 5000000000 | bytes 1000 | tf_op jit(solution)/shard_map/pallas_call | solution.py:480
  11.8 3.7 %collective-permute-done.2.ca_ref = f32[48,128]{1,0:T(8,128)S(1)} collective-permute-done((f32[48,128]{1,0:T(8,128)S(1)}, f32[48,128]{1,0:T(8,128)S(1)}, u32[]{:S(2)}, u32[]{:S(2)}) %collective-permute-start.2) | collective-permute-done | bytes 24608 | tf_op jit(solution)/shard_map/ppermute | solution.py:506
  15.6 0.0 collective-permute-done.3.cb_ref
  15.6 0.0 collective-permute-done.4.xa_ref
  15.6 0.0 collective-permute-done.5.xb_ref
  15.6 0.5 %shard_map.124 = (f32[13,20,8,128]{3,2,1,0:T(8,128)S(1)}, f32[24,512]{1,0:T(8,128)S(1)}) custom-call(f32[20,16,128]{2,1,0:T(8,128)S(1)} %get-tuple-element.47.acc_ref, f32[17,16,128]{2,1,0:T(8,128)S(1)} %collective-permute-done.4.xa_ref, f32[17,16,128]{2,1,0:T(8,128)S(1)} %collective-permute-done.5.xb_ref, f32[48,128]{1,0:T(8,128)S(1)} %collective-permute-done.2.ca_ref, ...), custom_call_target="tpu_custom_call" | custom-call | tf_op jit(solution)/shard_map/pallas_call | solution.py:480
  16.0 0.1 collective-permute-start.6
  16.1 1.2 %collective-permute-done.6.zg_ref = f32[24,512]{1,0:T(8,128)S(1)} collective-permute-done((f32[24,512]{1,0:T(8,128)S(1)}, f32[24,512]{1,0:T(8,128)S(1)}, u32[]{:S(2)}, u32[]{:S(2)}) %collective-permute-start.6) | collective-permute-done | bytes 49184 | tf_op jit(solution)/shard_map/ppermute | solution.py:550
  17.3 0.0 slice-done
  17.3 0.0 slice-done.1
  17.3 4.6 %shard_map.125 = (f32[3,16,16,128]{3,2,1,0:T(8,128)S(1)}, f32[3,16,16,128]{3,2,1,0:T(8,128)S(1)}, f32[272,128]{1,0:T(8,128)}) custom-call(f32[13,20,16,128]{3,2,1,0:T(8,128)S(1)} %get-tuple-element.42.body_ref, f32[13,20,8,128]{3,2,1,0:T(8,128)S(1)} %get-tuple-element.52.side_ref, f32[24,512]{1,0:T(8,128)S(1)} %get-tuple-element.53.zo_ref, ...), custom_call_target="tpu_custom_call" | custom-call | tf_op jit(solution)/shard_map/pallas_call | solution.py:480
  21.9 6.5 %all-to-all-start = ((f32[272,1,128]{2,1,0:T(1,128)}), f32[272,1,128]{2,1,0:T(1,128)S(1)}, u32[]{:S(2)}, u32[]{:S(2)}) async-start(f32[272,1,128]{2,1,0:T(1,128)} %bitcast.4), calls=%async_computation | async-start | bytes 278528 | tf_op jit(solution)/shard_map/all_to_all | solution.py:568
  28.5 0.7 %copy.14 = f32[3,16,16,128]{3,2,1,0:T(8,128)} copy(f32[3,16,16,128]{3,2,1,0:T(8,128)S(1)} %get-tuple-element.63) | data formatting | bytes 786432
  29.2 0.7 %copy.15 = f32[3,16,16,128]{3,2,1,0:T(8,128)} copy(f32[3,16,16,128]{3,2,1,0:T(8,128)S(1)} %get-tuple-element.64) | data formatting | bytes 786432
  30.0 6.8 %all-to-all-done = f32[272,1,128]{2,1,0:T(1,128)S(1)} async-done(((f32[272,1,128]{2,1,0:T(1,128)}), f32[272,1,128]{2,1,0:T(1,128)S(1)}, u32[]{:S(2)}, u32[]{:S(2)}) %all-to-all-start) | async-done | bytes 139296 | tf_op jit(solution)/shard_map/all_to_all | solution.py:568
  36.8 1.2 %shard_map.126 = f32[64,128]{1,0:T(8,128)} custom-call(f32[272,128]{1,0:T(8,128)S(1)} %bitcast.10), custom_call_target="tpu_custom_call" | custom-call | tf_op jit(solution)/shard_map/pallas_call | solution.py:480
  (1 shorter events, 0.0 us)
Async XLA Ops:
  2.6 6.8 %collective-permute-start = (f32[17,16,128]{2,1,0:T(8,128)S(1)}, f32[17,16,128]{2,1,0:T(8,128)S(1)}, u32[]{:S(2)}, u32[]{:S(2)}) collective-permute-start(f32[17,16,128]{2,1,0:T(8,128)S(1)} %get-tuple-element.34), channel_id=1, source_target_pairs={{0,2},{1,3},{2,0},{3,1},{4,6},{5,7},{6,4},{7,5},{8,10},{9,11},{10,... | collective-permute-start | bytes 417800 | tf_op jit(solution)/shard_map/ppermute | solution.py:506
  5.7 3.7 %collective-permute-start.1 = (f32[17,16,128]{2,1,0:T(8,128)S(1)}, f32[17,16,128]{2,1,0:T(8,128)S(1)}, u32[]{:S(2)}, u32[]{:S(2)}) collective-permute-start(f32[17,16,128]{2,1,0:T(8,128)S(1)} %get-tuple-element.35), channel_id=1, source_target_pairs={{0,1},{1,0},{2,4},{3,5},{4,2},{5,3},{6,7},{7,6},{8,9},{9,8},{10,12... | collective-permute-start | bytes 417800 | tf_op jit(solution)/shard_map/ppermute | solution.py:506
  5.7 9.9 %collective-permute-start.4 = (f32[17,16,128]{2,1,0:T(8,128)S(1)}, f32[17,16,128]{2,1,0:T(8,128)S(1)}, u32[]{:S(2)}, u32[]{:S(2)}) collective-permute-start(f32[17,16,128]{2,1,0:T(8,128)S(1)} %get-tuple-element.48), channel_id=1, source_target_pairs={{0,8},{1,9},{2,10},{3,11},{4,12},{5,13},{6,14},{7,15},{8,0},{9,1},... | collective-permute-start | bytes 417800 | tf_op jit(solution)/shard_map/ppermute | solution.py:506
  7.2 8.4 %collective-permute-start.5 = (f32[17,16,128]{2,1,0:T(8,128)S(1)}, f32[17,16,128]{2,1,0:T(8,128)S(1)}, u32[]{:S(2)}, u32[]{:S(2)}) collective-permute-start(f32[17,16,128]{2,1,0:T(8,128)S(1)} %get-tuple-element.49), channel_id=1, source_target_pairs={{0,1},{1,0},{2,3},{3,2},{4,5},{5,4},{6,7},{7,6},{8,16},{9,17},{10,... | collective-permute-start | bytes 417800 | tf_op jit(solution)/shard_map/ppermute | solution.py:506
  9.4 6.1 %collective-permute-start.2 = (f32[48,128]{1,0:T(8,128)S(1)}, f32[48,128]{1,0:T(8,128)S(1)}, u32[]{:S(2)}, u32[]{:S(2)}) collective-permute-start(f32[48,128]{1,0:T(8,128)S(1)} %get-tuple-element.43), channel_id=1, source_target_pairs={{0,8},{1,9},{2,10},{3,11},{4,12},{5,13},{6,14},{7,15},{8,0},{9,1},... | collective-permute-start | bytes 73736 | tf_op jit(solution)/shard_map/ppermute | solution.py:506
  11.2 4.4 %collective-permute-start.3 = (f32[48,128]{1,0:T(8,128)S(1)}, f32[48,128]{1,0:T(8,128)S(1)}, u32[]{:S(2)}, u32[]{:S(2)}) collective-permute-start(f32[48,128]{1,0:T(8,128)S(1)} %get-tuple-element.44), channel_id=1, source_target_pairs={{0,1},{1,0},{2,3},{3,2},{4,5},{5,4},{6,7},{7,6},{8,16},{9,17},{10,... | collective-permute-start | bytes 73736 | tf_op jit(solution)/shard_map/ppermute | solution.py:506
  11.2 6.2 %slice-start = ((s8[8388608]{0:T(1024)(128)(4,1)}), s8[4194304]{0:T(1024)(128)(4,1)S(1)}, s32[]{:S(2)}) async-start(s8[8388608]{0:T(1024)(128)(4,1)} %bitcast.7), calls=%async_computation.1 | async-start | bytes 8388608
  11.2 6.2 %slice-start.1 = ((s8[8388608]{0:T(1024)(128)(4,1)}), s8[4194304]{0:T(1024)(128)(4,1)S(1)}, s32[]{:S(2)}) async-start(s8[8388608]{0:T(1024)(128)(4,1)} %bitcast.7), calls=%async_computation.2 | async-start | bytes 8388608
  16.0 1.3 %collective-permute-start.6 = (f32[24,512]{1,0:T(8,128)S(1)}, f32[24,512]{1,0:T(8,128)S(1)}, u32[]{:S(2)}, u32[]{:S(2)}) collective-permute-start(f32[24,512]{1,0:T(8,128)S(1)} %get-tuple-element.53.zo_ref), channel_id=1, source_target_pairs={{0,1},{1,0},{2,3},{3,2},{4,5},{5,4},{6,7},{7,6},{8,9},{9,8},{10,11... | collective-permute-start | bytes 147464 | tf_op jit(solution)/shard_map/ppermute | solution.py:550
  21.9 14.9 %all-to-all-start = ((f32[272,1,128]{2,1,0:T(1,128)}), f32[272,1,128]{2,1,0:T(1,128)S(1)}, u32[]{:S(2)}, u32[]{:S(2)}) async-start(f32[272,1,128]{2,1,0:T(1,128)} %bitcast.4), calls=%async_computation | async-start | bytes 278528 | tf_op jit(solution)/shard_map/all_to_all | solution.py:568

commit v6 on v5

--- a/solution.py
+++ b/solution.py
@@ -123,7 +123,7 @@
     return below, lower[:ARRAYS], upper[:ARRAYS], above
 
 
-def corner_kernel(ga_ref, gb_ref, ca_ref, cb_ref):
+def corner_kernel(gb_ref, ga_ref, cb_ref, ca_ref):
     nx = ga_ref.shape[1]
     rows = rows_along_y(ga_ref, gb_ref)
     even = is_even("bx")
@@ -157,7 +157,7 @@
     return acc
 
 
-def widen_kernel(rows, width, own_ref, ga_ref, gb_ref, owner_ref, group_ref, body_ref, acc_ref, place_ref, ids_ref):
+def widen_kernel(rows, width, own_ref, gb_ref, ga_ref, owner_ref, group_ref, body_ref, acc_ref, place_ref, ids_ref):
     make_places(rows, width, owner_ref, group_ref, place_ref, ids_ref)
     ny = own_ref.shape[1]
     body_ref[:, 2:ny + 2] = own_ref[...]
@@ -170,7 +170,7 @@
         acc_ref[y] = gather_planes(body_ref, y, back)
 
 
-def extend_kernel(acc_ref, xa_ref, xb_ref, ca_ref, cb_ref, side_ref, zp_ref, all_ref):
+def extend_kernel(acc_ref, xb_ref, xa_ref, cb_ref, ca_ref, side_ref, zp_ref, all_ref):
     wy, nx, nz = acc_ref.shape
     ny, ws = wy - 4, side_ref.shape[2]
     wx = nx + ws
@@ -488,12 +488,12 @@
     )(*[keep(a, space) for a, space in zip(ins, spaces)])
 
 
-def swapped(first, second, axis):
+def swapped(first, second, axis, starts=(0, 1)):
     axes = ("bx", "by", "gz")
     sizes = [lax.axis_size(name) for name in axes]
     along = axes.index(axis)
     arrived = []
-    for start, value in ((0, first), (1, second)):
+    for start, value in zip(starts, (first, second)):
         pairs = []
         for flat in range(sizes[0] * sizes[1] * sizes[2]):
             at = [flat // (sizes[1] * sizes[2]), flat // sizes[2] % sizes[1], flat % sizes[2]]
@@ -526,25 +526,25 @@
         places=[pltpu.SMEM] + [None] * 8,
         limit=58,
     )
-    ga, gb = swapped(fa, fb, "by")
-    xa, xb = swapped(xa, xb, "bx")
-    ca, cb = call(corner_kernel, [corner, corner], [ga, gb])
-    ca, cb, owner, group = lax.optimization_barrier((ca, cb, owner, group))
-    ca, cb = swapped(ca, cb, "bx")
+    gb, ga = swapped(fb, fa, "by", (1, 0))
+    xb, xa = swapped(xb, xa, "bx", (1, 0))
+    cb, ca = call(corner_kernel, [corner, corner], [gb, ga])
+    cb, ca, owner, group = lax.optimization_barrier((cb, ca, owner, group))
+    cb, ca = swapped(cb, ca, "bx", (1, 0))
     flat_basis = basis.reshape(blocks * KB, basis.shape[2])
     chunk = 2 * nx * nz // basis.shape[2] * (2 * KB)
     body, acc, place, ids = call(
         functools.partial(widen_kernel, rows, width),
         [((ARRAYS, wy, nx, nz), F32), ((wy, nx, nz), F32), ((2, planes * width, blocks), BF16), ((planes, 128), F32)],
-        [own, ga, gb, owner, group],
+        [own, gb, ga, owner, group],
         cost=pl.CostEstimate(flops=5_000_000_000, transcendentals=0, bytes_accessed=1000),
     )
-    ca, cb, ids, acc = lax.optimization_barrier((ca, cb, ids, acc))
+    cb, ca, ids, acc = lax.optimization_barrier((cb, ca, ids, acc))
     full = -(-wy * wx // 128) * 128
     side, zp = call(
         extend_kernel,
         [((ARRAYS, wy, wx - nx, nz), F32), ((Z_UNITS, full), F32)],
-        [acc, xa, xb, ca, cb],
+        [acc, xb, xa, cb, ca],
         scratch=[pltpu.VMEM((full, nz), F32)],
     )
     zg = lax.ppermute(zp, "gz", [(0, 1), (1, 0)])

time: 38.2 us -> 37.7 us (0.987)
  waiting for transfers between devices: 13.7 us -> 11.1 us
  starting transfers between devices: 13.1 us -> 15.2 us
    ppermute x6, starting transfers between devices: 6.53 us -> 10.7 us  [swapped(): arrived.append(lax.ppermute(value, axes, pairs))]
    ppermute x6, waiting for transfers between devices: 5.69 us -> 3.08 us  [swapped(): arrived.append(lax.ppermute(value, axes, pairs))]
    all_to_all x1, starting transfers between devices: 6.54 us -> 4.45 us  [local(): lax.all_to_all(send, ('bx', 'by'), split_axis=0, concat_axis=0, tiled=True)]
where the time goes in v6:
time: 37.7 us; the launch traced here: 37.4 us
  starting transfers between devices  15.2 us (40%)
  waiting for transfers between devices  11.1 us (29%)
  Pallas kernels  8.92 us (24%)
  local copies, waits for them, and re-layouts  1.5 us (4%)
  between operations  0.7 us (2%)
    ppermute x6, starting transfers between devices, swapped(): arrived.append(lax.ppermute(value, axes, pairs))  10.7 us
    pallas_call x6, Pallas kernels, call(): pl.pallas_call(kernel, out_shape=[jax.ShapeDtypeStruct(*o) if i < leave e...  8.92 us
    all_to_all x1, waiting for transfers between devices, local(): lax.all_to_all(send, ('bx', 'by'), split_axis=0, concat_axis=0, tiled=True)  6.83 us
    all_to_all x1, starting transfers between devices, local(): lax.all_to_all(send, ('bx', 'by'), split_axis=0, concat_axis=0, tiled=True)  4.45 us
    ppermute x6, waiting for transfers between devices, swapped(): arrived.append(lax.ppermute(value, axes, pairs))  3.08 us
    unnamed x6, local copies, waits for them, and re-layouts  1.5 us
    ppermute x1, waiting for transfers between devices, local(): zg = lax.ppermute(zp, 'gz', [(0, 1), (1, 0)])  1.22 us
  transfers between devices with their start and end apart: 8, of which 4 were waited for; matrix products, arithmetic and copies ran while one was open for 4% of the time, Pallas kernels for 2%

profile of v6, /device:TPU:0, one launch (start us, length us, event | category | flops | bytes accessed | tf_op | source)
XLA Modules:
  0.0 37.4 jit_solution(16383364523316666280)
XLA Ops:
  0.6 2.0 %shard_map.121 = (f32[17,16,128]{2,1,0:T(8,128)S(1)}, f32[17,16,128]{2,1,0:T(8,128)S(1)}, f32[17,16,128]{2,1,0:T(8,128)S(1)}, f32[17,16,128]{2,1,0:T(8,128)S(1)}...) custom-call(s32[8]{0:T(128)} %cells_ref.1, ...), custom_call_target="tpu_custom_call" | custom-call | tf_op jit(solution)/shard_map/pallas_call | solution.py:480
  2.6 0.5 %collective-permute-start = (f32[17,16,128]{2,1,0:T(8,128)S(1)}, f32[17,16,128]{2,1,0:T(8,128)S(1)}, u32[]{:S(2)}, u32[]{:S(2)}) collective-permute-start(f32[17,16,128]{2,1,0:T(8,128)S(1)} %get-tuple-element.34), channel_id=1, source_target_pairs={{0,1},{1,0},{2,4},{3,5},{4,2},{5,3},{6,7},{7,6},{8,9},{9,8},{10,12... | collective-permute-start | bytes 417800 | tf_op jit(solution)/shard_map/ppermute | solution.py:506
  3.1 4.1 %collective-permute-start.1 = (f32[17,16,128]{2,1,0:T(8,128)S(1)}, f32[17,16,128]{2,1,0:T(8,128)S(1)}, u32[]{:S(2)}, u32[]{:S(2)}) collective-permute-start(f32[17,16,128]{2,1,0:T(8,128)S(1)} %get-tuple-element.35), channel_id=1, source_target_pairs={{0,2},{1,3},{2,0},{3,1},{4,6},{5,7},{6,4},{7,5},{8,10},{9,11},{10,... | collective-permute-start | bytes 417800 | tf_op jit(solution)/shard_map/ppermute | solution.py:506
  7.3 0.0 collective-permute-start.4
  7.3 3.0 %collective-permute-start.5 = (f32[17,16,128]{2,1,0:T(8,128)S(1)}, f32[17,16,128]{2,1,0:T(8,128)S(1)}, u32[]{:S(2)}, u32[]{:S(2)}) collective-permute-start(f32[17,16,128]{2,1,0:T(8,128)S(1)} %get-tuple-element.49), channel_id=1, source_target_pairs={{0,8},{1,9},{2,10},{3,11},{4,12},{5,13},{6,14},{7,15},{8,0},{9,1},... | collective-permute-start | bytes 417800 | tf_op jit(solution)/shard_map/ppermute | solution.py:506
  10.3 0.0 collective-permute-done.gb_ref
  10.3 0.4 %collective-permute-done.1.ga_ref = f32[17,16,128]{2,1,0:T(8,128)S(1)} collective-permute-done((f32[17,16,128]{2,1,0:T(8,128)S(1)}, f32[17,16,128]{2,1,0:T(8,128)S(1)}, u32[]{:S(2)}, u32[]{:S(2)}) %collective-permute-start.1) | collective-permute-done | bytes 139296 | tf_op jit(solution)/shard_map/ppermute | solution.py:506
  10.7 0.1 shard_map.122
  10.7 0.1 collective-permute-start.2
  10.8 3.0 %collective-permute-start.3 = (f32[48,128]{1,0:T(8,128)S(1)}, f32[48,128]{1,0:T(8,128)S(1)}, u32[]{:S(2)}, u32[]{:S(2)}) collective-permute-start(f32[48,128]{1,0:T(8,128)S(1)} %get-tuple-element.44), channel_id=1, source_target_pairs={{0,8},{1,9},{2,10},{3,11},{4,12},{5,13},{6,14},{7,15},{8,0},{9,1},... | collective-permute-start | bytes 73736 | tf_op jit(solution)/shard_map/ppermute | solution.py:506
  13.8 0.0 slice-start
  13.8 0.0 slice-start.1
  13.8 0.7 %shard_map.123 = (f32[13,20,16,128]{3,2,1,0:T(8,128)S(1)}, f32[20,16,128]{2,1,0:T(8,128)S(1)}, bf16[2,272,256]{2,1,0:T(8,128)(2,1)S(1)}, f32[16,128]{1,0:T(8,128)S(1)}) custom-call(f32[13,16,16,128]{3,2,1,0:T(8,128)S(1)} %get-tuple-element.33.own_ref, f32[17,16,128]{2,1,0:T(8,128)S(1)} %collective-permute-done.gb_ref, ...), custom_call_target="tpu_custom_call" | custom-call | flops 5000000000 | bytes 1000 | tf_op jit(solution)/shard_map/pallas_call | solution.py:480
  14.4 0.0 collective-permute-done.2.cb_ref
  14.4 2.7 %collective-permute-done.3.ca_ref = f32[48,128]{1,0:T(8,128)S(1)} collective-permute-done((f32[48,128]{1,0:T(8,128)S(1)}, f32[48,128]{1,0:T(8,128)S(1)}, u32[]{:S(2)}, u32[]{:S(2)}) %collective-permute-start.3) | collective-permute-done | bytes 24608 | tf_op jit(solution)/shard_map/ppermute | solution.py:506
  17.1 0.0 collective-permute-done.4.xb_ref
  17.1 0.0 collective-permute-done.5.xa_ref
  17.1 0.5 %shard_map.124 = (f32[13,20,8,128]{3,2,1,0:T(8,128)S(1)}, f32[24,512]{1,0:T(8,128)S(1)}) custom-call(f32[20,16,128]{2,1,0:T(8,128)S(1)} %get-tuple-element.47.acc_ref, f32[17,16,128]{2,1,0:T(8,128)S(1)} %collective-permute-done.4.xb_ref, f32[17,16,128]{2,1,0:T(8,128)S(1)} %collective-permute-done.5.xa_ref, f32[48,128]{1,0:T(8,128)S(1)} %collective-permute-done.2.cb_ref, ...), custom_call_target="tpu_custom_call" | custom-call | tf_op jit(solution)/shard_map/pallas_call | solution.py:480
  17.6 0.1 collective-permute-start.6
  17.7 1.2 %collective-permute-done.6.zg_ref = f32[24,512]{1,0:T(8,128)S(1)} collective-permute-done((f32[24,512]{1,0:T(8,128)S(1)}, f32[24,512]{1,0:T(8,128)S(1)}, u32[]{:S(2)}, u32[]{:S(2)}) %collective-permute-start.6) | collective-permute-done | bytes 49184 | tf_op jit(solution)/shard_map/ppermute | solution.py:550
  18.9 0.0 slice-done
  18.9 0.0 slice-done.1
  18.9 4.6 %shard_map.125 = (f32[3,16,16,128]{3,2,1,0:T(8,128)S(1)}, f32[3,16,16,128]{3,2,1,0:T(8,128)S(1)}, f32[272,128]{1,0:T(8,128)}) custom-call(f32[13,20,16,128]{3,2,1,0:T(8,128)S(1)} %get-tuple-element.42.body_ref, f32[13,20,8,128]{3,2,1,0:T(8,128)S(1)} %get-tuple-element.52.side_ref, f32[24,512]{1,0:T(8,128)S(1)} %get-tuple-element.53.zo_ref, ...), custom_call_target="tpu_custom_call" | custom-call | tf_op jit(solution)/shard_map/pallas_call | solution.py:480
  23.5 4.5 %all-to-all-start = ((f32[272,1,128]{2,1,0:T(1,128)}), f32[272,1,128]{2,1,0:T(1,128)S(1)}, u32[]{:S(2)}, u32[]{:S(2)}) async-start(f32[272,1,128]{2,1,0:T(1,128)} %bitcast.4), calls=%async_computation | async-start | bytes 278528 | tf_op jit(solution)/shard_map/all_to_all | solution.py:568
  27.9 0.7 %copy.14 = f32[3,16,16,128]{3,2,1,0:T(8,128)} copy(f32[3,16,16,128]{3,2,1,0:T(8,128)S(1)} %get-tuple-element.63) | data formatting | bytes 786432
  28.7 0.7 %copy.15 = f32[3,16,16,128]{3,2,1,0:T(8,128)} copy(f32[3,16,16,128]{3,2,1,0:T(8,128)S(1)} %get-tuple-element.64) | data formatting | bytes 786432
  29.4 6.8 %all-to-all-done = f32[272,1,128]{2,1,0:T(1,128)S(1)} async-done(((f32[272,1,128]{2,1,0:T(1,128)}), f32[272,1,128]{2,1,0:T(1,128)S(1)}, u32[]{:S(2)}, u32[]{:S(2)}) %all-to-all-start) | async-done | bytes 139296 | tf_op jit(solution)/shard_map/all_to_all | solution.py:568
  36.3 1.2 %shard_map.126 = f32[64,128]{1,0:T(8,128)} custom-call(f32[272,128]{1,0:T(8,128)S(1)} %bitcast.10), custom_call_target="tpu_custom_call" | custom-call | tf_op jit(solution)/shard_map/pallas_call | solution.py:480
  (1 shorter events, 0.0 us)
Async XLA Ops:
  2.6 7.7 %collective-permute-start = (f32[17,16,128]{2,1,0:T(8,128)S(1)}, f32[17,16,128]{2,1,0:T(8,128)S(1)}, u32[]{:S(2)}, u32[]{:S(2)}) collective-permute-start(f32[17,16,128]{2,1,0:T(8,128)S(1)} %get-tuple-element.34), channel_id=1, source_target_pairs={{0,1},{1,0},{2,4},{3,5},{4,2},{5,3},{6,7},{7,6},{8,9},{9,8},{10,12... | collective-permute-start | bytes 417800 | tf_op jit(solution)/shard_map/ppermute | solution.py:506
  3.1 7.5 %collective-permute-start.1 = (f32[17,16,128]{2,1,0:T(8,128)S(1)}, f32[17,16,128]{2,1,0:T(8,128)S(1)}, u32[]{:S(2)}, u32[]{:S(2)}) collective-permute-start(f32[17,16,128]{2,1,0:T(8,128)S(1)} %get-tuple-element.35), channel_id=1, source_target_pairs={{0,2},{1,3},{2,0},{3,1},{4,6},{5,7},{6,4},{7,5},{8,10},{9,11},{10,... | collective-permute-start | bytes 417800 | tf_op jit(solution)/shard_map/ppermute | solution.py:506
  7.3 9.8 %collective-permute-start.4 = (f32[17,16,128]{2,1,0:T(8,128)S(1)}, f32[17,16,128]{2,1,0:T(8,128)S(1)}, u32[]{:S(2)}, u32[]{:S(2)}) collective-permute-start(f32[17,16,128]{2,1,0:T(8,128)S(1)} %get-tuple-element.48), channel_id=1, source_target_pairs={{0,1},{1,0},{2,3},{3,2},{4,5},{5,4},{6,7},{7,6},{8,16},{9,17},{10,... | collective-permute-start | bytes 417800 | tf_op jit(solution)/shard_map/ppermute | solution.py:506
  7.3 9.8 %collective-permute-start.5 = (f32[17,16,128]{2,1,0:T(8,128)S(1)}, f32[17,16,128]{2,1,0:T(8,128)S(1)}, u32[]{:S(2)}, u32[]{:S(2)}) collective-permute-start(f32[17,16,128]{2,1,0:T(8,128)S(1)} %get-tuple-element.49), channel_id=1, source_target_pairs={{0,8},{1,9},{2,10},{3,11},{4,12},{5,13},{6,14},{7,15},{8,0},{9,1},... | collective-permute-start | bytes 417800 | tf_op jit(solution)/shard_map/ppermute | solution.py:506
  10.7 3.7 %collective-permute-start.2 = (f32[48,128]{1,0:T(8,128)S(1)}, f32[48,128]{1,0:T(8,128)S(1)}, u32[]{:S(2)}, u32[]{:S(2)}) collective-permute-start(f32[48,128]{1,0:T(8,128)S(1)} %get-tuple-element.43), channel_id=1, source_target_pairs={{0,1},{1,0},{2,3},{3,2},{4,5},{5,4},{6,7},{7,6},{8,16},{9,17},{10,... | collective-permute-start | bytes 73736 | tf_op jit(solution)/shard_map/ppermute | solution.py:506
  10.8 6.3 %collective-permute-start.3 = (f32[48,128]{1,0:T(8,128)S(1)}, f32[48,128]{1,0:T(8,128)S(1)}, u32[]{:S(2)}, u32[]{:S(2)}) collective-permute-start(f32[48,128]{1,0:T(8,128)S(1)} %get-tuple-element.44), channel_id=1, source_target_pairs={{0,8},{1,9},{2,10},{3,11},{4,12},{5,13},{6,14},{7,15},{8,0},{9,1},... | collective-permute-start | bytes 73736 | tf_op jit(solution)/shard_map/ppermute | solution.py:506
  13.8 5.1 %slice-start = ((s8[8388608]{0:T(1024)(128)(4,1)}), s8[4194304]{0:T(1024)(128)(4,1)S(1)}, s32[]{:S(2)}) async-start(s8[8388608]{0:T(1024)(128)(4,1)} %bitcast.7), calls=%async_computation.1 | async-start | bytes 8388608
  13.8 5.1 %slice-start.1 = ((s8[8388608]{0:T(1024)(128)(4,1)}), s8[4194304]{0:T(1024)(128)(4,1)S(1)}, s32[]{:S(2)}) async-start(s8[8388608]{0:T(1024)(128)(4,1)} %bitcast.7), calls=%async_computation.2 | async-start | bytes 8388608
  17.6 1.3 %collective-permute-start.6 = (f32[24,512]{1,0:T(8,128)S(1)}, f32[24,512]{1,0:T(8,128)S(1)}, u32[]{:S(2)}, u32[]{:S(2)}) collective-permute-start(f32[24,512]{1,0:T(8,128)S(1)} %get-tuple-element.53.zo_ref), channel_id=1, source_target_pairs={{0,1},{1,0},{2,3},{3,2},{4,5},{5,4},{6,7},{7,6},{8,9},{9,8},{10,11... | collective-permute-start | bytes 147464 | tf_op jit(solution)/shard_map/ppermute | solution.py:550
  23.5 12.8 %all-to-all-start = ((f32[272,1,128]{2,1,0:T(1,128)}), f32[272,1,128]{2,1,0:T(1,128)S(1)}, u32[]{:S(2)}, u32[]{:S(2)}) async-start(f32[272,1,128]{2,1,0:T(1,128)} %bitcast.4), calls=%async_computation | async-start | bytes 278528 | tf_op jit(solution)/shard_map/all_to_all | solution.py:568

commit v7 on v6

--- a/solution.py
+++ b/solution.py
@@ -20,7 +20,8 @@
 
 PAIRS, ARRAYS = 9, 13
 UNITS = ARRAYS + 4
-CORNER = [(0, u) for u in (1, 5, 6, 7, 8, 15)] + [(k, u) for k in (1, 2) for u in range(UNITS)] + [(3, u) for u in (6, 8, 14)]
+CORNER = [(0, u) for u in (1, 7)] + [(1, u) for u in (0, 1, 2, 3, 4, 5, 6, 7, 8, 10, 12, 15)]
+CORNER += [(2, u) for u in (0, 1, 2, 4, 5, 6, 7, 8, 9, 12, 13, 14)] + [(3, 6)]
 CORNER_LINES = -(-len(CORNER) // 8) * 8
 Z_UNITS = 24
 F32 = jnp.float32

time: 37.7 us -> 37.6 us (level)
  no operation moved by 1% of the time
where the time goes in v7:
time: 37.6 us; the launch traced here: 37.3 us
  starting transfers between devices  15.4 us (41%)
  waiting for transfers between devices  10.8 us (29%)
  Pallas kernels  8.89 us (24%)
  local copies, waits for them, and re-layouts  1.5 us (4%)
  between operations  0.7 us (2%)
    ppermute x6, starting transfers between devices, swapped(): arrived.append(lax.ppermute(value, axes, pairs))  10.7 us
    pallas_call x6, Pallas kernels, call(): pl.pallas_call(kernel, out_shape=[jax.ShapeDtypeStruct(*o) if i < leave e...  8.89 us
    all_to_all x1, waiting for transfers between devices, local(): lax.all_to_all(send, ('bx', 'by'), split_axis=0, concat_axis=0, tiled=True)  6.83 us
    all_to_all x1, starting transfers between devices, local(): lax.all_to_all(send, ('bx', 'by'), split_axis=0, concat_axis=0, tiled=True)  4.71 us
    ppermute x6, waiting for transfers between devices, swapped(): arrived.append(lax.ppermute(value, axes, pairs))  2.74 us
    unnamed x6, local copies, waits for them, and re-layouts  1.5 us
    ppermute x1, waiting for transfers between devices, local(): zg = lax.ppermute(zp, 'gz', [(0, 1), (1, 0)])  1.22 us
  transfers between devices with their start and end apart: 8, of which 4 were waited for; matrix products, arithmetic and copies ran while one was open for 4% of the time, Pallas kernels for 2%

profile of v7, /device:TPU:0, one launch (start us, length us, event | category | flops | bytes accessed | tf_op | source)
XLA Modules:
  0.0 37.3 jit_solution(12662371023919584087)
XLA Ops:
  0.6 2.0 %shard_map.121 = (f32[17,16,128]{2,1,0:T(8,128)S(1)}, f32[17,16,128]{2,1,0:T(8,128)S(1)}, f32[17,16,128]{2,1,0:T(8,128)S(1)}, f32[17,16,128]{2,1,0:T(8,128)S(1)}...) custom-call(s32[8]{0:T(128)} %cells_ref.1, ...), custom_call_target="tpu_custom_call" | custom-call | tf_op jit(solution)/shard_map/pallas_call | solution.py:481
  2.6 0.5 %collective-permute-start = (f32[17,16,128]{2,1,0:T(8,128)S(1)}, f32[17,16,128]{2,1,0:T(8,128)S(1)}, u32[]{:S(2)}, u32[]{:S(2)}) collective-permute-start(f32[17,16,128]{2,1,0:T(8,128)S(1)} %get-tuple-element.34), channel_id=1, source_target_pairs={{0,1},{1,0},{2,4},{3,5},{4,2},{5,3},{6,7},{7,6},{8,9},{9,8},{10,12... | collective-permute-start | bytes 417800 | tf_op jit(solution)/shard_map/ppermute | solution.py:507
  3.1 4.1 %collective-permute-start.1 = (f32[17,16,128]{2,1,0:T(8,128)S(1)}, f32[17,16,128]{2,1,0:T(8,128)S(1)}, u32[]{:S(2)}, u32[]{:S(2)}) collective-permute-start(f32[17,16,128]{2,1,0:T(8,128)S(1)} %get-tuple-element.35), channel_id=1, source_target_pairs={{0,2},{1,3},{2,0},{3,1},{4,6},{5,7},{6,4},{7,5},{8,10},{9,11},{10,... | collective-permute-start | bytes 417800 | tf_op jit(solution)/shard_map/ppermute | solution.py:507
  7.3 0.0 collective-permute-start.4
  7.3 3.0 %collective-permute-start.5 = (f32[17,16,128]{2,1,0:T(8,128)S(1)}, f32[17,16,128]{2,1,0:T(8,128)S(1)}, u32[]{:S(2)}, u32[]{:S(2)}) collective-permute-start(f32[17,16,128]{2,1,0:T(8,128)S(1)} %get-tuple-element.49), channel_id=1, source_target_pairs={{0,8},{1,9},{2,10},{3,11},{4,12},{5,13},{6,14},{7,15},{8,0},{9,1},... | collective-permute-start | bytes 417800 | tf_op jit(solution)/shard_map/ppermute | solution.py:507
  10.3 0.0 collective-permute-done.gb_ref
  10.3 0.4 %collective-permute-done.1.ga_ref = f32[17,16,128]{2,1,0:T(8,128)S(1)} collective-permute-done((f32[17,16,128]{2,1,0:T(8,128)S(1)}, f32[17,16,128]{2,1,0:T(8,128)S(1)}, u32[]{:S(2)}, u32[]{:S(2)}) %collective-permute-start.1) | collective-permute-done | bytes 139296 | tf_op jit(solution)/shard_map/ppermute | solution.py:507
  10.7 0.1 collective-permute-start.2
  10.8 3.0 %collective-permute-start.3 = (f32[32,128]{1,0:T(8,128)S(1)}, f32[32,128]{1,0:T(8,128)S(1)}, u32[]{:S(2)}, u32[]{:S(2)}) collective-permute-start(f32[32,128]{1,0:T(8,128)S(1)} %get-tuple-element.44), channel_id=1, source_target_pairs={{0,8},{1,9},{2,10},{3,11},{4,12},{5,13},{6,14},{7,15},{8,0},{9,1},... | collective-permute-start | bytes 49160 | tf_op jit(solution)/shard_map/ppermute | solution.py:507
  13.8 0.0 slice-start
  13.8 0.0 slice-start.1
  13.8 0.7 %shard_map.123 = (f32[13,20,16,128]{3,2,1,0:T(8,128)S(1)}, f32[20,16,128]{2,1,0:T(8,128)S(1)}, bf16[2,272,256]{2,1,0:T(8,128)(2,1)S(1)}, f32[16,128]{1,0:T(8,128)S(1)}) custom-call(f32[13,16,16,128]{3,2,1,0:T(8,128)S(1)} %get-tuple-element.33.own_ref, f32[17,16,128]{2,1,0:T(8,128)S(1)} %collective-permute-done.gb_ref, ...), custom_call_target="tpu_custom_call" | custom-call | flops 5000000000 | bytes 1000 | tf_op jit(solution)/shard_map/pallas_call | solution.py:481
  14.4 0.0 collective-permute-done.2.cb_ref
  14.4 2.3 %collective-permute-done.3.ca_ref = f32[32,128]{1,0:T(8,128)S(1)} collective-permute-done((f32[32,128]{1,0:T(8,128)S(1)}, f32[32,128]{1,0:T(8,128)S(1)}, u32[]{:S(2)}, u32[]{:S(2)}) %collective-permute-start.3) | collective-permute-done | bytes 16416 | tf_op jit(solution)/shard_map/ppermute | solution.py:507
  16.8 0.0 collective-permute-done.4.xb_ref
  16.8 0.0 collective-permute-done.5.xa_ref
  16.8 0.5 %shard_map.124 = (f32[13,20,8,128]{3,2,1,0:T(8,128)S(1)}, f32[24,512]{1,0:T(8,128)S(1)}) custom-call(f32[20,16,128]{2,1,0:T(8,128)S(1)} %get-tuple-element.47.acc_ref, f32[17,16,128]{2,1,0:T(8,128)S(1)} %collective-permute-done.4.xb_ref, f32[17,16,128]{2,1,0:T(8,128)S(1)} %collective-permute-done.5.xa_ref, f32[32,128]{1,0:T(8,128)S(1)} %collective-permute-done.2.cb_ref, ...), custom_call_target="tpu_custom_call" | custom-call | tf_op jit(solution)/shard_map/pallas_call | solution.py:481
  17.2 0.1 collective-permute-start.6
  17.3 1.2 %collective-permute-done.6.zg_ref = f32[24,512]{1,0:T(8,128)S(1)} collective-permute-done((f32[24,512]{1,0:T(8,128)S(1)}, f32[24,512]{1,0:T(8,128)S(1)}, u32[]{:S(2)}, u32[]{:S(2)}) %collective-permute-start.6) | collective-permute-done | bytes 49184 | tf_op jit(solution)/shard_map/ppermute | solution.py:551
  18.5 0.0 slice-done
  18.5 0.0 slice-done.1
  18.5 4.6 %shard_map.125 = (f32[3,16,16,128]{3,2,1,0:T(8,128)S(1)}, f32[3,16,16,128]{3,2,1,0:T(8,128)S(1)}, f32[272,128]{1,0:T(8,128)}) custom-call(f32[13,20,16,128]{3,2,1,0:T(8,128)S(1)} %get-tuple-element.42.body_ref, f32[13,20,8,128]{3,2,1,0:T(8,128)S(1)} %get-tuple-element.52.side_ref, f32[24,512]{1,0:T(8,128)S(1)} %get-tuple-element.53.zo_ref, ...), custom_call_target="tpu_custom_call" | custom-call | tf_op jit(solution)/shard_map/pallas_call | solution.py:481
  23.1 4.7 %all-to-all-start = ((f32[272,1,128]{2,1,0:T(1,128)}), f32[272,1,128]{2,1,0:T(1,128)S(1)}, u32[]{:S(2)}, u32[]{:S(2)}) async-start(f32[272,1,128]{2,1,0:T(1,128)} %bitcast.4), calls=%async_computation | async-start | bytes 278528 | tf_op jit(solution)/shard_map/all_to_all | solution.py:569
  27.8 0.7 %copy.14 = f32[3,16,16,128]{3,2,1,0:T(8,128)} copy(f32[3,16,16,128]{3,2,1,0:T(8,128)S(1)} %get-tuple-element.63) | data formatting | bytes 786432
  28.6 0.7 %copy.15 = f32[3,16,16,128]{3,2,1,0:T(8,128)} copy(f32[3,16,16,128]{3,2,1,0:T(8,128)S(1)} %get-tuple-element.64) | data formatting | bytes 786432
  29.3 6.8 %all-to-all-done = f32[272,1,128]{2,1,0:T(1,128)S(1)} async-done(((f32[272,1,128]{2,1,0:T(1,128)}), f32[272,1,128]{2,1,0:T(1,128)S(1)}, u32[]{:S(2)}, u32[]{:S(2)}) %all-to-all-start) | async-done | bytes 139296 | tf_op jit(solution)/shard_map/all_to_all | solution.py:569
  36.1 1.2 %shard_map.126 = f32[64,128]{1,0:T(8,128)} custom-call(f32[272,128]{1,0:T(8,128)S(1)} %bitcast.10), custom_call_target="tpu_custom_call" | custom-call | tf_op jit(solution)/shard_map/pallas_call | solution.py:481
  (2 shorter events, 0.0 us)
Async XLA Ops:
  2.6 7.7 %collective-permute-start = (f32[17,16,128]{2,1,0:T(8,128)S(1)}, f32[17,16,128]{2,1,0:T(8,128)S(1)}, u32[]{:S(2)}, u32[]{:S(2)}) collective-permute-start(f32[17,16,128]{2,1,0:T(8,128)S(1)} %get-tuple-element.34), channel_id=1, source_target_pairs={{0,1},{1,0},{2,4},{3,5},{4,2},{5,3},{6,7},{7,6},{8,9},{9,8},{10,12... | collective-permute-start | bytes 417800 | tf_op jit(solution)/shard_map/ppermute | solution.py:507
  3.1 7.5 %collective-permute-start.1 = (f32[17,16,128]{2,1,0:T(8,128)S(1)}, f32[17,16,128]{2,1,0:T(8,128)S(1)}, u32[]{:S(2)}, u32[]{:S(2)}) collective-permute-start(f32[17,16,128]{2,1,0:T(8,128)S(1)} %get-tuple-element.35), channel_id=1, source_target_pairs={{0,2},{1,3},{2,0},{3,1},{4,6},{5,7},{6,4},{7,5},{8,10},{9,11},{10,... | collective-permute-start | bytes 417800 | tf_op jit(solution)/shard_map/ppermute | solution.py:507
  7.3 9.5 %collective-permute-start.4 = (f32[17,16,128]{2,1,0:T(8,128)S(1)}, f32[17,16,128]{2,1,0:T(8,128)S(1)}, u32[]{:S(2)}, u32[]{:S(2)}) collective-permute-start(f32[17,16,128]{2,1,0:T(8,128)S(1)} %get-tuple-element.48), channel_id=1, source_target_pairs={{0,1},{1,0},{2,3},{3,2},{4,5},{5,4},{6,7},{7,6},{8,16},{9,17},{10,... | collective-permute-start | bytes 417800 | tf_op jit(solution)/shard_map/ppermute | solution.py:507
  7.3 9.5 %collective-permute-start.5 = (f32[17,16,128]{2,1,0:T(8,128)S(1)}, f32[17,16,128]{2,1,0:T(8,128)S(1)}, u32[]{:S(2)}, u32[]{:S(2)}) collective-permute-start(f32[17,16,128]{2,1,0:T(8,128)S(1)} %get-tuple-element.49), channel_id=1, source_target_pairs={{0,8},{1,9},{2,10},{3,11},{4,12},{5,13},{6,14},{7,15},{8,0},{9,1},... | collective-permute-start | bytes 417800 | tf_op jit(solution)/shard_map/ppermute | solution.py:507
  10.7 3.7 %collective-permute-start.2 = (f32[32,128]{1,0:T(8,128)S(1)}, f32[32,128]{1,0:T(8,128)S(1)}, u32[]{:S(2)}, u32[]{:S(2)}) collective-permute-start(f32[32,128]{1,0:T(8,128)S(1)} %get-tuple-element.43), channel_id=1, source_target_pairs={{0,1},{1,0},{2,3},{3,2},{4,5},{5,4},{6,7},{7,6},{8,16},{9,17},{10,... | collective-permute-start | bytes 49160 | tf_op jit(solution)/shard_map/ppermute | solution.py:507
  10.8 6.0 %collective-permute-start.3 = (f32[32,128]{1,0:T(8,128)S(1)}, f32[32,128]{1,0:T(8,128)S(1)}, u32[]{:S(2)}, u32[]{:S(2)}) collective-permute-start(f32[32,128]{1,0:T(8,128)S(1)} %get-tuple-element.44), channel_id=1, source_target_pairs={{0,8},{1,9},{2,10},{3,11},{4,12},{5,13},{6,14},{7,15},{8,0},{9,1},... | collective-permute-start | bytes 49160 | tf_op jit(solution)/shard_map/ppermute | solution.py:507
  13.8 4.8 %slice-start = ((s8[8388608]{0:T(1024)(128)(4,1)}), s8[4194304]{0:T(1024)(128)(4,1)S(1)}, s32[]{:S(2)}) async-start(s8[8388608]{0:T(1024)(128)(4,1)} %bitcast.7), calls=%async_computation.1 | async-start | bytes 8388608
  13.8 4.8 %slice-start.1 = ((s8[8388608]{0:T(1024)(128)(4,1)}), s8[4194304]{0:T(1024)(128)(4,1)S(1)}, s32[]{:S(2)}) async-start(s8[8388608]{0:T(1024)(128)(4,1)} %bitcast.7), calls=%async_computation.2 | async-start | bytes 8388608
  17.2 1.3 %collective-permute-start.6 = (f32[24,512]{1,0:T(8,128)S(1)}, f32[24,512]{1,0:T(8,128)S(1)}, u32[]{:S(2)}, u32[]{:S(2)}) collective-permute-start(f32[24,512]{1,0:T(8,128)S(1)} %get-tuple-element.53.zo_ref), channel_id=1, source_target_pairs={{0,1},{1,0},{2,3},{3,2},{4,5},{5,4},{6,7},{7,6},{8,9},{9,8},{10,11... | collective-permute-start | bytes 147464 | tf_op jit(solution)/shard_map/ppermute | solution.py:551
  23.1 13.0 %all-to-all-start = ((f32[272,1,128]{2,1,0:T(1,128)}), f32[272,1,128]{2,1,0:T(1,128)S(1)}, u32[]{:S(2)}, u32[]{:S(2)}) async-start(f32[272,1,128]{2,1,0:T(1,128)} %bitcast.4), calls=%async_computation | async-start | bytes 278528 | tf_op jit(solution)/shard_map/all_to_all | solution.py:569

commit v8 on v7

--- a/solution.py
+++ b/solution.py
@@ -69,7 +69,7 @@
             c_out_ref[c, y] = weight
         return carry
 
-    lax.fori_loop(0, ny, row, 0, unroll=8)
+    lax.fori_loop(0, ny, row, 0, unroll=16)
 
     def y_face(out, near, deep, up):
         layers = [[own_ref[i, y] for i in range(ARRAYS)] for y in (near, deep)]
@@ -529,7 +529,7 @@
     )
     gb, ga = swapped(fb, fa, "by", (1, 0))
     xb, xa = swapped(xb, xa, "bx", (1, 0))
-    cb, ca = call(corner_kernel, [corner, corner], [gb, ga])
+    cb, ca = call(corner_kernel, [corner, corner], [gb, ga], cost=pl.CostEstimate(flops=5_000_000_000, transcendentals=0, bytes_accessed=1000))
     cb, ca, owner, group = lax.optimization_barrier((cb, ca, owner, group))
     cb, ca = swapped(cb, ca, "bx", (1, 0))
     flat_basis = basis.reshape(blocks * KB, basis.shape[2])
@@ -538,7 +538,6 @@
         functools.partial(widen_kernel, rows, width),
         [((ARRAYS, wy, nx, nz), F32), ((wy, nx, nz), F32), ((2, planes * width, blocks), BF16), ((planes, 128), F32)],
         [own, gb, ga, owner, group],
-        cost=pl.CostEstimate(flops=5_000_000_000, transcendentals=0, bytes_accessed=1000),
     )
     cb, ca, ids, acc = lax.optimization_barrier((cb, ca, ids, acc))
     full = -(-wy * wx // 128) * 128

time: 37.6 us -> 37.6 us (level)
  no operation moved by 1% of the time
where the time goes in v8:
time: 37.6 us; the launch traced here: 37.3 us
  starting transfers between devices  15.4 us (41%)
  waiting for transfers between devices  10.8 us (29%)
  Pallas kernels  8.87 us (24%)
  local copies, waits for them, and re-layouts  1.5 us (4%)
  between operations  0.7 us (2%)
    ppermute x6, starting transfers between devices, swapped(): arrived.append(lax.ppermute(value, axes, pairs))  10.7 us
    pallas_call x6, Pallas kernels, call(): pl.pallas_call(kernel, out_shape=[jax.ShapeDtypeStruct(*o) if i < leave e...  8.87 us
    all_to_all x1, waiting for transfers between devices, local(): lax.all_to_all(send, ('bx', 'by'), split_axis=0, concat_axis=0, tiled=True)  6.83 us
    all_to_all x1, starting transfers between devices, local(): lax.all_to_all(send, ('bx', 'by'), split_axis=0, concat_axis=0, tiled=True)  4.71 us
    ppermute x6, waiting for transfers between devices, swapped(): arrived.append(lax.ppermute(value, axes, pairs))  2.74 us
    unnamed x6, local copies, waits for them, and re-layouts  1.5 us
    ppermute x1, waiting for transfers between devices, local(): zg = lax.ppermute(zp, 'gz', [(0, 1), (1, 0)])  1.22 us
  transfers between devices with their start and end apart: 8, of which 4 were waited for; matrix products, arithmetic and copies ran while one was open for 4% of the time, Pallas kernels for 2%

profile of v8, /device:TPU:0, one launch (start us, length us, event | category | flops | bytes accessed | tf_op | source)
XLA Modules:
  0.0 37.3 jit_solution(10234091085923707641)
XLA Ops:
  0.6 1.9 %shard_map.121 = (f32[17,16,128]{2,1,0:T(8,128)S(1)}, f32[17,16,128]{2,1,0:T(8,128)S(1)}, f32[17,16,128]{2,1,0:T(8,128)S(1)}, f32[17,16,128]{2,1,0:T(8,128)S(1)}...) custom-call(s32[8]{0:T(128)} %cells_ref.1, ...), custom_call_target="tpu_custom_call" | custom-call | tf_op jit(solution)/shard_map/pallas_call | solution.py:481
  2.6 0.5 %collective-permute-start = (f32[17,16,128]{2,1,0:T(8,128)S(1)}, f32[17,16,128]{2,1,0:T(8,128)S(1)}, u32[]{:S(2)}, u32[]{:S(2)}) collective-permute-start(f32[17,16,128]{2,1,0:T(8,128)S(1)} %get-tuple-element.34), channel_id=1, source_target_pairs={{0,1},{1,0},{2,4},{3,5},{4,2},{5,3},{6,7},{7,6},{8,9},{9,8},{10,12... | collective-permute-start | bytes 417800 | tf_op jit(solution)/shard_map/ppermute | solution.py:507
  3.1 4.1 %collective-permute-start.1 = (f32[17,16,128]{2,1,0:T(8,128)S(1)}, f32[17,16,128]{2,1,0:T(8,128)S(1)}, u32[]{:S(2)}, u32[]{:S(2)}) collective-permute-start(f32[17,16,128]{2,1,0:T(8,128)S(1)} %get-tuple-element.35), channel_id=1, source_target_pairs={{0,2},{1,3},{2,0},{3,1},{4,6},{5,7},{6,4},{7,5},{8,10},{9,11},{10,... | collective-permute-start | bytes 417800 | tf_op jit(solution)/shard_map/ppermute | solution.py:507
  7.2 0.0 collective-permute-start.4
  7.2 0.0 slice-start
  7.3 0.0 slice-start.1
  7.3 3.0 %collective-permute-start.5 = (f32[17,16,128]{2,1,0:T(8,128)S(1)}, f32[17,16,128]{2,1,0:T(8,128)S(1)}, u32[]{:S(2)}, u32[]{:S(2)}) collective-permute-start(f32[17,16,128]{2,1,0:T(8,128)S(1)} %get-tuple-element.49), channel_id=1, source_target_pairs={{0,8},{1,9},{2,10},{3,11},{4,12},{5,13},{6,14},{7,15},{8,0},{9,1},... | collective-permute-start | bytes 417800 | tf_op jit(solution)/shard_map/ppermute | solution.py:507
  10.2 0.0 collective-permute-done.gb_ref
  10.2 0.4 %collective-permute-done.1.ga_ref = f32[17,16,128]{2,1,0:T(8,128)S(1)} collective-permute-done((f32[17,16,128]{2,1,0:T(8,128)S(1)}, f32[17,16,128]{2,1,0:T(8,128)S(1)}, u32[]{:S(2)}, u32[]{:S(2)}) %collective-permute-start.1) | collective-permute-done | bytes 139296 | tf_op jit(solution)/shard_map/ppermute | solution.py:507
  10.7 0.1 collective-permute-start.2
  10.8 3.0 %collective-permute-start.3 = (f32[32,128]{1,0:T(8,128)S(1)}, f32[32,128]{1,0:T(8,128)S(1)}, u32[]{:S(2)}, u32[]{:S(2)}) collective-permute-start(f32[32,128]{1,0:T(8,128)S(1)} %get-tuple-element.44), channel_id=1, source_target_pairs={{0,8},{1,9},{2,10},{3,11},{4,12},{5,13},{6,14},{7,15},{8,0},{9,1},... | collective-permute-start | bytes 49160 | tf_op jit(solution)/shard_map/ppermute | solution.py:507
  13.7 0.7 %shard_map.123 = (f32[13,20,16,128]{3,2,1,0:T(8,128)S(1)}, f32[20,16,128]{2,1,0:T(8,128)S(1)}, bf16[2,272,256]{2,1,0:T(8,128)(2,1)S(1)}, f32[16,128]{1,0:T(8,128)S(1)}) custom-call(f32[13,16,16,128]{3,2,1,0:T(8,128)S(1)} %get-tuple-element.33.own_ref, f32[17,16,128]{2,1,0:T(8,128)S(1)} %collective-permute-done.gb_ref, ...), custom_call_target="tpu_custom_call" | custom-call | tf_op jit(solution)/shard_map/pallas_call | solution.py:481
  14.4 0.0 collective-permute-done.2.cb_ref
  14.4 2.3 %collective-permute-done.3.ca_ref = f32[32,128]{1,0:T(8,128)S(1)} collective-permute-done((f32[32,128]{1,0:T(8,128)S(1)}, f32[32,128]{1,0:T(8,128)S(1)}, u32[]{:S(2)}, u32[]{:S(2)}) %collective-permute-start.3) | collective-permute-done | bytes 16416 | tf_op jit(solution)/shard_map/ppermute | solution.py:507
  16.7 0.0 collective-permute-done.4.xb_ref
  16.7 0.0 collective-permute-done.5.xa_ref
  16.7 0.5 %shard_map.124 = (f32[13,20,8,128]{3,2,1,0:T(8,128)S(1)}, f32[24,512]{1,0:T(8,128)S(1)}) custom-call(f32[20,16,128]{2,1,0:T(8,128)S(1)} %get-tuple-element.47.acc_ref, f32[17,16,128]{2,1,0:T(8,128)S(1)} %collective-permute-done.4.xb_ref, f32[17,16,128]{2,1,0:T(8,128)S(1)} %collective-permute-done.5.xa_ref, f32[32,128]{1,0:T(8,128)S(1)} %collective-permute-done.2.cb_ref, ...), custom_call_target="tpu_custom_call" | custom-call | tf_op jit(solution)/shard_map/pallas_call | solution.py:481
  17.2 0.1 collective-permute-start.6
  17.3 1.2 %collective-permute-done.6.zg_ref = f32[24,512]{1,0:T(8,128)S(1)} collective-permute-done((f32[24,512]{1,0:T(8,128)S(1)}, f32[24,512]{1,0:T(8,128)S(1)}, u32[]{:S(2)}, u32[]{:S(2)}) %collective-permute-start.6) | collective-permute-done | bytes 49184 | tf_op jit(solution)/shard_map/ppermute | solution.py:550
  18.5 0.0 slice-done
  18.5 0.0 slice-done.1
  18.5 4.6 %shard_map.125 = (f32[3,16,16,128]{3,2,1,0:T(8,128)S(1)}, f32[3,16,16,128]{3,2,1,0:T(8,128)S(1)}, f32[272,128]{1,0:T(8,128)}) custom-call(f32[13,20,16,128]{3,2,1,0:T(8,128)S(1)} %get-tuple-element.42.body_ref, f32[13,20,8,128]{3,2,1,0:T(8,128)S(1)} %get-tuple-element.52.side_ref, f32[24,512]{1,0:T(8,128)S(1)} %get-tuple-element.53.zo_ref, ...), custom_call_target="tpu_custom_call" | custom-call | tf_op jit(solution)/shard_map/pallas_call | solution.py:481
  23.1 4.7 %all-to-all-start = ((f32[272,1,128]{2,1,0:T(1,128)}), f32[272,1,128]{2,1,0:T(1,128)S(1)}, u32[]{:S(2)}, u32[]{:S(2)}) async-start(f32[272,1,128]{2,1,0:T(1,128)} %bitcast.4), calls=%async_computation | async-start | bytes 278528 | tf_op jit(solution)/shard_map/all_to_all | solution.py:568
  27.8 0.7 %copy.14 = f32[3,16,16,128]{3,2,1,0:T(8,128)} copy(f32[3,16,16,128]{3,2,1,0:T(8,128)S(1)} %get-tuple-element.63) | data formatting | bytes 786432
  28.5 0.7 %copy.15 = f32[3,16,16,128]{3,2,1,0:T(8,128)} copy(f32[3,16,16,128]{3,2,1,0:T(8,128)S(1)} %get-tuple-element.64) | data formatting | bytes 786432
  29.3 6.8 %all-to-all-done = f32[272,1,128]{2,1,0:T(1,128)S(1)} async-done(((f32[272,1,128]{2,1,0:T(1,128)}), f32[272,1,128]{2,1,0:T(1,128)S(1)}, u32[]{:S(2)}, u32[]{:S(2)}) %all-to-all-start) | async-done | bytes 139296 | tf_op jit(solution)/shard_map/all_to_all | solution.py:568
  36.1 1.2 %shard_map.126 = f32[64,128]{1,0:T(8,128)} custom-call(f32[272,128]{1,0:T(8,128)S(1)} %bitcast.10), custom_call_target="tpu_custom_call" | custom-call | tf_op jit(solution)/shard_map/pallas_call | solution.py:481
  (2 shorter events, 0.0 us)
Async XLA Ops:
  2.6 7.7 %collective-permute-start = (f32[17,16,128]{2,1,0:T(8,128)S(1)}, f32[17,16,128]{2,1,0:T(8,128)S(1)}, u32[]{:S(2)}, u32[]{:S(2)}) collective-permute-start(f32[17,16,128]{2,1,0:T(8,128)S(1)} %get-tuple-element.34), channel_id=1, source_target_pairs={{0,1},{1,0},{2,4},{3,5},{4,2},{5,3},{6,7},{7,6},{8,9},{9,8},{10,12... | collective-permute-start | bytes 417800 | tf_op jit(solution)/shard_map/ppermute | solution.py:507
  3.1 7.5 %collective-permute-start.1 = (f32[17,16,128]{2,1,0:T(8,128)S(1)}, f32[17,16,128]{2,1,0:T(8,128)S(1)}, u32[]{:S(2)}, u32[]{:S(2)}) collective-permute-start(f32[17,16,128]{2,1,0:T(8,128)S(1)} %get-tuple-element.35), channel_id=1, source_target_pairs={{0,2},{1,3},{2,0},{3,1},{4,6},{5,7},{6,4},{7,5},{8,10},{9,11},{10,... | collective-permute-start | bytes 417800 | tf_op jit(solution)/shard_map/ppermute | solution.py:507
  7.2 9.5 %collective-permute-start.4 = (f32[17,16,128]{2,1,0:T(8,128)S(1)}, f32[17,16,128]{2,1,0:T(8,128)S(1)}, u32[]{:S(2)}, u32[]{:S(2)}) collective-permute-start(f32[17,16,128]{2,1,0:T(8,128)S(1)} %get-tuple-element.48), channel_id=1, source_target_pairs={{0,1},{1,0},{2,3},{3,2},{4,5},{5,4},{6,7},{7,6},{8,16},{9,17},{10,... | collective-permute-start | bytes 417800 | tf_op jit(solution)/shard_map/ppermute | solution.py:507
  7.2 11.2 %slice-start = ((s8[8388608]{0:T(1024)(128)(4,1)}), s8[4194304]{0:T(1024)(128)(4,1)S(1)}, s32[]{:S(2)}) async-start(s8[8388608]{0:T(1024)(128)(4,1)} %bitcast.7), calls=%async_computation.1 | async-start | bytes 8388608
  7.3 11.2 %slice-start.1 = ((s8[8388608]{0:T(1024)(128)(4,1)}), s8[4194304]{0:T(1024)(128)(4,1)S(1)}, s32[]{:S(2)}) async-start(s8[8388608]{0:T(1024)(128)(4,1)} %bitcast.7), calls=%async_computation.2 | async-start | bytes 8388608
  7.3 9.5 %collective-permute-start.5 = (f32[17,16,128]{2,1,0:T(8,128)S(1)}, f32[17,16,128]{2,1,0:T(8,128)S(1)}, u32[]{:S(2)}, u32[]{:S(2)}) collective-permute-start(f32[17,16,128]{2,1,0:T(8,128)S(1)} %get-tuple-element.49), channel_id=1, source_target_pairs={{0,8},{1,9},{2,10},{3,11},{4,12},{5,13},{6,14},{7,15},{8,0},{9,1},... | collective-permute-start | bytes 417800 | tf_op jit(solution)/shard_map/ppermute | solution.py:507
  10.7 3.7 %collective-permute-start.2 = (f32[32,128]{1,0:T(8,128)S(1)}, f32[32,128]{1,0:T(8,128)S(1)}, u32[]{:S(2)}, u32[]{:S(2)}) collective-permute-start(f32[32,128]{1,0:T(8,128)S(1)} %get-tuple-element.43), channel_id=1, source_target_pairs={{0,1},{1,0},{2,3},{3,2},{4,5},{5,4},{6,7},{7,6},{8,16},{9,17},{10,... | collective-permute-start | bytes 49160 | tf_op jit(solution)/shard_map/ppermute | solution.py:507
  10.8 6.0 %collective-permute-start.3 = (f32[32,128]{1,0:T(8,128)S(1)}, f32[32,128]{1,0:T(8,128)S(1)}, u32[]{:S(2)}, u32[]{:S(2)}) collective-permute-start(f32[32,128]{1,0:T(8,128)S(1)} %get-tuple-element.44), channel_id=1, source_target_pairs={{0,8},{1,9},{2,10},{3,11},{4,12},{5,13},{6,14},{7,15},{8,0},{9,1},... | collective-permute-start | bytes 49160 | tf_op jit(solution)/shard_map/ppermute | solution.py:507
  17.2 1.3 %collective-permute-start.6 = (f32[24,512]{1,0:T(8,128)S(1)}, f32[24,512]{1,0:T(8,128)S(1)}, u32[]{:S(2)}, u32[]{:S(2)}) collective-permute-start(f32[24,512]{1,0:T(8,128)S(1)} %get-tuple-element.53.zo_ref), channel_id=1, source_target_pairs={{0,1},{1,0},{2,3},{3,2},{4,5},{5,4},{6,7},{7,6},{8,9},{9,8},{10,11... | collective-permute-start | bytes 147464 | tf_op jit(solution)/shard_map/ppermute | solution.py:550
  23.1 13.0 %all-to-all-start = ((f32[272,1,128]{2,1,0:T(1,128)}), f32[272,1,128]{2,1,0:T(1,128)S(1)}, u32[]{:S(2)}, u32[]{:S(2)}) async-start(f32[272,1,128]{2,1,0:T(1,128)} %bitcast.4), calls=%async_computation | async-start | bytes 278528 | tf_op jit(solution)/shard_map/all_to_all | solution.py:568

commit v9 on v8

--- a/solution.py
+++ b/solution.py
@@ -384,14 +384,10 @@
     for n in range(1, ny // 2):
         for y in (2 * n + 2, 2 * n + 3):
             second_electric(y)
-        for y in (2 * n, 2 * n + 1):
-            last_magnetic(y)
-        for y in (2 * n, 2 * n + 1):
-            last_electric(y)
         project(n - 1)
-    for y in (ny, ny + 1):
+    for y in range(2, ny + 2):
         last_magnetic(y)
-    for y in (ny, ny + 1):
+    for y in range(2, ny + 2):
         last_electric(y)
     project(ny // 2 - 1)
 

time: 37.6 us -> 37.7 us (level)
  no operation moved by 1% of the time
where the time goes in v9:
time: 37.7 us; the launch traced here: 37.4 us
  starting transfers between devices  15.4 us (41%)
  waiting for transfers between devices  10.8 us (29%)
  Pallas kernels  8.99 us (24%)
  local copies, waits for them, and re-layouts  1.5 us (4%)
  between operations  0.7 us (2%)
    ppermute x6, starting transfers between devices, swapped(): arrived.append(lax.ppermute(value, axes, pairs))  10.7 us
    pallas_call x6, Pallas kernels, call(): pl.pallas_call(kernel, out_shape=[jax.ShapeDtypeStruct(*o) if i < leave e...  8.99 us
    all_to_all x1, waiting for transfers between devices, local(): lax.all_to_all(send, ('bx', 'by'), split_axis=0, concat_axis=0, tiled=True)  6.83 us
    all_to_all x1, starting transfers between devices, local(): lax.all_to_all(send, ('bx', 'by'), split_axis=0, concat_axis=0, tiled=True)  4.71 us
    ppermute x6, waiting for transfers between devices, swapped(): arrived.append(lax.ppermute(value, axes, pairs))  2.74 us
    unnamed x6, local copies, waits for them, and re-layouts  1.5 us
    ppermute x1, waiting for transfers between devices, local(): zg = lax.ppermute(zp, 'gz', [(0, 1), (1, 0)])  1.22 us
  transfers between devices with their start and end apart: 8, of which 4 were waited for; matrix products, arithmetic and copies ran while one was open for 4% of the time, Pallas kernels for 2%

profile of v9, /device:TPU:0, one launch (start us, length us, event | category | flops | bytes accessed | tf_op | source)
XLA Modules:
  0.0 37.4 jit_solution(12917885526914123291)
XLA Ops:
  0.6 1.9 %shard_map.121 = (f32[17,16,128]{2,1,0:T(8,128)S(1)}, f32[17,16,128]{2,1,0:T(8,128)S(1)}, f32[17,16,128]{2,1,0:T(8,128)S(1)}, f32[17,16,128]{2,1,0:T(8,128)S(1)}...) custom-call(s32[8]{0:T(128)} %cells_ref.1, ...), custom_call_target="tpu_custom_call" | custom-call | tf_op jit(solution)/shard_map/pallas_call | solution.py:477
  2.6 0.5 %collective-permute-start = (f32[17,16,128]{2,1,0:T(8,128)S(1)}, f32[17,16,128]{2,1,0:T(8,128)S(1)}, u32[]{:S(2)}, u32[]{:S(2)}) collective-permute-start(f32[17,16,128]{2,1,0:T(8,128)S(1)} %get-tuple-element.34), channel_id=1, source_target_pairs={{0,1},{1,0},{2,4},{3,5},{4,2},{5,3},{6,7},{7,6},{8,9},{9,8},{10,12... | collective-permute-start | bytes 417800 | tf_op jit(solution)/shard_map/ppermute | solution.py:503
  3.1 4.1 %collective-permute-start.1 = (f32[17,16,128]{2,1,0:T(8,128)S(1)}, f32[17,16,128]{2,1,0:T(8,128)S(1)}, u32[]{:S(2)}, u32[]{:S(2)}) collective-permute-start(f32[17,16,128]{2,1,0:T(8,128)S(1)} %get-tuple-element.35), channel_id=1, source_target_pairs={{0,2},{1,3},{2,0},{3,1},{4,6},{5,7},{6,4},{7,5},{8,10},{9,11},{10,... | collective-permute-start | bytes 417800 | tf_op jit(solution)/shard_map/ppermute | solution.py:503
  7.2 0.0 collective-permute-start.4
  7.2 0.0 slice-start
  7.3 0.0 slice-start.1
  7.3 3.0 %collective-permute-start.5 = (f32[17,16,128]{2,1,0:T(8,128)S(1)}, f32[17,16,128]{2,1,0:T(8,128)S(1)}, u32[]{:S(2)}, u32[]{:S(2)}) collective-permute-start(f32[17,16,128]{2,1,0:T(8,128)S(1)} %get-tuple-element.49), channel_id=1, source_target_pairs={{0,8},{1,9},{2,10},{3,11},{4,12},{5,13},{6,14},{7,15},{8,0},{9,1},... | collective-permute-start | bytes 417800 | tf_op jit(solution)/shard_map/ppermute | solution.py:503
  10.2 0.0 collective-permute-done.gb_ref
  10.2 0.4 %collective-permute-done.1.ga_ref = f32[17,16,128]{2,1,0:T(8,128)S(1)} collective-permute-done((f32[17,16,128]{2,1,0:T(8,128)S(1)}, f32[17,16,128]{2,1,0:T(8,128)S(1)}, u32[]{:S(2)}, u32[]{:S(2)}) %collective-permute-start.1) | collective-permute-done | bytes 139296 | tf_op jit(solution)/shard_map/ppermute | solution.py:503
  10.7 0.1 collective-permute-start.2
  10.8 3.0 %collective-permute-start.3 = (f32[32,128]{1,0:T(8,128)S(1)}, f32[32,128]{1,0:T(8,128)S(1)}, u32[]{:S(2)}, u32[]{:S(2)}) collective-permute-start(f32[32,128]{1,0:T(8,128)S(1)} %get-tuple-element.44), channel_id=1, source_target_pairs={{0,8},{1,9},{2,10},{3,11},{4,12},{5,13},{6,14},{7,15},{8,0},{9,1},... | collective-permute-start | bytes 49160 | tf_op jit(solution)/shard_map/ppermute | solution.py:503
  13.7 0.7 %shard_map.123 = (f32[13,20,16,128]{3,2,1,0:T(8,128)S(1)}, f32[20,16,128]{2,1,0:T(8,128)S(1)}, bf16[2,272,256]{2,1,0:T(8,128)(2,1)S(1)}, f32[16,128]{1,0:T(8,128)S(1)}) custom-call(f32[13,16,16,128]{3,2,1,0:T(8,128)S(1)} %get-tuple-element.33.own_ref, f32[17,16,128]{2,1,0:T(8,128)S(1)} %collective-permute-done.gb_ref, ...), custom_call_target="tpu_custom_call" | custom-call | tf_op jit(solution)/shard_map/pallas_call | solution.py:477
  14.4 0.0 collective-permute-done.2.cb_ref
  14.4 2.3 %collective-permute-done.3.ca_ref = f32[32,128]{1,0:T(8,128)S(1)} collective-permute-done((f32[32,128]{1,0:T(8,128)S(1)}, f32[32,128]{1,0:T(8,128)S(1)}, u32[]{:S(2)}, u32[]{:S(2)}) %collective-permute-start.3) | collective-permute-done | bytes 16416 | tf_op jit(solution)/shard_map/ppermute | solution.py:503
  16.7 0.0 collective-permute-done.4.xb_ref
  16.7 0.0 collective-permute-done.5.xa_ref
  16.7 0.5 %shard_map.124 = (f32[13,20,8,128]{3,2,1,0:T(8,128)S(1)}, f32[24,512]{1,0:T(8,128)S(1)}) custom-call(f32[20,16,128]{2,1,0:T(8,128)S(1)} %get-tuple-element.47.acc_ref, f32[17,16,128]{2,1,0:T(8,128)S(1)} %collective-permute-done.4.xb_ref, f32[17,16,128]{2,1,0:T(8,128)S(1)} %collective-permute-done.5.xa_ref, f32[32,128]{1,0:T(8,128)S(1)} %collective-permute-done.2.cb_ref, ...), custom_call_target="tpu_custom_call" | custom-call | tf_op jit(solution)/shard_map/pallas_call | solution.py:477
  17.2 0.1 collective-permute-start.6
  17.3 1.2 %collective-permute-done.6.zg_ref = f32[24,512]{1,0:T(8,128)S(1)} collective-permute-done((f32[24,512]{1,0:T(8,128)S(1)}, f32[24,512]{1,0:T(8,128)S(1)}, u32[]{:S(2)}, u32[]{:S(2)}) %collective-permute-start.6) | collective-permute-done | bytes 49184 | tf_op jit(solution)/shard_map/ppermute | solution.py:546
  18.5 0.0 slice-done
  18.5 0.0 slice-done.1
  18.5 4.7 %shard_map.125 = (f32[3,16,16,128]{3,2,1,0:T(8,128)S(1)}, f32[3,16,16,128]{3,2,1,0:T(8,128)S(1)}, f32[272,128]{1,0:T(8,128)}) custom-call(f32[13,20,16,128]{3,2,1,0:T(8,128)S(1)} %get-tuple-element.42.body_ref, f32[13,20,8,128]{3,2,1,0:T(8,128)S(1)} %get-tuple-element.52.side_ref, f32[24,512]{1,0:T(8,128)S(1)} %get-tuple-element.53.zo_ref, ...), custom_call_target="tpu_custom_call" | custom-call | tf_op jit(solution)/shard_map/pallas_call | solution.py:477
  23.2 4.7 %all-to-all-start = ((f32[272,1,128]{2,1,0:T(1,128)}), f32[272,1,128]{2,1,0:T(1,128)S(1)}, u32[]{:S(2)}, u32[]{:S(2)}) async-start(f32[272,1,128]{2,1,0:T(1,128)} %bitcast.4), calls=%async_computation | async-start | bytes 278528 | tf_op jit(solution)/shard_map/all_to_all | solution.py:564
  27.9 0.7 %copy.14 = f32[3,16,16,128]{3,2,1,0:T(8,128)} copy(f32[3,16,16,128]{3,2,1,0:T(8,128)S(1)} %get-tuple-element.63) | data formatting | bytes 786432
  28.7 0.7 %copy.15 = f32[3,16,16,128]{3,2,1,0:T(8,128)} copy(f32[3,16,16,128]{3,2,1,0:T(8,128)S(1)} %get-tuple-element.64) | data formatting | bytes 786432
  29.4 6.8 %all-to-all-done = f32[272,1,128]{2,1,0:T(1,128)S(1)} async-done(((f32[272,1,128]{2,1,0:T(1,128)}), f32[272,1,128]{2,1,0:T(1,128)S(1)}, u32[]{:S(2)}, u32[]{:S(2)}) %all-to-all-start) | async-done | bytes 139296 | tf_op jit(solution)/shard_map/all_to_all | solution.py:564
  36.2 1.2 %shard_map.126 = f32[64,128]{1,0:T(8,128)} custom-call(f32[272,128]{1,0:T(8,128)S(1)} %bitcast.10), custom_call_target="tpu_custom_call" | custom-call | tf_op jit(solution)/shard_map/pallas_call | solution.py:477
  (2 shorter events, 0.0 us)
Async XLA Ops:
  2.6 7.7 %collective-permute-start = (f32[17,16,128]{2,1,0:T(8,128)S(1)}, f32[17,16,128]{2,1,0:T(8,128)S(1)}, u32[]{:S(2)}, u32[]{:S(2)}) collective-permute-start(f32[17,16,128]{2,1,0:T(8,128)S(1)} %get-tuple-element.34), channel_id=1, source_target_pairs={{0,1},{1,0},{2,4},{3,5},{4,2},{5,3},{6,7},{7,6},{8,9},{9,8},{10,12... | collective-permute-start | bytes 417800 | tf_op jit(solution)/shard_map/ppermute | solution.py:503
  3.1 7.5 %collective-permute-start.1 = (f32[17,16,128]{2,1,0:T(8,128)S(1)}, f32[17,16,128]{2,1,0:T(8,128)S(1)}, u32[]{:S(2)}, u32[]{:S(2)}) collective-permute-start(f32[17,16,128]{2,1,0:T(8,128)S(1)} %get-tuple-element.35), channel_id=1, source_target_pairs={{0,2},{1,3},{2,0},{3,1},{4,6},{5,7},{6,4},{7,5},{8,10},{9,11},{10,... | collective-permute-start | bytes 417800 | tf_op jit(solution)/shard_map/ppermute | solution.py:503
  7.2 9.5 %collective-permute-start.4 = (f32[17,16,128]{2,1,0:T(8,128)S(1)}, f32[17,16,128]{2,1,0:T(8,128)S(1)}, u32[]{:S(2)}, u32[]{:S(2)}) collective-permute-start(f32[17,16,128]{2,1,0:T(8,128)S(1)} %get-tuple-element.48), channel_id=1, source_target_pairs={{0,1},{1,0},{2,3},{3,2},{4,5},{5,4},{6,7},{7,6},{8,16},{9,17},{10,... | collective-permute-start | bytes 417800 | tf_op jit(solution)/shard_map/ppermute | solution.py:503
  7.2 11.2 %slice-start = ((s8[8388608]{0:T(1024)(128)(4,1)}), s8[4194304]{0:T(1024)(128)(4,1)S(1)}, s32[]{:S(2)}) async-start(s8[8388608]{0:T(1024)(128)(4,1)} %bitcast.7), calls=%async_computation.1 | async-start | bytes 8388608
  7.3 11.2 %slice-start.1 = ((s8[8388608]{0:T(1024)(128)(4,1)}), s8[4194304]{0:T(1024)(128)(4,1)S(1)}, s32[]{:S(2)}) async-start(s8[8388608]{0:T(1024)(128)(4,1)} %bitcast.7), calls=%async_computation.2 | async-start | bytes 8388608
  7.3 9.5 %collective-permute-start.5 = (f32[17,16,128]{2,1,0:T(8,128)S(1)}, f32[17,16,128]{2,1,0:T(8,128)S(1)}, u32[]{:S(2)}, u32[]{:S(2)}) collective-permute-start(f32[17,16,128]{2,1,0:T(8,128)S(1)} %get-tuple-element.49), channel_id=1, source_target_pairs={{0,8},{1,9},{2,10},{3,11},{4,12},{5,13},{6,14},{7,15},{8,0},{9,1},... | collective-permute-start | bytes 417800 | tf_op jit(solution)/shard_map/ppermute | solution.py:503
  10.7 3.7 %collective-permute-start.2 = (f32[32,128]{1,0:T(8,128)S(1)}, f32[32,128]{1,0:T(8,128)S(1)}, u32[]{:S(2)}, u32[]{:S(2)}) collective-permute-start(f32[32,128]{1,0:T(8,128)S(1)} %get-tuple-element.43), channel_id=1, source_target_pairs={{0,1},{1,0},{2,3},{3,2},{4,5},{5,4},{6,7},{7,6},{8,16},{9,17},{10,... | collective-permute-start | bytes 49160 | tf_op jit(solution)/shard_map/ppermute | solution.py:503
  10.8 6.0 %collective-permute-start.3 = (f32[32,128]{1,0:T(8,128)S(1)}, f32[32,128]{1,0:T(8,128)S(1)}, u32[]{:S(2)}, u32[]{:S(2)}) collective-permute-start(f32[32,128]{1,0:T(8,128)S(1)} %get-tuple-element.44), channel_id=1, source_target_pairs={{0,8},{1,9},{2,10},{3,11},{4,12},{5,13},{6,14},{7,15},{8,0},{9,1},... | collective-permute-start | bytes 49160 | tf_op jit(solution)/shard_map/ppermute | solution.py:503
  17.2 1.3 %collective-permute-start.6 = (f32[24,512]{1,0:T(8,128)S(1)}, f32[24,512]{1,0:T(8,128)S(1)}, u32[]{:S(2)}, u32[]{:S(2)}) collective-permute-start(f32[24,512]{1,0:T(8,128)S(1)} %get-tuple-element.53.zo_ref), channel_id=1, source_target_pairs={{0,1},{1,0},{2,3},{3,2},{4,5},{5,4},{6,7},{7,6},{8,9},{9,8},{10,11... | collective-permute-start | bytes 147464 | tf_op jit(solution)/shard_map/ppermute | solution.py:546
  23.2 13.0 %all-to-all-start = ((f32[272,1,128]{2,1,0:T(1,128)}), f32[272,1,128]{2,1,0:T(1,128)S(1)}, u32[]{:S(2)}, u32[]{:S(2)}) async-start(f32[272,1,128]{2,1,0:T(1,128)} %bitcast.4), calls=%async_computation | async-start | bytes 278528 | tf_op jit(solution)/shard_map/all_to_all | solution.py:564
